TPU v7x, 128 devices: a whole 4x4x4 slice. The times are simulated.
128 devices in a mesh: scene: 4 (over x), view: 16 (over y, z), row: 2 (over core).
Axes of the slice: x: 4, y: 4, z: 4, core: 2. Of those that a mesh axis runs over, the one named last changes fastest.
Arguments:
- latents: bfloat16 [4, 64, 2, 32, 1536], P('scene', 'view', 'row'), may hold values from -6 to 6
- norm_gain: float32 [1536], replicated, may hold values from 0.5 to 4
- w_query: bfloat16 [1536, 768], replicated, may hold values from -0.15625 to 0.15625
- w_key: bfloat16 [1536, 768], replicated, may hold values from -0.15625 to 0.15625
- w_value: bfloat16 [1536, 768], replicated, may hold values from -0.15625 to 0.15625
- w_out: bfloat16 [768, 1536], replicated, may hold values from -0.21875 to 0.21875
- kernel: bfloat16 [9, 1536], replicated, may hold values from -4 to 4
- partners: int32 [4, 64, 8], P('scene', 'view'), may hold values from -1 to 63, as said below
- counts: int32 [4, 64], P('scene', 'view'), may hold values from 2 to 8, as said below
- cotangent: bfloat16 [4, 64, 2, 32, 1536], P('scene', 'view', 'row'), may hold values from -1.5 to 1.5
Outputs:
- grad_query: float32 [1536, 768], P(('scene', 'view', 'row'))
- grad_key: float32 [1536, 768], P(('scene', 'view', 'row'))
- grad_value: float32 [1536, 768], P(('scene', 'view', 'row'))
- grad_out: float32 [768, 1536], P(('scene', 'view', 'row'))
Inputs may be any that keep to these rules, and one draw needn't show every extreme that they name: Entries j < counts of a view are distinct views held by other groups of 4 views (views 4 * i to 4 * i + 3 form group i); all partners that the views of one group take from another group are one and the same view; entries from counts on are -1. `counts`: the first view of every group has 8 partners.
All inputs are finite; a program needn't handle non-finite values.
Results may differ from a plain program's by a relative error of at most 0.0049.
The roundings to bfloat16 on the way count: a program that leaves them out, or rounds other values in their place, can miss the bound.
Values may be sent and summed in bfloat16 or wider, within the bound.
A program may use at most 192 MiB of HBM per device.

v0:
```python
import jax
import jax.numpy as jnp
from jax import lax
from jax.sharding import PartitionSpec as P

HEAD_DIM = 64


epsilon = 1e-06


def padded_2(x, sides, width):
    for axis, dim in sides:
        count, length = (lax.axis_size(axis), x.shape[dim])
        up = [(i, (i + 1) % count) for i in range(count - 1)]
        down = [(j, i) for i, j in up]
        last = lax.slice_in_dim(x, length - width, length, axis=dim)
        leading = lax.slice_in_dim(x, 0, width, axis=dim)
        before = lax.ppermute(last, axis, up)
        after = lax.ppermute(leading, axis, down)
        x = jnp.concatenate([before, x, after], axis=dim)
    return x


def rim_conv(padded, kernel, rows, columns):
    result = padded[:, 1 : 1 + rows, 1 : 1 + columns].astype(jnp.float32)
    for row_step in range(3):
        for col_step in range(3):
            result = result + kernel[3 * row_step + col_step].astype(jnp.float32) * padded[
                :, 2 - row_step : 2 - row_step + rows, 2 - col_step : 2 - col_step + columns
            ].astype(jnp.float32)
    return result.astype(jnp.bfloat16)


def shards(latents, norm_gain, w_query, w_key, w_value, w_out, kernel, partners, counts, cotangent):
    views_here, strip_rows, columns, width = latents.shape[1:]
    inner_width = w_query.shape[1]
    head_count = inner_width // HEAD_DIM
    view_count = lax.axis_size("view")
    tokens_here = views_here * strip_rows * columns
    scale = HEAD_DIM ** (-0.5)
    lat_f = latents[0].astype(jnp.float32)
    normed = (
        lat_f * lax.rsqrt(jnp.mean(lat_f * lat_f, -1, keepdims=True) + epsilon) * norm_gain
    ).astype(jnp.bfloat16)
    flat_rows = normed.reshape(tokens_here, width)
    queries = jnp.dot(flat_rows, w_query, preferred_element_type=jnp.float32).astype(jnp.bfloat16)
    queries = queries.reshape(views_here, strip_rows * columns, head_count, HEAD_DIM)
    pair_weight = jnp.concatenate((w_key, w_value), axis=1)
    key_value = jnp.dot(flat_rows, pair_weight, preferred_element_type=jnp.float32).astype(
        jnp.bfloat16
    )
    key_value = key_value.reshape(views_here, strip_rows, columns, 2 * inner_width)
    partner_ids = partners[0]
    max_partners = partner_ids.shape[1]
    alive_slots = jnp.arange(max_partners, dtype=jnp.int32)[None, :] < counts[0][:, None]
    source_group = jnp.where(alive_slots, partner_ids // views_here, -1)
    source_view = partner_ids % views_here
    matches = source_group[:, :, None] == jnp.arange(view_count, dtype=jnp.int32)[None, None, :]
    wanted_ok = jnp.any(matches, axis=(0, 1)).astype(jnp.int32)
    wanted_view = jnp.max(jnp.where(matches, source_view[:, :, None], 0), axis=(0, 1))
    request = jnp.stack((wanted_view, wanted_ok), axis=1)
    granted = lax.all_to_all(request, "view", split_axis=0, concat_axis=0, tiled=True)
    grant_view = granted[:, 0]
    grant_ok = granted[:, 1] > 0
    safe_source = jnp.maximum(source_group, 0)
    full_own = lax.all_gather(key_value, "row", axis=1, tiled=True)
    outgoing = jnp.where(
        grant_ok[:, None, None, None],
        jnp.take(full_own, grant_view, axis=0),
        jnp.zeros((), jnp.bfloat16),
    )
    full_arrived = lax.all_to_all(outgoing, "view", split_axis=0, concat_axis=0, tiled=True)
    all_rows = full_own.shape[1]
    view_tokens = all_rows * columns
    block_count = 1 + max_partners
    fetched = jnp.take(full_arrived, safe_source, axis=0)
    blocks = jnp.concatenate((full_own[:, None], fetched), axis=1)
    blocks = blocks.reshape(views_here, block_count * view_tokens, 2, head_count, HEAD_DIM)
    key_rows = blocks[:, :, 0]
    value_rows = blocks[:, :, 1]
    block_alive = jnp.concatenate((jnp.ones((views_here, 1), bool), alive_slots), axis=1)
    key_alive = jnp.repeat(block_alive, view_tokens, axis=1)
    scores = (
        jnp.einsum("uqhd,ukhd->uhqk", queries, key_rows, preferred_element_type=jnp.float32) * scale
    )
    scores = jnp.where(key_alive[:, None, None, :], scores, -1e30)
    highest = jnp.max(scores, -1, keepdims=True)
    expo = jnp.exp(scores - highest)
    attention = expo / jnp.sum(expo, -1, keepdims=True)
    attention_b = attention.astype(jnp.bfloat16)
    mixed = jnp.einsum(
        "uhqk,ukhd->uqhd", attention_b, value_rows, preferred_element_type=jnp.float32
    )
    mixed = mixed.astype(jnp.bfloat16).reshape(tokens_here, inner_width)
    grad_in = cotangent[0]
    padded = padded_2(grad_in, (("row", 1),), 1)
    padded = jnp.pad(padded, ((0, 0), (0, 0), (1, 1), (0, 0)))
    upstream = rim_conv(padded, kernel, strip_rows, columns)
    up_flat = upstream.reshape(tokens_here, width)
    grad_out = jnp.einsum("ti,td->id", mixed, up_flat, preferred_element_type=jnp.float32)
    out_grad = jnp.einsum("td,id->ti", up_flat, w_out, preferred_element_type=jnp.float32).astype(
        jnp.bfloat16
    )
    out_grad = out_grad.reshape(views_here, strip_rows * columns, head_count, HEAD_DIM)
    dprob = jnp.einsum("uqhd,ukhd->uhqk", out_grad, value_rows, preferred_element_type=jnp.float32)
    row_delta = jnp.sum(attention * dprob, -1, keepdims=True)
    dscore = (attention * (dprob - row_delta) * scale).astype(jnp.bfloat16)
    dquery = jnp.einsum("uhqk,ukhd->uqhd", dscore, key_rows, preferred_element_type=jnp.float32)
    dquery = dquery.astype(jnp.bfloat16).reshape(tokens_here, inner_width)
    grad_query = jnp.einsum("tc,ti->ci", flat_rows, dquery, preferred_element_type=jnp.float32)
    dkey = jnp.einsum("uhqk,uqhd->ukhd", dscore, queries, preferred_element_type=jnp.float32)
    dvalue = jnp.einsum(
        "uhqk,uqhd->ukhd", attention_b, out_grad, preferred_element_type=jnp.float32
    )
    block_shape = (views_here, block_count, all_rows, columns, inner_width)
    dpair = jnp.concatenate((dkey.reshape(block_shape), dvalue.reshape(block_shape)), axis=-1)
    own_part = lax.optimization_barrier(dpair[:, 0].astype(jnp.bfloat16))
    match_table = matches.astype(jnp.float32)
    returned_part = jnp.einsum(
        "ujs,ujhwc->shwc", match_table, dpair[:, 1:], precision=lax.Precision.HIGHEST
    ).astype(jnp.bfloat16)
    came_back = lax.all_to_all(returned_part, "view", split_axis=0, concat_axis=0, tiled=True)
    grant_table = (
        (grant_view[:, None] == jnp.arange(views_here, dtype=jnp.int32)[None, :])
        & grant_ok[:, None]
    ).astype(jnp.float32)
    totals = own_part.astype(jnp.float32) + jnp.einsum(
        "ev,ehwc->vhwc", grant_table, came_back.astype(jnp.float32), precision=lax.Precision.HIGHEST
    )
    own_strip = lax.psum_scatter(totals, "row", scatter_dimension=1, tiled=True)
    own_strip = own_strip.reshape(tokens_here, 2 * inner_width)
    rows_f = flat_rows.astype(jnp.float32)
    grad_key = jnp.dot(rows_f.T, own_strip[:, :inner_width], precision=lax.Precision.HIGHEST)
    grad_value = jnp.dot(rows_f.T, own_strip[:, inner_width:], precision=lax.Precision.HIGHEST)
    summed = (
        lax.psum_scatter(grad_query, ("scene", "view", "row"), scatter_dimension=0, tiled=True),
        lax.psum_scatter(grad_key, ("scene", "view", "row"), scatter_dimension=0, tiled=True),
        lax.psum_scatter(grad_value, ("scene", "view", "row"), scatter_dimension=0, tiled=True),
        lax.psum_scatter(grad_out, ("scene", "view", "row"), scatter_dimension=0, tiled=True),
    )
    return (summed[0], summed[1], summed[2], summed[3])


def solution(mesh):
    placed = (
        P("scene", "view", "row", None, None),
        P(),
        P(),
        P(),
        P(),
        P(),
        P(),
        P("scene", "view", None),
        P("scene", "view"),
        P("scene", "view", "row", None, None),
    )
    return jax.shard_map(
        shards,
        mesh=mesh,
        in_specs=placed,
        out_specs=(
            P(("scene", "view", "row"), None),
            P(("scene", "view", "row"), None),
            P(("scene", "view", "row"), None),
            P(("scene", "view", "row"), None),
        ),
        check_vma=False,
    )
```

profile of v0, /device:TPU:1, one launch (start us, length us, event | category | flops | bytes accessed | tf_op | source)
XLA Modules:
  0.0 1295.6 jit_solution(5833965806034760408)
XLA Ops:
  10.2 8.6 all-to-all-start
  37.0 7.1 all-to-all-start.1
  61.8 22.9 %all-to-all-done.1 = bf16[16,2,32,1536]{3,2,1,0:T(8,128)(2,1)} async-done(((bf16[16,2,32,1536]{3,2,1,0:T(8,128)(2,1)}), bf16[16,2,32,1536]{3,2,1,0:T(8,128)(2,1)}, u32[]{:S(2)}, u32[]{:S(2)}) %all-to-all-start.1) | async-done | bytes 3145760 | tf_op jit(solution)/shard_map/all_to_all | solution.py:73
  84.8 5.5 gather_fusion.1
  97.2 23.7 %reshape.408 = bf16[4,576,2,12,64]{4,3,2,1,0:T(8,128)(2,1)} reshape(bf16[4,9,2,32,1536]{4,3,2,1,0:T(8,128)(2,1)} %pad_maximum_fusion.2) | data formatting | bytes 14155776 | tf_op jit(solution)/shard_map/reshape | solution.py:79
  120.9 15.7 %fusion.109 = (bf16[4,576,1,12,64]{4,3,2,1,0:T(8,128)(2,1)}, bf16[4,576,1,12,64]{4,3,2,1,0:T(8,128)(2,1)}) fusion(bf16[4,576,2,12,64]{4,3,2,1,0:T(8,128)(2,1)} %reshape.408), kind=kLoop, calls=%fused_computation.150 | loop fusion | bytes 14155776 | tf_op jit(solution)/shard_map/slice | solution.py:80
  136.7 11.2 copy.100
  147.9 11.2 copy.101
  159.1 4.9 fusion.14
  168.3 4.5 convolution_bitcast_fusion
  172.8 15.5 %convolution_bitcast_fusion.1 = f32[4,576,12,64]{1,3,2,0:T(8,128)} fusion(f32[4,12,32,576]{3,2,1,0:T(8,128)} %fusion.14, bf16[4,32,12,64]{3,2,1,0:T(8,128)(2,1)S(1)} %copy-done.5, f32[4,12,32,576]{3,2,1,0:T(8,128)} %copy-done.3, f32[4,12,32]{2,1,0:T(8,128)S(1)} %get-tuple-element.30), kind=kOutput, calls=%fused_computation.35 | convolution fusion | flops 119441472 | bytes 14358528 | tf_op jit(solution)/shard_map/uhqk,uqhd->ukhd/dot_general | solution.py:112
  188.2 23.2 %reshape.449 = f32[4,9,2,32,768]{3,2,1,4,0:T(2,128)} reshape(f32[4,576,12,64]{1,3,2,0:T(8,128)} %convolution_bitcast_fusion) | data formatting | bytes 14155776 | tf_op jit(solution)/shard_map/reshape | solution.py:117
  211.5 40.3 %copy.86 = f32[4,9,2,32,768]{4,1,0,3,2:T(8,128)} copy(f32[4,9,2,32,768]{3,2,1,4,0:T(2,128)} %reshape.449) | data formatting | bytes 14155776 | tf_op jit(solution)/shard_map/reshape | solution.py:117
  251.8 23.2 %reshape.448 = f32[4,9,2,32,768]{3,2,1,4,0:T(2,128)} reshape(f32[4,576,12,64]{1,3,2,0:T(8,128)} %convolution_bitcast_fusion.1) | data formatting | bytes 14155776 | tf_op jit(solution)/shard_map/reshape | solution.py:117
  275.0 40.4 %copy.85 = f32[4,9,2,32,768]{4,1,0,3,2:T(8,128)} copy(f32[4,9,2,32,768]{3,2,1,4,0:T(2,128)} %reshape.448) | data formatting | bytes 14155776 | tf_op jit(solution)/shard_map/reshape | solution.py:117
  315.4 23.3 %bitcast_convert_fusion = bf16[16,2,32,1536]{3,0,2,1:T(8,128)(2,1)S(1)} fusion(f32[4,9,2,32,768]{4,1,0,3,2:T(8,128)} %copy.86, f32[4,9,2,32,768]{4,1,0,3,2:T(8,128)} %copy.85, s32[4,8]{1,0:T(4,128)S(1)} %get-tuple-element.22), kind=kOutput, calls=%fused_computation.10 | convolution fusion | flops 608698880 | bytes 17301632 | tf_op jit(solution)/shard_map/ujs,ujhwc->shwc/dot_general | solution.py:120
  342.2 11.0 all-to-all-start.2
  353.3 5.4 fusion.41
  359.2 32.9 %all-to-all-done.2 = bf16[16,2,32,1536]{3,2,1,0:T(8,128)(2,1)} async-done(((bf16[16,2,32,1536]{3,2,1,0:T(8,128)(2,1)}), bf16[16,2,32,1536]{3,2,1,0:T(8,128)(2,1)}, u32[]{:S(2)}, u32[]{:S(2)}) %all-to-all-start.2) | async-done | bytes 3145760 | tf_op jit(solution)/shard_map/all_to_all | solution.py:123
  398.1 15.2 %fusion.55 = bf16[4,32,12,64]{3,1,2,0:T(8,128)(2,1)S(1)} fusion(f32[4,12,32,576]{3,2,1,0:T(8,128)} %fusion.14, bf16[4,576,1,12,64]{1,4,3,0,2:T(8,128)(2,1)} %copy.100, f32[4,12,32,576]{3,2,1,0:T(8,128)} %copy-done.3, f32[4,12,32]{2,1,0:T(8,128)S(1)} %copy-done.54), kind=kOutput, calls=%fused_computation.54 | convolution fusion | flops 119539776 | bytes 10819584 | tf_op jit(solution)/shard_map/uhqk,ukhd->uqhd/dot_general | solution.py:109
  413.8 4.7 fusion.52
  425.0 5.2 fusion.73
  430.3 4.4 fusion.75
  434.6 369.4 %fusion.107 = (f32[16,768]{1,0:T(8,128)S(1)}, f32[16,768]{1,0:T(8,128)S(1)}, f32[16,768]{1,0:T(8,128)S(1)}, f32[8,1536]{1,0:T(8,128)S(1)}) fusion(f32[1536,768]{1,0:T(8,128)} %fusion.111, f32[1536,768]{1,0:T(8,128)} %fusion.75, f32[1536,768]{1,0:T(8,128)} %fusion.73, f32[768,1536]{1,0:T(8,128)} %fusion.112), kind=kCustom, calls=%all-reduce-scatter.4 | all-reduce-scatter fusion | flops 6291458 | bytes 19070976
  806.8 10.3 collective-permute-start.97
  824.0 7.3 collective-permute-start.31
  850.8 5.1 collective-permute-start.24
  1030.2 4.2 collective-permute-start.76
  1094.3 6.3 concatenate.20
  1113.5 47.7 %concatenate.21 = f32[524,768]{1,0:T(8,128)} concatenate(f32[12,768]{1,0:T(8,128)S(1)} %collective-permute-done.65, f32[16,768]{1,0:T(8,128)S(1)} %collective-permute-done.64, f32[16,768]{1,0:T(8,128)S(1)} %collective-permute-done.63, f32[16,768]{1,0:T(8,128)S(1)} %collective-permute-done.62, f32[16,768]{1,0:T(8,128)} %copy-done.8, f32[16,768]{1,0:T(8,128)} %copy-done.9, ...), dimensions={0} | concatenate | bytes 3219456
  1174.7 47.8 %concatenate.22 = f32[524,768]{1,0:T(8,128)} concatenate(f32[12,768]{1,0:T(8,128)S(1)} %collective-permute-done.97, f32[16,768]{1,0:T(8,128)} %copy-done.30, f32[16,768]{1,0:T(8,128)} %copy-done.32, f32[16,768]{1,0:T(8,128)} %copy-done.34, f32[16,768]{1,0:T(8,128)} %copy-done.36, f32[16,768]{1,0:T(8,128)} %copy-done.38, f32[16,768]{1,0:T(8,128)} %copy-done.40, ...), dimensions={0} | concatenate | bytes 3219456
  1237.9 48.9 %concatenate.23 = f32[262,1536]{1,0:T(8,128)} concatenate(f32[6,1536]{1,0:T(8,128)S(1)} %collective-permute-done.129, f32[8,1536]{1,0:T(8,128)} %collective-permute-done.128, f32[8,1536]{1,0:T(8,128)} %collective-permute-done.127, f32[8,1536]{1,0:T(8,128)} %collective-permute-done.126, f32[8,1536]{1,0:T(8,128)} %collective-permute-done.125, f32[8,1536]{1,0:T(8,128)} %collective-permute-done.124, ...), dimensions={0} | concatenate | bytes 3219456
  (440 shorter events, 371.2 us)
Async XLA Ops:
  10.2 17.2 %all-to-all-start = ((s32[16,1,2]{2,1,0:T(1,128)}), s32[16,1,2]{2,1,0:T(1,128)S(1)}, u32[]{:S(2)}, u32[]{:S(2)}) async-start(s32[16,1,2]{2,1,0:T(1,128)} %copy.74), calls=%async_computation | async-start | bytes 16384 | tf_op jit(solution)/shard_map/all_to_all | solution.py:63
  37.0 47.8 %all-to-all-start.1 = ((bf16[16,2,32,1536]{3,2,1,0:T(8,128)(2,1)}), bf16[16,2,32,1536]{3,2,1,0:T(8,128)(2,1)}, u32[]{:S(2)}, u32[]{:S(2)}) async-start(bf16[16,2,32,1536]{3,2,1,0:T(8,128)(2,1)} %select_select_fusion), calls=%async_computation.1 | async-start | bytes 6291456 | tf_op jit(solution)/shard_map/all_to_all | solution.py:73
  342.2 49.9 %all-to-all-start.2 = ((bf16[16,2,32,1536]{3,2,1,0:T(8,128)(2,1)}), bf16[16,2,32,1536]{3,2,1,0:T(8,128)(2,1)}, u32[]{:S(2)}, u32[]{:S(2)}) async-start(bf16[16,2,32,1536]{3,2,1,0:T(8,128)(2,1)} %copy.88), calls=%async_computation.2 | async-start | bytes 6291456 | tf_op jit(solution)/shard_map/all_to_all | solution.py:123
  353.2 71.8 %reduce-scatter.10.cloned.1.call-start = ((), (), s32[]{:S(2)}) async-start(), calls=%async_computation.4 | async-start | bytes 2359296 | tf_op jit(solution)/shard_map/reduce_scatter | solution.py:131
  804.1 27.2 %collective-permute-start.129 = (f32[6,1536]{1,0:T(8,128)S(1)}, f32[6,1536]{1,0:T(8,128)S(1)}, u32[]{:S(2)}, u32[]{:S(2)}) collective-permute-start(f32[6,1536]{1,0:T(8,128)S(1)} %slice.119), channel_id=1, source_target_pairs={{0,32},{1,33},{2,34},{3,35},{4,36},{5,37},{6,38},{7,39},{8,40},{9,... | collective-permute-start | bytes 110600
  806.8 26.8 %collective-permute-start.97 = (f32[12,768]{1,0:T(8,128)S(1)}, f32[12,768]{1,0:T(8,128)S(1)}, u32[]{:S(2)}, u32[]{:S(2)}) collective-permute-start(f32[12,768]{1,0:T(8,128)S(1)} %slice.118), channel_id=1, source_target_pairs={{0,32},{1,33},{2,34},{3,35},{4,36},{5,37},{6,38},{7,39},{8,40},{9,... | collective-permute-start | bytes 110600
  817.1 20.4 %collective-permute-start.65 = (f32[12,768]{1,0:T(8,128)S(1)}, f32[12,768]{1,0:T(8,128)S(1)}, u32[]{:S(2)}, u32[]{:S(2)}) collective-permute-start(f32[12,768]{1,0:T(8,128)S(1)} %slice.117), channel_id=1, source_target_pairs={{0,32},{1,33},{2,34},{3,35},{4,36},{5,37},{6,38},{7,39},{8,40},{9,... | collective-permute-start | bytes 110600
  820.4 23.2 %collective-permute-start.32 = (f32[16,768]{1,0:T(8,128)S(1)}, f32[16,768]{1,0:T(8,128)S(1)}, u32[]{:S(2)}, u32[]{:S(2)}) collective-permute-start(f32[16,768]{1,0:T(8,128)S(1)} %get-tuple-element.17), channel_id=1, source_target_pairs={{0,31},{1,32},{2,33},{3,34},{4,35},{5,36},{6,37},{7,38},{8,39},{9,... | collective-permute-start | bytes 147464
  824.0 23.5 %collective-permute-start.31 = (f32[16,768]{1,0:T(8,128)S(1)}, f32[16,768]{1,0:T(8,128)S(1)}, u32[]{:S(2)}, u32[]{:S(2)}) collective-permute-start(f32[16,768]{1,0:T(8,128)S(1)} %get-tuple-element.17), channel_id=1, source_target_pairs={{0,30},{1,31},{2,32},{3,33},{4,34},{5,35},{6,36},{7,37},{8,38},{9,... | collective-permute-start | bytes 147464
  831.3 17.8 %collective-permute-start.30 = (f32[16,768]{1,0:T(8,128)S(1)}, f32[16,768]{1,0:T(8,128)S(1)}, u32[]{:S(2)}, u32[]{:S(2)}) collective-permute-start(f32[16,768]{1,0:T(8,128)S(1)} %get-tuple-element.17), channel_id=1, source_target_pairs={{0,29},{1,30},{2,31},{3,32},{4,33},{5,34},{6,35},{7,36},{8,37},{9,... | collective-permute-start | bytes 147464
  833.6 17.2 %collective-permute-start.29 = (f32[16,768]{1,0:T(8,128)S(1)}, f32[16,768]{1,0:T(8,128)S(1)}, u32[]{:S(2)}, u32[]{:S(2)}) collective-permute-start(f32[16,768]{1,0:T(8,128)S(1)} %get-tuple-element.17), channel_id=1, source_target_pairs={{0,28},{1,29},{2,30},{3,31},{4,32},{5,33},{6,34},{7,35},{8,36},{9,... | collective-permute-start | bytes 147464
  840.0 15.9 %collective-permute-start.28 = (f32[16,768]{1,0:T(8,128)S(1)}, f32[16,768]{1,0:T(8,128)S(1)}, u32[]{:S(2)}, u32[]{:S(2)}) collective-permute-start(f32[16,768]{1,0:T(8,128)S(1)} %get-tuple-element.17), channel_id=1, source_target_pairs={{0,27},{1,28},{2,29},{3,30},{4,31},{5,32},{6,33},{7,34},{8,35},{9,... | collective-permute-start | bytes 147464
  843.6 15.8 %collective-permute-start.27 = (f32[16,768]{1,0:T(8,128)S(1)}, f32[16,768]{1,0:T(8,128)S(1)}, u32[]{:S(2)}, u32[]{:S(2)}) collective-permute-start(f32[16,768]{1,0:T(8,128)S(1)} %get-tuple-element.17), channel_id=1, source_target_pairs={{0,26},{1,27},{2,28},{3,29},{4,30},{5,31},{6,32},{7,33},{8,34},{9,... | collective-permute-start | bytes 147464
  850.8 16.1 %collective-permute-start.24 = (f32[16,768]{1,0:T(8,128)S(1)}, f32[16,768]{1,0:T(8,128)S(1)}, u32[]{:S(2)}, u32[]{:S(2)}) collective-permute-start(f32[16,768]{1,0:T(8,128)S(1)} %get-tuple-element.17), channel_id=1, source_target_pairs={{0,23},{1,24},{2,25},{3,26},{4,27},{5,28},{6,29},{7,30},{8,31},{9,... | collective-permute-start | bytes 147464
  894.9 16.1 %collective-permute-start.8 = (f32[16,768]{1,0:T(8,128)S(1)}, f32[16,768]{1,0:T(8,128)S(1)}, u32[]{:S(2)}, u32[]{:S(2)}) collective-permute-start(f32[16,768]{1,0:T(8,128)S(1)} %get-tuple-element.17), channel_id=1, source_target_pairs={{0,7},{1,8},{2,9},{3,10},{4,11},{5,12},{6,13},{7,14},{8,15},{9,16}... | collective-permute-start | bytes 147464
  897.7 16.2 %collective-permute-start.7 = (f32[16,768]{1,0:T(8,128)S(1)}, f32[16,768]{1,0:T(8,128)S(1)}, u32[]{:S(2)}, u32[]{:S(2)}) collective-permute-start(f32[16,768]{1,0:T(8,128)S(1)} %get-tuple-element.17), channel_id=1, source_target_pairs={{0,6},{1,7},{2,8},{3,9},{4,10},{5,11},{6,12},{7,13},{8,14},{9,15},... | collective-permute-start | bytes 147464
  900.7 15.6 %collective-permute-start.6 = (f32[16,768]{1,0:T(8,128)S(1)}, f32[16,768]{1,0:T(8,128)S(1)}, u32[]{:S(2)}, u32[]{:S(2)}) collective-permute-start(f32[16,768]{1,0:T(8,128)S(1)} %get-tuple-element.17), channel_id=1, source_target_pairs={{0,5},{1,6},{2,7},{3,8},{4,9},{5,10},{6,11},{7,12},{8,13},{9,14},{... | collective-permute-start | bytes 147464
  1082.6 18.0 %collective-permute-start.117 = (f32[8,1536]{1,0:T(8,128)S(1)}, f32[8,1536]{1,0:T(8,128)}, u32[]{:S(2)}, u32[]{:S(2)}) collective-permute-start(f32[8,1536]{1,0:T(8,128)S(1)} %get-tuple-element.20), channel_id=1, source_target_pairs={{0,20},{1,21},{2,22},{3,23},{4,24},{5,25},{6,26},{7,27},{8,28},{9,... | collective-permute-start | bytes 147464
  1085.3 16.8 %collective-permute-start.116 = (f32[8,1536]{1,0:T(8,128)S(1)}, f32[8,1536]{1,0:T(8,128)}, u32[]{:S(2)}, u32[]{:S(2)}) collective-permute-start(f32[8,1536]{1,0:T(8,128)S(1)} %get-tuple-element.20), channel_id=1, source_target_pairs={{0,19},{1,20},{2,21},{3,22},{4,23},{5,24},{6,25},{7,26},{8,27},{9,... | collective-permute-start | bytes 147464
  1087.5 17.0 %collective-permute-start.115 = (f32[8,1536]{1,0:T(8,128)S(1)}, f32[8,1536]{1,0:T(8,128)}, u32[]{:S(2)}, u32[]{:S(2)}) collective-permute-start(f32[8,1536]{1,0:T(8,128)S(1)} %get-tuple-element.20), channel_id=1, source_target_pairs={{0,18},{1,19},{2,20},{3,21},{4,22},{5,23},{6,24},{7,25},{8,26},{9,... | collective-permute-start | bytes 147464
  1089.4 17.5 %collective-permute-start.114 = (f32[8,1536]{1,0:T(8,128)S(1)}, f32[8,1536]{1,0:T(8,128)}, u32[]{:S(2)}, u32[]{:S(2)}) collective-permute-start(f32[8,1536]{1,0:T(8,128)S(1)} %get-tuple-element.20), channel_id=1, source_target_pairs={{0,17},{1,18},{2,19},{3,20},{4,21},{5,22},{6,23},{7,24},{8,25},{9,... | collective-permute-start | bytes 147464
  1091.8 17.0 %collective-permute-start.113 = (f32[8,1536]{1,0:T(8,128)S(1)}, f32[8,1536]{1,0:T(8,128)}, u32[]{:S(2)}, u32[]{:S(2)}) collective-permute-start(f32[8,1536]{1,0:T(8,128)S(1)} %get-tuple-element.20), channel_id=1, source_target_pairs={{0,16},{1,17},{2,18},{3,19},{4,20},{5,21},{6,22},{7,23},{8,24},{9,... | collective-permute-start | bytes 147464
  1100.6 60.6 %collective-permute-start.112 = (f32[8,1536]{1,0:T(8,128)S(1)}, f32[8,1536]{1,0:T(8,128)S(1)}, u32[]{:S(2)}, u32[]{:S(2)}) collective-permute-start(f32[8,1536]{1,0:T(8,128)S(1)} %get-tuple-element.20), channel_id=1, source_target_pairs={{0,15},{1,16},{2,17},{3,18},{4,19},{5,20},{6,21},{7,22},{8,23},{9,... | collective-permute-start | bytes 147464
  1102.1 60.4 %collective-permute-start.111 = (f32[8,1536]{1,0:T(8,128)S(1)}, f32[8,1536]{1,0:T(8,128)S(1)}, u32[]{:S(2)}, u32[]{:S(2)}) collective-permute-start(f32[8,1536]{1,0:T(8,128)S(1)} %get-tuple-element.20), channel_id=1, source_target_pairs={{0,14},{1,15},{2,16},{3,17},{4,18},{5,19},{6,20},{7,21},{8,22},{9,... | collective-permute-start | bytes 147464
  1104.5 60.8 %collective-permute-start.110 = (f32[8,1536]{1,0:T(8,128)S(1)}, f32[8,1536]{1,0:T(8,128)S(1)}, u32[]{:S(2)}, u32[]{:S(2)}) collective-permute-start(f32[8,1536]{1,0:T(8,128)S(1)} %get-tuple-element.20), channel_id=1, source_target_pairs={{0,13},{1,14},{2,15},{3,16},{4,17},{5,18},{6,19},{7,20},{8,21},{9,... | collective-permute-start | bytes 147464
  1106.9 60.1 %collective-permute-start.109 = (f32[8,1536]{1,0:T(8,128)S(1)}, f32[8,1536]{1,0:T(8,128)S(1)}, u32[]{:S(2)}, u32[]{:S(2)}) collective-permute-start(f32[8,1536]{1,0:T(8,128)S(1)} %get-tuple-element.20), channel_id=1, source_target_pairs={{0,12},{1,13},{2,14},{3,15},{4,16},{5,17},{6,18},{7,19},{8,20},{9,... | collective-permute-start | bytes 147464
  1108.8 60.9 %collective-permute-start.108 = (f32[8,1536]{1,0:T(8,128)S(1)}, f32[8,1536]{1,0:T(8,128)S(1)}, u32[]{:S(2)}, u32[]{:S(2)}) collective-permute-start(f32[8,1536]{1,0:T(8,128)S(1)} %get-tuple-element.20), channel_id=1, source_target_pairs={{0,11},{1,12},{2,13},{3,14},{4,15},{5,16},{6,17},{7,18},{8,19},{9,... | collective-permute-start | bytes 147464
  1161.2 61.3 %collective-permute-start.107 = (f32[8,1536]{1,0:T(8,128)S(1)}, f32[8,1536]{1,0:T(8,128)S(1)}, u32[]{:S(2)}, u32[]{:S(2)}) collective-permute-start(f32[8,1536]{1,0:T(8,128)S(1)} %get-tuple-element.20), channel_id=1, source_target_pairs={{0,10},{1,11},{2,12},{3,13},{4,14},{5,15},{6,16},{7,17},{8,18},{9,... | collective-permute-start | bytes 147464
  1162.5 62.6 %collective-permute-start.106 = (f32[8,1536]{1,0:T(8,128)S(1)}, f32[8,1536]{1,0:T(8,128)S(1)}, u32[]{:S(2)}, u32[]{:S(2)}) collective-permute-start(f32[8,1536]{1,0:T(8,128)S(1)} %get-tuple-element.20), channel_id=1, source_target_pairs={{0,9},{1,10},{2,11},{3,12},{4,13},{5,14},{6,15},{7,16},{8,17},{9,1... | collective-permute-start | bytes 147464
  1165.3 62.8 %collective-permute-start.105 = (f32[8,1536]{1,0:T(8,128)S(1)}, f32[8,1536]{1,0:T(8,128)S(1)}, u32[]{:S(2)}, u32[]{:S(2)}) collective-permute-start(f32[8,1536]{1,0:T(8,128)S(1)} %get-tuple-element.20), channel_id=1, source_target_pairs={{0,8},{1,9},{2,10},{3,11},{4,12},{5,13},{6,14},{7,15},{8,16},{9,17... | collective-permute-start | bytes 147464
  1167.0 64.7 %collective-permute-start.104 = (f32[8,1536]{1,0:T(8,128)S(1)}, f32[8,1536]{1,0:T(8,128)S(1)}, u32[]{:S(2)}, u32[]{:S(2)}) collective-permute-start(f32[8,1536]{1,0:T(8,128)S(1)} %get-tuple-element.20), channel_id=1, source_target_pairs={{0,7},{1,8},{2,9},{3,10},{4,11},{5,12},{6,13},{7,14},{8,15},{9,16}... | collective-permute-start | bytes 147464
  1169.8 64.3 %collective-permute-start.103 = (f32[8,1536]{1,0:T(8,128)S(1)}, f32[8,1536]{1,0:T(8,128)S(1)}, u32[]{:S(2)}, u32[]{:S(2)}) collective-permute-start(f32[8,1536]{1,0:T(8,128)S(1)} %get-tuple-element.20), channel_id=1, source_target_pairs={{0,6},{1,7},{2,8},{3,9},{4,10},{5,11},{6,12},{7,13},{8,14},{9,15},... | collective-permute-start | bytes 147464
  (164 other events, 6001.3 us)
Sparse Core Ops, SparseCore 0:
  398.0 14.5 reduce-scatter.9
where the time goes:
time: 1320 us; the launch traced here: 1300 us
  blocking collectives  372 us (28%)
  local copies, waits for them, and re-layouts  367 us (28%)
  starting transfers between devices  356 us (27%)
  matrix products  93.5 us (7%)
  waiting for transfers between devices  57.4 us (4%)
  other arithmetic  32.3 us (2%)
  between operations  17.1 us (1%)
    unnamed x1, blocking collectives  369 us
    unnamed x128, starting transfers between devices  324 us
    unnamed x138, local copies, waits for them, and re-layouts  180 us
    reshape x2, local copies, waits for them, and re-layouts, shards(): dkey.reshape(block_shape)  63.6 us
    reshape x2, local copies, waits for them, and re-layouts, shards(): dvalue.reshape(block_shape)  63.5 us
    all_to_all x1, waiting for transfers between devices, shards(): lax.all_to_all(returned_part, 'view', split_axis=0, concat_axis=0, tiled=...  32.9 us
  transfers between devices with their start and end apart: 134, of which 3 were waited for; matrix products, arithmetic and copies ran while one was open for 12% of the time, Pallas kernels for 0%

commit v1 on v0

v1 whole, which is shorter than its diff:
```python
import functools

import jax
import jax.numpy as jnp
from jax import lax
from jax.experimental import pallas as pl
from jax.experimental.pallas import tpu as pltpu
from jax.sharding import PartitionSpec as P

HEAD_DIM = 64
LANES = 128
EPSILON = 1e-06
MESH = pl.DeviceIdType.MESH
VMEM_LIMIT = 60 * 1024 * 1024
NT = (((1,), (1,)), ((), ()))
NN = (((1,), (0,)), ((), ()))


def matmul(a, b, dims=NN):
    return lax.dot_general(a, b, dims, preferred_element_type=jnp.float32)


def vmem(count):
    return [pl.BlockSpec(memory_space=pltpu.VMEM)] * count


def exchange_kernel(
    groups, norm, cot, request, x, cot_all, grant, outbuf,
    req_send, req_recv, out_send, out_recv, fwd_send, fwd_recv, own_send, own_recv,
):
    scene, me, row = lax.axis_index("scene"), lax.axis_index("view"), lax.axis_index("row")
    views = norm.shape[0]
    sibling = (scene, me, 1 - row)
    barrier = pltpu.get_barrier_semaphore()

    def peer(step):
        return lax.rem(me + step, groups)

    for step in range(1, groups):
        pl.semaphore_signal(barrier, inc=1, device_id=(scene, peer(step), row), device_id_type=MESH)
    pl.semaphore_signal(barrier, inc=1, device_id=sibling, device_id_type=MESH)
    pl.semaphore_wait(barrier, groups)

    def remote(src, dst, send, recv, device):
        return pltpu.make_async_remote_copy(
            src_ref=src, dst_ref=dst, send_sem=send, recv_sem=recv, device_id=device, device_id_type=MESH
        )

    asks = [
        remote(request.at[peer(s)], grant.at[me], req_send.at[s], req_recv.at[s], (scene, peer(s), row))
        for s in range(1, groups)
    ]
    for copy in asks:
        copy.start()
    own = [
        remote(norm.at[0], x.at[row, me], own_send.at[0], own_recv.at[0], sibling),
        remote(
            norm.at[pl.ds(1, views - 1)], x.at[row, pl.ds(groups, views - 1)],
            own_send.at[1], own_recv.at[1], sibling,
        ),
        remote(cot, cot_all.at[row], own_send.at[2], own_recv.at[2], sibling),
    ]
    for copy in own:
        copy.start()
    x[row, me] = norm[0]
    x[row, pl.ds(groups, views - 1)] = norm[1:]
    cot_all[row] = cot[...]

    blocks = []
    for s in range(1, groups):
        back = groups - s
        asks[back - 1].wait_recv()
        want = grant[peer(s)][0:1, 0:1]
        block = norm[0]
        for v in range(1, views):
            block = jnp.where(want == v, norm[v], block)
        outbuf[s - 1] = block
        blocks.append(
            remote(outbuf.at[s - 1], x.at[row, me], out_send.at[s], out_recv.at[s], (scene, peer(s), row))
        )
        blocks[-1].start()
    forwards = []
    for s in range(1, groups):
        blocks[s - 1].wait_recv()
        source = lax.rem(me + groups - s, groups)
        forwards.append(
            remote(x.at[row, source], x.at[row, source], fwd_send.at[s], fwd_recv.at[s], sibling)
        )
        forwards[-1].start()
    for copy in own + forwards:
        copy.wait()
    for copy in asks + blocks:
        copy.wait_send()


def exchange(norm, cot, request, groups):
    views, columns, width = norm.shape
    slots = groups + views - 1
    dma = pltpu.SemaphoreType.DMA
    return pl.pallas_call(
        functools.partial(exchange_kernel, groups),
        out_shape=(
            jax.ShapeDtypeStruct((2, slots, columns, width), jnp.bfloat16),
            jax.ShapeDtypeStruct((2, views, columns, width), jnp.bfloat16),
        ),
        in_specs=vmem(3),
        out_specs=tuple(vmem(2)),
        scratch_shapes=[
            pltpu.VMEM((groups, 8, LANES), jnp.int32),
            pltpu.VMEM((groups - 1, columns, width), jnp.bfloat16),
            dma((groups,)), dma((groups,)), dma((groups,)), dma((groups,)),
            dma((groups,)), dma((groups,)), dma((3,)), dma((3,)),
        ],
        compiler_params=pltpu.CompilerParams(
            collective_id=0, has_side_effects=True, vmem_limit_bytes=VMEM_LIMIT
        ),
    )(norm, cot, request)


def local_kernel(
    groups, x, cot, taps, bias, wq_hbm, wk_hbm, wv_hbm, wo_hbm, ga, mt, up,
    wq, wkv, wo, xo, xt, xot, keys, values, qm, om, s_buf, dp_buf, p_buf, ds_buf, dkv, sems,
):
    me, core = lax.axis_index("view"), lax.axis_index("row")
    width = x.shape[-1]
    half = wq.shape[1]
    pairs = half // LANES
    key_rows, queries = s_buf.shape
    columns, views = cot.shape[2], cot.shape[1]
    slots = key_rows // (2 * columns)
    scale = HEAD_DIM ** (-0.5)
    cols = pl.ds(pl.multiple_of(core * half, LANES), half)
    loads = [
        pltpu.make_async_copy(wq_hbm.at[:, cols], wq, sems.at[0]),
        pltpu.make_async_copy(wk_hbm.at[:, cols], wkv.at[:, pl.ds(0, half)], sems.at[1]),
        pltpu.make_async_copy(wv_hbm.at[:, cols], wkv.at[:, pl.ds(half, half)], sems.at[2]),
        pltpu.make_async_copy(wo_hbm.at[cols, :], wo, sems.at[3]),
    ]
    for copy in loads:
        copy.start()

    for strip in range(2):
        base = strip * slots * columns
        top = strip * views * columns
        xo[pl.ds(top, columns)] = x[pl.ds(pl.multiple_of(base + me * columns, columns), columns)]
        rest = (views - 1) * columns
        xo[pl.ds(top + columns, rest)] = x[pl.ds(base + groups * columns, rest)]

    chunk = 4 * LANES
    place = lax.broadcasted_iota(jnp.int32, (columns, chunk), 0)

    def conv_view(view, carry):
        for part in range(width // chunk):
            lanes = pl.ds(part * chunk, chunk)
            kern = taps[:, lanes].astype(jnp.float32)
            shifted = []
            for strip in range(2):
                mid = cot[strip, view, :, lanes].astype(jnp.float32)
                after = jnp.where(place == columns - 1, 0.0, pltpu.roll(mid, columns - 1, 0))
                before = jnp.where(place == 0, 0.0, pltpu.roll(mid, 1, 0))
                shifted.append((after, mid, before))
            for strip in range(2):
                total = shifted[strip][1]
                for a, source in ((1, strip), (2 * strip, 1 - strip)):
                    for b in range(3):
                        total = total + kern[3 * a + b : 3 * a + b + 1] * shifted[source][b]
                where = (part * chunk) // (width // 2)
                offset = part * chunk - where * (width // 2)
                size = min(chunk, width // 2 - offset)
                rows = pl.ds(pl.multiple_of((strip * views + view) * columns, columns), columns)
                rounded = total.astype(jnp.bfloat16)
                up[where, rows, pl.ds(offset, size)] = rounded[:, :size]
                if size < chunk:
                    up[where + 1, rows, pl.ds(0, chunk - size)] = rounded[:, size:]
        return carry

    lax.fori_loop(0, views, conv_view, 0)

    for copy in loads:
        copy.wait()

    lane = lax.broadcasted_iota(jnp.int32, (queries, LANES), 1)

    def split_heads(out, rows_f):
        rounded = rows_f.astype(jnp.bfloat16).astype(jnp.float32)
        for pair in range(pairs):
            block = rounded[:, pair * LANES : (pair + 1) * LANES]
            out[pair, pl.ds(0, queries)] = jnp.where(lane < HEAD_DIM, block, 0.0).astype(jnp.bfloat16)
            out[pair, pl.ds(queries, queries)] = jnp.where(lane < HEAD_DIM, 0.0, block).astype(jnp.bfloat16)

    split_heads(qm, matmul(xo[...], wq[...]))
    og = matmul(up[0], wo[:, pl.ds(0, width // 2)], NT) + matmul(up[1], wo[:, pl.ds(width // 2, width // 2)], NT)
    split_heads(om, og)

    block_rows = key_rows // 4

    def project(i, carry):
        rows = pl.ds(pl.multiple_of(i * block_rows, 16), block_rows)
        out = matmul(x[rows], wkv[...]).astype(jnp.bfloat16)
        for pair in range(pairs):
            keys[pair, rows] = out[:, pair * LANES : (pair + 1) * LANES]
            values[pair, rows] = out[:, half + pair * LANES : half + (pair + 1) * LANES]
        return carry

    lax.fori_loop(0, 4, project, 0)

    eye = (
        lax.broadcasted_iota(jnp.int32, (LANES, LANES), 0) == lax.broadcasted_iota(jnp.int32, (LANES, LANES), 1)
    ).astype(jnp.float32).astype(jnp.bfloat16)

    def turn(j, carry):
        lanes = pl.ds(pl.multiple_of(j * LANES, LANES), LANES)
        xt[lanes] = matmul(eye, x[:, lanes], NT).astype(jnp.bfloat16)
        xot[lanes] = matmul(eye, xo[:, lanes], NT).astype(jnp.bfloat16)
        return carry

    lax.fori_loop(0, width // LANES, turn, 0)

    step = 64
    steps = key_rows // step

    def fold(v, op):
        return op(v.reshape(step // 8, 8, queries), axis=0)

    def one_pair(pair, carry):
        for head in range(2):
            mine = pl.ds(head * queries, queries)
            s_buf[...] = matmul(keys[pair], qm[pair, mine], NT)
            dp_buf[...] = matmul(values[pair], om[pair, mine], NT)

            def high(i, top):
                rows = pl.ds(pl.multiple_of(i * step, step), step)
                v = s_buf[rows] * scale + bias[rows]
                s_buf[rows] = v
                return jnp.maximum(top, fold(v, jnp.max))

            top = lax.fori_loop(0, steps, high, jnp.full((8, queries), -3e38, jnp.float32))
            top = jnp.max(top, axis=0, keepdims=True)

            def weigh(i, sums):
                rows = pl.ds(pl.multiple_of(i * step, step), step)
                e = jnp.exp(s_buf[rows] - top)
                s_buf[rows] = e
                return sums[0] + fold(e, jnp.sum), sums[1] + fold(e * dp_buf[rows], jnp.sum)

            zero = jnp.zeros((8, queries), jnp.float32)
            total, delta = lax.fori_loop(0, steps, weigh, (zero, zero))
            inverse = 1.0 / jnp.sum(total, axis=0, keepdims=True)
            delta = jnp.sum(delta, axis=0, keepdims=True) * inverse

            def finish(i, carry):
                rows = pl.ds(pl.multiple_of(i * step, step), step)
                p = s_buf[rows] * inverse
                p_buf[rows, mine] = p.astype(jnp.bfloat16)
                ds_buf[rows, mine] = (p * (dp_buf[rows] - delta) * scale).astype(jnp.bfloat16)
                return carry

            lax.fori_loop(0, steps, finish, 0)

        dkv[:, pl.ds(0, LANES)] = matmul(ds_buf[...], qm[pair]).astype(jnp.bfloat16)
        dkv[:, pl.ds(LANES, LANES)] = matmul(p_buf[...], om[pair]).astype(jnp.bfloat16)
        vt = matmul(eye, values[pair], NT).astype(jnp.bfloat16)
        kt = matmul(eye, keys[pair], NT).astype(jnp.bfloat16)
        mixed = matmul(vt, p_buf[...]).astype(jnp.bfloat16)
        dq = matmul(kt, ds_buf[...])
        row_of = pl.multiple_of(pair * LANES, LANES)
        mt[pl.ds(row_of, HEAD_DIM)] = mixed[:HEAD_DIM, :queries]
        mt[pl.ds(row_of + HEAD_DIM, HEAD_DIM)] = mixed[HEAD_DIM:, queries:]
        dqt = jnp.concatenate((dq[:HEAD_DIM, :queries], dq[HEAD_DIM:, queries:]), axis=0).astype(jnp.bfloat16)

        def grads(i, carry):
            rows = pl.ds(pl.multiple_of(i * (width // 4), width // 4), width // 4)
            blocks = pl.ds(i * 4, 4)
            gq = matmul(xot[rows], dqt, NT).astype(jnp.bfloat16)
            gkv = matmul(xt[rows], dkv[...]).astype(jnp.bfloat16)
            ga[pair, blocks, :, pl.ds(0, LANES)] = gq.reshape(4, width // 16, LANES)
            ga[pair, blocks, :, pl.ds(LANES, 2 * LANES)] = gkv.reshape(4, width // 16, 2 * LANES)
            return carry

        lax.fori_loop(0, 4, grads, 0)
        return carry

    lax.fori_loop(0, pairs, one_pair, 0)


def local_part(x, cot, taps, bias, wq, wk, wv, wo, groups):
    key_rows, width = x.shape
    queries = bias.shape[1]
    half = wq.shape[1] // 2
    pairs = half // LANES
    bf = jnp.bfloat16
    return pl.pallas_call(
        functools.partial(local_kernel, groups),
        out_shape=(
            jax.ShapeDtypeStruct((pairs, 16, width // 16, 3 * LANES), bf),
            jax.ShapeDtypeStruct((half, queries), bf),
            jax.ShapeDtypeStruct((2, queries, width // 2), bf),
        ),
        in_specs=vmem(4) + [pl.BlockSpec(memory_space=pl.ANY)] * 4,
        out_specs=tuple(vmem(3)),
        scratch_shapes=[
            pltpu.VMEM((width, half), bf),
            pltpu.VMEM((width, 2 * half), bf),
            pltpu.VMEM((half, width), bf),
            pltpu.VMEM((queries, width), bf),
            pltpu.VMEM((width, key_rows), bf),
            pltpu.VMEM((width, queries), bf),
            pltpu.VMEM((pairs, key_rows, LANES), bf),
            pltpu.VMEM((pairs, key_rows, LANES), bf),
            pltpu.VMEM((pairs, 2 * queries, LANES), bf),
            pltpu.VMEM((pairs, 2 * queries, LANES), bf),
            pltpu.VMEM((key_rows, queries), jnp.float32),
            pltpu.VMEM((key_rows, queries), jnp.float32),
            pltpu.VMEM((key_rows, 2 * queries), bf),
            pltpu.VMEM((key_rows, 2 * queries), bf),
            pltpu.VMEM((key_rows, 2 * LANES), bf),
            pltpu.SemaphoreType.DMA((4,)),
        ],
        compiler_params=pltpu.CompilerParams(vmem_limit_bytes=VMEM_LIMIT),
    )(x, cot, taps, bias, wq, wk, wv, wo)


def sums_kernel(
    ga, mt, up, out_a, out_o,
    mixed, o1, r1a, r1b, r1o, p2a, p2b, p2o, r2a, r2b, r2o, p3, p3o, r3, r3o, f_own, f_sib, fo_own, fo_sib,
    m_send, m_recv, s1, d1, s2, d2, s3, d3, s4, d4,
):
    xx, vv, core = lax.axis_index("scene"), lax.axis_index("view"), lax.axis_index("row")
    yy, zz = vv // 4, lax.rem(vv, 4)
    sibling = (xx, vv, 1 - core)

    def along(axis, step):
        if axis == 0:
            at = lax.rem(xx + step, 4)
            return at, (at, vv, core)
        if axis == 1:
            at = lax.rem(yy + step, 4)
            return at, (xx, at * 4 + zz, core)
        at = lax.rem(zz + step, 4)
        return at, (xx, yy * 4 + at, core)

    barrier = pltpu.get_barrier_semaphore()
    for axis in range(3):
        for step in range(1, 4):
            pl.semaphore_signal(barrier, inc=1, device_id=along(axis, step)[1], device_id_type=MESH)
    pl.semaphore_signal(barrier, inc=1, device_id=sibling, device_id_type=MESH)
    pl.semaphore_wait(barrier, 10)

    def remote(src, dst, send, recv, device):
        copy = pltpu.make_async_remote_copy(
            src_ref=src, dst_ref=dst, send_sem=send, recv_sem=recv, device_id=device, device_id_type=MESH
        )
        copy.start()
        return copy

    everything = []

    def send_three(axis, source, target, send, recv, base):
        copies = []
        for step in range(1, 4):
            at, device = along(axis, step)
            copies.append(
                remote(source(at), target.at[step - 1], send.at[base + step - 1], recv.at[base + step - 1], device)
            )
        everything.extend(copies)
        return copies

    swap = remote(mt, mixed.at[core], m_send, m_recv, sibling)
    first_a = send_three(0, lambda at: ga.at[0, at], r1a, s1, d1, 0)
    first_b = [
        send_three(1, lambda at, t=t: ga.at[t, :, at], r1b.at[t - 1], s1, d1, 3 * t) for t in (1, 2)
    ]
    mixed[core] = mt[...]
    swap.wait()
    channels = 2 * mt.shape[0]
    mixed_all = mixed[...].reshape(channels, mt.shape[1])
    half_up = up[core]
    for i in range(4):
        rows = channels // 4
        part = matmul(mixed_all[i * rows : (i + 1) * rows], half_up).astype(jnp.bfloat16)
        o1[i] = part.reshape(4, rows // 4, half_up.shape[1])
    first_o = send_three(0, lambda at: o1.at[at], r1o, s1, d1, 9)

    f32 = jnp.float32

    def collect(copies):
        for copy in copies:
            copy.wait_recv()

    collect(first_a)
    for j in range(4):
        p2a[j] = (
            ga[0, xx, j].astype(f32) + r1a[0, j].astype(f32) + r1a[1, j].astype(f32) + r1a[2, j].astype(f32)
        )
    second = [send_three(1, lambda at: p2a.at[at], r2a, s2, d2, 0)]
    for t in (0, 1):
        collect(first_b[t])
        for j in range(4):
            p2b[t, j] = (
                ga[t + 1, j, yy].astype(f32) + r1b[t, 0, j].astype(f32) + r1b[t, 1, j].astype(f32)
                + r1b[t, 2, j].astype(f32)
            )
        second.append(send_three(0, lambda at, t=t: p2b.at[t, at], r2b.at[t], s2, d2, 3 + 3 * t))
    collect(first_o)
    for j in range(4):
        p2o[j] = (
            o1[xx, j].astype(f32) + r1o[0, j].astype(f32) + r1o[1, j].astype(f32) + r1o[2, j].astype(f32)
        )
    second_o = send_three(1, lambda at: p2o.at[at], r2o, s2, d2, 9)

    third = []
    for t in range(3):
        collect(second[t])
        own, got = (p2a.at[yy], r2a) if t == 0 else (p2b.at[t - 1, xx], r2b.at[t - 1])
        whole = own[...] + got[0] + got[1] + got[2]
        rows = whole.shape[0] // 4
        for j in range(4):
            p3[t, j] = whole[j * rows : (j + 1) * rows]
        third.append(send_three(2, lambda at, t=t: p3.at[t, at], r3.at[t], s3, d3, 3 * t))
    collect(second_o)
    whole = p2o[yy] + r2o[0] + r2o[1] + r2o[2]
    rows = whole.shape[0] // 4
    for j in range(4):
        p3o[j] = whole[j * rows : (j + 1) * rows]
    third_o = send_three(2, lambda at: p3o.at[at], r3o, s3, d3, 9)

    for t in range(3):
        collect(third[t])
        whole = p3[t, zz] + r3[t, 0] + r3[t, 1] + r3[t, 2]
        rows = whole.shape[0] // 2
        for j in range(2):
            f_own[j, t] = whole[j * rows : (j + 1) * rows]
    last_a = remote(f_own.at[1 - core], f_sib, s4.at[0], d4.at[0], sibling)
    collect(third_o)
    whole = p3o[zz] + r3o[0] + r3o[1] + r3o[2]
    rows = whole.shape[0] // 2
    for j in range(2):
        fo_own[j] = whole[j * rows : (j + 1) * rows]
    last_o = remote(fo_own.at[1 - core], fo_sib, s4.at[1], d4.at[1], sibling)
    out_a[core] = f_own[core]
    out_o[core] = fo_own[core]
    last_a.wait()
    last_o.wait()
    out_a[1 - core] = f_sib[...]
    out_o[1 - core] = fo_sib[...]
    for copy in everything:
        copy.wait_send()


def chip_sums(ga, mt, up):
    pairs = ga.shape[0]
    rows, cols = ga.shape[2:]
    half, queries = mt.shape
    wide = up.shape[2]
    orows = 2 * half // 16
    bf, f32 = jnp.bfloat16, jnp.float32
    dma = pltpu.SemaphoreType.DMA
    ga = ga.reshape(pairs, 4, 4, rows, cols)
    return pl.pallas_call(
        sums_kernel,
        out_shape=(
            jax.ShapeDtypeStruct((2, pairs, rows // 8, cols), f32),
            jax.ShapeDtypeStruct((2, orows // 8, wide), f32),
        ),
        in_specs=vmem(3),
        out_specs=tuple(vmem(2)),
        scratch_shapes=[
            pltpu.VMEM((2, half, queries), bf),
            pltpu.VMEM((4, 4, orows, wide), bf),
            pltpu.VMEM((3, 4, rows, cols), bf),
            pltpu.VMEM((2, 3, 4, rows, cols), bf),
            pltpu.VMEM((3, 4, orows, wide), bf),
            pltpu.VMEM((4, rows, cols), f32),
            pltpu.VMEM((2, 4, rows, cols), f32),
            pltpu.VMEM((4, orows, wide), f32),
            pltpu.VMEM((3, rows, cols), f32),
            pltpu.VMEM((2, 3, rows, cols), f32),
            pltpu.VMEM((3, orows, wide), f32),
            pltpu.VMEM((3, 4, rows // 4, cols), f32),
            pltpu.VMEM((4, orows // 4, wide), f32),
            pltpu.VMEM((3, 3, rows // 4, cols), f32),
            pltpu.VMEM((3, orows // 4, wide), f32),
            pltpu.VMEM((2, 3, rows // 8, cols), f32),
            pltpu.VMEM((3, rows // 8, cols), f32),
            pltpu.VMEM((2, orows // 8, wide), f32),
            pltpu.VMEM((orows // 8, wide), f32),
            dma, dma, dma((12,)), dma((12,)), dma((12,)), dma((12,)), dma((12,)), dma((12,)), dma((2,)), dma((2,)),
        ],
        compiler_params=pltpu.CompilerParams(
            collective_id=1, has_side_effects=True, vmem_limit_bytes=VMEM_LIMIT
        ),
    )(ga, mt, up)


def shards(latents, norm_gain, w_query, w_key, w_value, w_out, kernel, partners, counts, cotangent):
    views, _, columns, width = latents.shape[1:]
    groups = lax.axis_size("view")
    me = lax.axis_index("view")
    lat_f = latents[0, :, 0].astype(jnp.float32)
    norm = (
        lat_f * lax.rsqrt(jnp.mean(lat_f * lat_f, -1, keepdims=True) + EPSILON) * norm_gain
    ).astype(jnp.bfloat16)

    partner_ids = partners[0]
    most = partner_ids.shape[1]
    alive = jnp.arange(most, dtype=jnp.int32)[None, :] < counts[0][:, None]
    source = jnp.where(alive, partner_ids // views, -1)
    matches = source[:, :, None] == jnp.arange(groups, dtype=jnp.int32)[None, None, :]
    wanted = jnp.max(jnp.where(matches, (partner_ids % views)[:, :, None], 0), axis=(0, 1))
    request = jnp.broadcast_to(wanted[:, None, None], (groups, 8, LANES))

    x, cot = exchange(norm, cotangent[0, :, 0], request, groups)

    slots = groups + views - 1
    view_of = jnp.arange(views, dtype=jnp.int32)
    slot_of = jnp.arange(slots, dtype=jnp.int32)
    home = jnp.where(view_of == 0, me, groups - 1 + view_of)
    seen = jnp.concatenate((jnp.any(matches, axis=1), jnp.zeros((views, views - 1), bool)), axis=1)
    seen = seen | (slot_of[None, :] == home[:, None])
    bias = jnp.where(seen.T, 0.0, -1e30).astype(jnp.float32)
    bias = jnp.broadcast_to(
        bias[None, :, None, None, :, None], (2, slots, columns, 2, views, columns)
    ).reshape(2 * slots * columns, 2 * views * columns)

    ga, mt, up = local_part(
        x.reshape(2 * slots * columns, width), cot, kernel, bias, w_query, w_key, w_value, w_out, groups
    )
    out_a, out_o = chip_sums(ga, mt, up)
    pairs, rows = out_a.shape[1:3]
    out_a = out_a.reshape(2, pairs, rows, 3, LANES).transpose(3, 2, 0, 1, 4).reshape(3, rows, 2 * pairs * LANES)
    out_o = out_o.transpose(1, 0, 2).reshape(out_o.shape[1], width)
    return out_a[0], out_a[1], out_a[2], out_o


def solution(mesh):
    strips = P("scene", "view", "row", None, None)
    return jax.shard_map(
        shards,
        mesh=mesh,
        in_specs=(
            strips, P(), P(), P(), P(), P(), P(),
            P("scene", "view", None), P("scene", "view"), strips,
        ),
        out_specs=(P(("scene", "view", "row"), None),) * 4,
        check_vma=False,
    )
```

time: 1320 us -> 149 us (0.11); the launches traced: 1300 us -> 149 us
  blocking collectives: 372 us -> 0 us
  starting transfers between devices: 356 us -> 0 us
  local copies, waits for them, and re-layouts: 367 us -> 14.1 us
  Pallas kernels: 0 us -> 130 us
  matrix products: 93.5 us -> 0 us
  waiting for transfers between devices: 57.4 us -> 0 us
  other arithmetic: 32.3 us -> 4.11 us
  between operations: 17.1 us -> 0.72 us
    unnamed x1 -> x0, blocking collectives: 369 us -> none
    unnamed x128 -> x0, starting transfers between devices: 324 us -> none
    unnamed x138 -> x1, local copies, waits for them, and re-layouts: 180 us -> 1.42 us
    reshape x9 -> x2, local copies, waits for them, and re-layouts: 154 us -> 5.96 us  [the longest x1 5.84 us: shards(): bias = jnp.broadcast_to(bias[None, :, None, None, :, None], (2, slots, co...]
    pallas_call x0 -> x3, Pallas kernels: none -> 130 us  [the longest x1 59.3 us: chip_sums(): pl.pallas_call(sums_kernel, out_shape=(jax.ShapeDtypeStruct((2, pairs, ro...]
    dot_general x15 -> x0, matrix products: 93.5 us -> none  [the longest x1 23.3 us: shards(): jnp.einsum('ujs,ujhwc->shwc', match_table, dpair[:, 1:], precision=lax.Pr...]
    all_to_all x3 -> x0, waiting for transfers between devices: 55.9 us -> none  [the longest x1 32.9 us: shards(): lax.all_to_all(returned_part, 'view', split_axis=0, concat_axis=0, tiled=...]
    all_to_all x3 -> x0, starting transfers between devices: 26.7 us -> none  [the longest x1 11 us: shards(): lax.all_to_all(returned_part, 'view', split_axis=0, concat_axis=0, tiled=...]
  transfers between devices with their start and end apart: 134 -> 0, of which waited for: 3 -> 0; matrix products, arithmetic and copies ran while one was open for 12% -> 0% of each run, Pallas kernels for 0% -> 0%
where the time goes in v1:
time: 149 us
  Pallas kernels  130 us (87%)
  local copies, waits for them, and re-layouts  14.1 us (9%)
  other arithmetic  4.11 us (3%)
    pallas_call x1, Pallas kernels, chip_sums(): pl.pallas_call(sums_kernel, out_shape=(jax.ShapeDtypeStruct((2, pairs, ro...  59.3 us
    pallas_call x1, Pallas kernels, exchange(): pl.pallas_call(functools.partial(exchange_kernel, groups), out_shape=(jax...  36.4 us
    pallas_call x1, Pallas kernels, local_part(): pl.pallas_call(functools.partial(local_kernel, groups), out_shape=(jax.Sh...  34.1 us
    reshape x1, local copies, waits for them, and re-layouts, shards(): bias = jnp.broadcast_to(bias[None, :, None, None, :, None], (2, slots, co...  5.84 us

profile of v1, /device:TPU:1, one launch (start us, length us, event | category | flops | bytes accessed | tf_op | source)
XLA Modules:
  0.0 148.7 jit_solution(4248820419916709068)
XLA Ops:
  0.6 1.1 fusion
  1.8 0.8 fusion.4
  2.6 0.1 select_reduce_fusion
  2.7 0.1 fusion.3
  2.8 0.1 select_bitcast_fusion
  2.8 0.1 copy.24
  2.9 0.7 broadcast_in_dim.48.request
  3.6 1.9 %fusion.2.norm = bf16[4,32,1536]{2,1,0:T(8,128)(2,1)} fusion(bf16[1,4,1,32,1536]{4,3,2,1,0:T(8,128)(2,1)} %param.10, f32[1536]{0:T(1024)} %param.11, f32[4,32]{1,0:T(4,128)S(1)} %add_rsqrt_fusion), kind=kLoop, calls=%fused_computation.4 | loop fusion | flops 786432 | bytes 793088 | tf_op jit(solution)/shard_map/convert_element_type | solution.py:502
  5.6 36.4 %shard_map.129 = (bf16[2,19,32,1536]{3,2,1,0:T(8,128)(2,1)}, bf16[2,4,32,1536]{3,2,1,0:T(8,128)(2,1)}) custom-call(bf16[4,32,1536]{2,1,0:T(8,128)(2,1)} %fusion.2.norm, bf16[4,32,1536]{2,1,0:T(8,128)(2,1)} %bitcast.43, s32[16,8,128]{2,1,0:T(8,128)} %broadcast_in_dim.48.request), custom_call_target="tpu_custom_call" | custom-call | tf_op jit(solution)/shard_map/pallas_call | solution.py:100
  41.9 2.9 %broadcast_in_dim.52 = f32[2,19,32,2,4,32]{5,4,3,2,1,0:T(4,128)} broadcast(f32[19,4]{1,0:T(8,128)S(1)} %copy.24), dimensions={1,4} | broadcast | bytes 1245488 | tf_op jit(solution)/shard_map/broadcast_in_dim | solution.py:521
  44.8 5.8 %reshape.125.bias = f32[1216,256]{1,0:T(8,128)} reshape(f32[2,19,32,2,4,32]{5,4,3,2,1,0:T(4,128)} %broadcast_in_dim.52) | data formatting | bytes 2490368 | tf_op jit(solution)/shard_map/reshape | solution.py:523
  50.7 34.1 %shard_map.130 = (bf16[3,16,96,384]{3,2,1,0:T(8,128)(2,1)}, bf16[384,256]{1,0:T(8,128)(2,1)}, bf16[2,256,768]{2,1,0:T(8,128)(2,1)}) custom-call(bf16[1216,1536]{1,0:T(8,128)(2,1)} %bitcast.40, bf16[2,4,32,1536]{3,2,1,0:T(8,128)(2,1)} %get-tuple-element.12.cot, bf16[9,1536]{1,0:T(8,128)(2,1)} %taps.1, f32[1216,256]{1,0:T(8,128)} %reshape.125.bias, ...), custom_call_target="tpu_custom_call" | custom-call | tf_op jit(solution)/shard_map/pallas_call | solution.py:292
  84.8 59.3 %shard_map.131 = (f32[2,3,12,384]{3,2,1,0:T(8,128)}, f32[2,6,768]{2,1,0:T(8,128)}) custom-call(bf16[3,4,4,96,384]{4,3,2,1,0:T(8,128)(2,1)} %bitcast.41, bf16[384,256]{1,0:T(8,128)(2,1)} %get-tuple-element.14.mt, bf16[2,256,768]{2,1,0:T(8,128)(2,1)} %get-tuple-element.15.up), custom_call_target="tpu_custom_call" | custom-call | tf_op jit(solution)/shard_map/pallas_call | solution.py:459
  144.1 1.0 copy.25
  145.0 0.1 reshape.127
  145.2 0.1 fusion.8
  145.3 0.6 squeeze.20
  145.9 0.6 squeeze.19
  146.6 0.6 squeeze.18
  147.2 1.4 copy.30
  (5 shorter events, 0.1 us)

commit v2 on v0

v2 whole, which is shorter than its diff:
```python
import functools

import jax
import jax.numpy as jnp
from jax import lax
from jax.experimental import pallas as pl
from jax.experimental.pallas import tpu as pltpu
from jax.sharding import PartitionSpec as P

HEAD_DIM = 64
LANES = 128
EPSILON = 1e-06
SIDE = 4
MESH = pl.DeviceIdType.MESH
VMEM_LIMIT = 62 * 1024 * 1024
NT = (((1,), (1,)), ((), ()))
NN = (((1,), (0,)), ((), ()))
BF = jnp.bfloat16
F32 = jnp.float32


def matmul(a, b, dims=NN):
    return lax.dot_general(a, b, dims, preferred_element_type=F32)


def kernel_body(
    lat, gain, cot, taps, partners, wq_hbm, wk_hbm, wv_hbm, wo_hbm,
    out_q, out_k, out_v, out_o,
    x, cot_all, ask, grant, outbuf, bias,
    wq, wkv, wo, xt, keys, values, qm, om, up, s_all, dp_all, tops, p_buf, ds_buf, dkv, mixed,
    gq, gk, gv, r1, p2, r2, p3, r3, f_own, f_sib,
    og, go_tmp, o1, po2, o2, po3, o3, fo_own, fo_sib,
    load_sem, own_send, own_recv, ask_send, ask_recv, out_send, out_recv, fwd_send, fwd_recv,
    mix_send, mix_recv, s1, d1, s2, d2, s3, d3, s4, d4,
):
    xx, me, core = lax.axis_index("scene"), lax.axis_index("view"), lax.axis_index("row")
    yy, zz = me // SIDE, lax.rem(me, SIDE)
    groups = SIDE * SIDE
    views, columns, width = lat.shape
    half = wq.shape[1]
    pairs = half // LANES
    slots = x.shape[0]
    slot_rows = 2 * columns
    key_rows = slots * slot_rows
    queries = views * slot_rows
    scale = HEAD_DIM ** (-0.5)
    sibling = (xx, me, 1 - core)

    def peer(step):
        return lax.rem(me + step, groups)

    def along(axis, step):
        if axis == 0:
            at = lax.rem(xx + step, SIDE)
            return at, (at, me, core)
        if axis == 1:
            at = lax.rem(yy + step, SIDE)
            return at, (xx, at * SIDE + zz, core)
        at = lax.rem(zz + step, SIDE)
        return at, (xx, yy * SIDE + at, core)

    barrier = pltpu.get_barrier_semaphore()
    for step in range(1, groups):
        pl.semaphore_signal(barrier, inc=1, device_id=(xx, peer(step), core), device_id_type=MESH)
    for step in range(1, SIDE):
        pl.semaphore_signal(barrier, inc=1, device_id=along(0, step)[1], device_id_type=MESH)
    pl.semaphore_signal(barrier, inc=1, device_id=sibling, device_id_type=MESH)

    cols = pl.ds(pl.multiple_of(core * half, LANES), half)
    loads = [
        pltpu.make_async_copy(wq_hbm.at[:, cols], wq, load_sem.at[0]),
        pltpu.make_async_copy(wk_hbm.at[:, cols], wkv.at[:, pl.ds(0, half)], load_sem.at[1]),
        pltpu.make_async_copy(wv_hbm.at[:, cols], wkv.at[:, pl.ds(half, half)], load_sem.at[2]),
        pltpu.make_async_copy(wo_hbm.at[cols, :], wo, load_sem.at[3]),
    ]
    for copy in loads:
        copy.start()

    steps_of = lax.broadcasted_iota(jnp.int32, (groups, LANES), 0)
    first_of = lax.rem(me + steps_of, groups) * views
    wanted = jnp.zeros((groups, LANES), jnp.int32)
    slot_of = lax.broadcasted_iota(jnp.int32, bias.shape, 0)
    view_of = lax.broadcasted_iota(jnp.int32, bias.shape, 1) // slot_rows
    slot_first = jnp.where(slot_of < views, -2 * views, lax.rem(me + groups + views - 1 - slot_of, groups) * views)
    seen = jnp.where(slot_of == view_of, 1, 0)
    for v in range(views):
        for j in range(partners.shape[1]):
            number = partners[v, j]
            local = number - first_of
            wanted = jnp.maximum(wanted, jnp.where((local >= 0) & (local < views), local, 0))
            local = number - slot_first
            hit = (local >= 0) & (local < views) & (view_of == v) & (number >= 0)
            seen = jnp.where(hit, 1, seen)
    bias[...] = jnp.where(seen > 0, 0.0, -1e30)
    for step in range(1, groups):
        ask[step] = jnp.broadcast_to(wanted[step : step + 1], ask.shape[1:])

    for v in range(views):
        rows = lat[v].astype(F32)
        mean = jnp.mean(rows * rows, -1, keepdims=True)
        x[v, core] = (rows * lax.rsqrt(mean + EPSILON) * gain[...]).astype(BF)
    cot_all[core] = cot[...]

    pl.semaphore_wait(barrier, groups + SIDE - 1)

    def remote(src, dst, send, recv, device):
        copy = pltpu.make_async_remote_copy(
            src_ref=src, dst_ref=dst, send_sem=send, recv_sem=recv, device_id=device, device_id_type=MESH
        )
        copy.start()
        return copy

    sent = []
    asks = [
        remote(ask.at[s], grant.at[s], ask_send.at[s], ask_recv.at[s], (xx, peer(s), core))
        for s in range(1, groups)
    ]
    mine = x.at[pl.ds(0, views), core]
    own_x = remote(mine, mine, own_send.at[0], own_recv.at[0], sibling)
    own_cot = remote(cot, cot_all.at[core], own_send.at[1], own_recv.at[1], sibling)

    blocks = []
    for s in range(1, groups):
        asks[groups - s - 1].wait_recv()
        want = grant[groups - s][0:1, 0:1]
        block = x[0, core]
        for v in range(1, views):
            block = jnp.where(want == v, x[v, core], block)
        outbuf[s - 1] = block
        blocks.append(
            remote(
                outbuf.at[s - 1], x.at[views - 1 + s, core], out_send.at[s], out_recv.at[s], (xx, peer(s), core)
            )
        )
    sent += asks + [own_x, own_cot] + blocks

    own_cot.wait_recv()
    chunk = 2 * LANES
    place = lax.broadcasted_iota(jnp.int32, (columns, chunk), 0)

    def conv_view(view, carry):
        for part in range(width // chunk):
            lanes = pl.ds(part * chunk, chunk)
            kern = taps[:, lanes].astype(F32)
            shifted = []
            for strip in range(2):
                mid = cot_all[strip, view, :, lanes].astype(F32)
                after = jnp.where(place == columns - 1, 0.0, pltpu.roll(mid, columns - 1, 0))
                before = jnp.where(place == 0, 0.0, pltpu.roll(mid, 1, 0))
                shifted.append((after, mid, before))
            for strip in range(2):
                total = shifted[strip][1]
                for a, source in ((1, strip), (2 * strip, 1 - strip)):
                    for b in range(3):
                        total = total + kern[3 * a + b : 3 * a + b + 1] * shifted[source][b]
                side = part * chunk // (width // 2)
                rows = pl.ds(pl.multiple_of(view * slot_rows + strip * columns, columns), columns)
                up[side, rows, pl.ds(part * chunk - side * (width // 2), chunk)] = total.astype(BF)
        return carry

    lax.fori_loop(0, views, conv_view, 0)

    for copy in loads:
        copy.wait()

    lane = lax.broadcasted_iota(jnp.int32, (queries, LANES), 1)

    def split_heads(out, rows_f):
        rounded = rows_f.astype(BF).astype(F32)
        for pair in range(pairs):
            block = rounded[:, pair * LANES : (pair + 1) * LANES]
            out[pair, pl.ds(0, queries)] = jnp.where(lane < HEAD_DIM, block, 0.0).astype(BF)
            out[pair, pl.ds(queries, queries)] = jnp.where(lane < HEAD_DIM, 0.0, block).astype(BF)

    split_heads(
        om,
        matmul(up[0], wo[:, pl.ds(0, width // 2)], NT) + matmul(up[1], wo[:, pl.ds(width // 2, width // 2)], NT),
    )
    own_x.wait_recv()
    split_heads(qm, matmul(x[pl.ds(0, views)].reshape(queries, width), wq[...]))

    tile = 2 * LANES
    eye = (
        lax.broadcasted_iota(jnp.int32, (tile, tile), 0) == lax.broadcasted_iota(jnp.int32, (tile, tile), 1)
    ).astype(F32).astype(BF)

    def fold(v, op):
        return op(v.reshape(v.shape[0] // 8, 8, v.shape[1]), axis=0)

    def batch(first, count):
        rows = pl.ds(first * slot_rows, count * slot_rows)
        flat = x[pl.ds(first, count)].reshape(count * slot_rows, width)
        out = matmul(flat, wkv[...]).astype(BF)
        for pair in range(pairs):
            keys[pair, rows] = out[:, pair * LANES : (pair + 1) * LANES]
            values[pair, rows] = out[:, half + pair * LANES : half + (pair + 1) * LANES]

        def turn(j, carry):
            lanes = pl.ds(pl.multiple_of(j * tile, tile), tile)
            part = x[pl.ds(first, count), :, :, lanes].reshape(count * slot_rows, tile)
            xt[lanes, rows] = matmul(eye, part, NT).astype(BF)
            return carry

        lax.fori_loop(0, width // tile, turn, 0)

        def score(pair, carry):
            for head in range(2):
                mine = pl.ds(head * queries, queries)
                s = matmul(keys[pair, rows], qm[pair, mine], NT) * scale
                top = jnp.full((8, queries), -3e38, F32) if first == 0 else tops[2 * pair + head]
                for i in range(count):
                    part = s[i * slot_rows : (i + 1) * slot_rows] + bias[pl.ds(first + i, 1)]
                    s_all[2 * pair + head, pl.ds((first + i) * slot_rows, slot_rows)] = part
                    top = jnp.maximum(top, fold(part, jnp.max))
                tops[2 * pair + head] = top
                dp_all[2 * pair + head, rows] = matmul(values[pair, rows], om[pair, mine], NT)
            return carry

        lax.fori_loop(0, pairs, score, 0)

    size = 4
    parts = [(i, min(size, slots - i)) for i in range(views, slots, size)]
    before = (0, views)
    forwards = []
    for first, count in parts:
        fresh = []
        for slot in range(first, first + count):
            s = slot - views + 1
            blocks[s - 1].wait_recv()
            place_x = x.at[slot, core]
            fresh.append(remote(place_x, place_x, fwd_send.at[s], fwd_recv.at[s], sibling))
        batch(*before)
        for copy in fresh:
            copy.wait_recv()
        forwards += fresh
        before = (first, count)
    batch(*before)
    sent += forwards

    def send_three(axis, source, target, send, recv, base):
        copies = []
        for step in range(1, SIDE):
            at, device = along(axis, step)
            copies.append(
                remote(source(at), target.at[step - 1], send.at[base + step - 1], recv.at[base + step - 1], device)
            )
        sent.extend(copies)
        return copies

    def collect(copies):
        for copy in copies:
            copy.wait_recv()

    place_of = (xx, yy, zz)
    orders = ((0, 1, 2), (1, 2, 0), (2, 0, 1))
    rows1 = gq.shape[3]
    rows2 = rows1 // SIDE

    def phase1(t):
        return [
            send_three(0, lambda at: gq.at[t, at], r1.at[t, 0], s1, d1, 9 * t),
            send_three(1, lambda at: gk.at[t, :, at], r1.at[t, 1], s1, d1, 9 * t + 3),
            send_three(2, lambda at: gv.at[t, at], r1.at[t, 2], s1, d1, 9 * t + 6),
        ]

    def phase2(t, arrived):
        copies = []
        for m in range(3):
            collect(arrived[m])
            for j in range(SIDE):
                own = (gq.at[t, xx, j], gk.at[t, j, yy], gv.at[t, zz, j])[m]
                total = own[...].astype(F32)
                for i in range(SIDE - 1):
                    total = total + r1[t, m, i, j].astype(F32)
                if m == 1:
                    for k in range(SIDE):
                        p2[t, m, k, pl.ds(j * rows2, rows2)] = total[k * rows2 : (k + 1) * rows2]
                else:
                    p2[t, m, j] = total
            copies.append(
                send_three(orders[m][1], lambda at, m=m: p2.at[t, m, at], r2.at[t, m], s2, d2, 9 * t + 3 * m)
            )
        return copies

    def phase3(t, arrived):
        copies = []
        for m in range(3):
            collect(arrived[m])
            total = p2[t, m, place_of[orders[m][1]]] + r2[t, m, 0] + r2[t, m, 1] + r2[t, m, 2]
            for j in range(SIDE):
                p3[t, m, j] = total[j * rows2 : (j + 1) * rows2]
            copies.append(
                send_three(orders[m][2], lambda at, m=m: p3.at[t, m, at], r3.at[t, m], s3, d3, 9 * t + 3 * m)
            )
        return copies

    outs = (out_q, out_k, out_v)

    def phase4(t, arrived):
        for m in range(3):
            collect(arrived[m])
            total = p3[t, m, place_of[orders[m][2]]] + r3[t, m, 0] + r3[t, m, 1] + r3[t, m, 2]
            for j in range(2):
                f_own[j, t, m] = total[j * (rows2 // 2) : (j + 1) * (rows2 // 2)]
            lanes = pl.ds(pl.multiple_of(core * half + t * LANES, LANES), LANES)
            outs[m][:, lanes] = f_own[core, t, m]
        copy = remote(f_own.at[1 - core, t], f_sib.at[t], s4.at[t], d4.at[t], sibling)
        sent.append(copy)
        return copy

    def finish(t, copy):
        copy.wait_recv()
        lanes = pl.ds(pl.multiple_of((1 - core) * half + t * LANES, LANES), LANES)
        for m in range(3):
            outs[m][:, lanes] = f_sib[t, m]

    step = 64
    steps = key_rows // step
    mixes = []

    def attend(t):
        for head in range(2):
            h = 2 * t + head
            mine = pl.ds(head * queries, queries)
            top = jnp.max(tops[h], axis=0, keepdims=True)

            def weigh(i, sums, h=h, top=top):
                rows = pl.ds(pl.multiple_of(i * step, step), step)
                e = jnp.exp(s_all[h, rows] - top)
                s_all[h, rows] = e
                return sums[0] + fold(e, jnp.sum), sums[1] + fold(e * dp_all[h, rows], jnp.sum)

            zero = jnp.zeros((8, queries), F32)
            total, delta = lax.fori_loop(0, steps, weigh, (zero, zero))
            inverse = 1.0 / jnp.sum(total, axis=0, keepdims=True)
            delta = jnp.sum(delta, axis=0, keepdims=True) * inverse

            def close(i, carry, h=h, mine=mine, inverse=inverse, delta=delta):
                rows = pl.ds(pl.multiple_of(i * step, step), step)
                p = s_all[h, rows] * inverse
                p_buf[rows, mine] = p.astype(BF)
                ds_buf[rows, mine] = (p * (dp_all[h, rows] - delta) * scale).astype(BF)
                return carry

            lax.fori_loop(0, steps, close, 0)

        small = eye[:LANES, :LANES]
        vt = matmul(small, values[t], NT).astype(BF)
        both = matmul(vt, p_buf[...]).astype(BF)
        mixed[core, pl.ds(t * LANES, HEAD_DIM)] = both[:HEAD_DIM, :queries]
        mixed[core, pl.ds(t * LANES + HEAD_DIM, HEAD_DIM)] = both[HEAD_DIM:, queries:]
        piece = mixed.at[core, pl.ds(t * LANES, LANES)]
        mixes.append(remote(piece, piece, mix_send.at[t], mix_recv.at[t], sibling))
        kt = matmul(small, keys[t], NT).astype(BF)
        dq = matmul(kt, ds_buf[...])
        dqt = jnp.concatenate((dq[:HEAD_DIM, :queries], dq[HEAD_DIM:, queries:]), axis=0).astype(BF)
        dkv[:, pl.ds(0, LANES)] = matmul(ds_buf[...], qm[t]).astype(BF)
        dkv[:, pl.ds(LANES, LANES)] = matmul(p_buf[...], om[t]).astype(BF)
        for i in range(SIDE):
            rows = pl.ds(i * (width // SIDE), width // SIDE)
            q_part = matmul(xt[rows, pl.ds(0, queries)], dqt, NT).astype(BF)
            gq[t, i] = q_part.reshape(SIDE, rows1, LANES)
            kv = matmul(xt[rows], dkv[...])
            gk[t, i] = kv[:, :LANES].astype(BF).reshape(SIDE, rows1, LANES)
            v_part = kv[:, LANES:]
            for z in range(SIDE):
                turned = jnp.concatenate(
                    [v_part[(SIDE * y + z) * rows2 : (SIDE * y + z + 1) * rows2] for y in range(SIDE)], axis=0
                )
                gv[t, z, i] = turned.astype(BF)

    first, second, third, last = {}, {}, {}, {}
    for t in range(pairs):
        attend(t)
        first[t] = phase1(t)
        if t >= 1:
            second[t - 1] = phase2(t - 1, first[t - 1])
        if t >= 2:
            third[t - 2] = phase3(t - 2, second[t - 2])
    sent += mixes

    collect(mixes)
    channels = 2 * half
    all_mixed = mixed[...].reshape(channels, queries)
    orows = og.shape[3]
    orows2 = orows // SIDE
    wide = og.shape[4]
    for i in range(SIDE):
        part = matmul(all_mixed[i * (channels // SIDE) : (i + 1) * (channels // SIDE)], up[core])
        for u in range(2):
            og[u, i] = part[:, u * wide : (u + 1) * wide].astype(BF).reshape(SIDE, orows, wide)
        for y in range(SIDE):
            for z in range(SIDE):
                top = (SIDE * y + z) * orows2
                go_tmp[z, pl.ds(y * orows2, orows2)] = part[top : top + orows2, 2 * wide : 3 * wide]
        for z in range(SIDE):
            og[2, z, i] = go_tmp[z].astype(BF)
    ofirst = [
        send_three(0, lambda at: og.at[0, at], o1.at[0], s1, d1, 9 * pairs),
        send_three(1, lambda at: og.at[1, :, at], o1.at[1], s1, d1, 9 * pairs + 3),
        send_three(2, lambda at: og.at[2, at], o1.at[2], s1, d1, 9 * pairs + 6),
    ]
    oorders = ((0, 1, 2), (1, 0, 2), (2, 0, 1))

    t = pairs - 1
    third[t - 1] = phase3(t - 1, second[t - 1])
    second[t] = phase2(t, first[t])
    osecond = []
    for u in range(3):
        collect(ofirst[u])
        for j in range(SIDE):
            own = (og.at[0, xx, j], og.at[1, j, yy], og.at[2, zz, j])[u]
            total = own[...].astype(F32)
            for i in range(SIDE - 1):
                total = total + o1[u, i, j].astype(F32)
            po2[u, j] = total
        osecond.append(
            send_three(oorders[u][1], lambda at, u=u: po2.at[u, at], o2.at[u], s2, d2, 9 * pairs + 3 * u)
        )
    last[t - 2] = phase4(t - 2, third[t - 2])
    third[t] = phase3(t, second[t])
    othird = []
    for u in range(3):
        collect(osecond[u])
        total = po2[u, place_of[oorders[u][1]]] + o2[u, 0] + o2[u, 1] + o2[u, 2]
        for j in range(SIDE):
            po3[u, j] = total[j * orows2 : (j + 1) * orows2]
        othird.append(
            send_three(oorders[u][2], lambda at, u=u: po3.at[u, at], o3.at[u], s3, d3, 9 * pairs + 3 * u)
        )
    last[t - 1] = phase4(t - 1, third[t - 1])
    last[t] = phase4(t, third[t])
    for u in range(3):
        collect(othird[u])
        total = po3[u, place_of[oorders[u][2]]] + o3[u, 0] + o3[u, 1] + o3[u, 2]
        for j in range(2):
            fo_own[j, u] = total[j * (orows2 // 2) : (j + 1) * (orows2 // 2)]
    olast = remote(fo_own.at[1 - core], fo_sib, s4.at[pairs], d4.at[pairs], sibling)
    sent.append(olast)
    for u in range(3):
        lanes = pl.ds(pl.multiple_of(core * (width // 2) + u * wide, LANES), wide)
        out_o[:, lanes] = fo_own[core, u]
    for t in range(pairs):
        finish(t, last[t])
    olast.wait_recv()
    for u in range(3):
        lanes = pl.ds(pl.multiple_of((1 - core) * (width // 2) + u * wide, LANES), wide)
        out_o[:, lanes] = fo_sib[u]
    for copy in sent:
        copy.wait_send()


def shards(latents, norm_gain, w_query, w_key, w_value, w_out, kernel, partners, counts, cotangent):
    del counts
    views, _, columns, width = latents.shape[1:]
    inner = w_query.shape[1]
    half = inner // 2
    pairs = half // LANES
    groups = lax.axis_size("view")
    slots = groups - 1 + views
    slot_rows = 2 * columns
    key_rows = slots * slot_rows
    queries = views * slot_rows
    rows1 = width // 16
    orows = inner // 16
    wide = width // 6
    vm = pltpu.VMEM
    dma = pltpu.SemaphoreType.DMA
    in_vmem = pl.BlockSpec(memory_space=pltpu.VMEM)
    in_hbm = pl.BlockSpec(memory_space=pl.ANY)
    units = 9 * (pairs + 1)
    return pl.pallas_call(
        kernel_body,
        out_shape=(jax.ShapeDtypeStruct((rows1 // 8, inner), F32),) * 3
        + (jax.ShapeDtypeStruct((orows // 8, width), F32),),
        in_specs=[in_vmem] * 4 + [pl.BlockSpec(memory_space=pltpu.SMEM)] + [in_hbm] * 4,
        out_specs=(in_vmem,) * 4,
        scratch_shapes=[
            vm((slots, 2, columns, width), BF),
            vm((2, views, columns, width), BF),
            vm((groups, 8, LANES), jnp.int32),
            vm((groups, 8, LANES), jnp.int32),
            vm((groups - 1, columns, width), BF),
            vm((24, queries), F32),
            vm((width, half), BF),
            vm((width, 2 * half), BF),
            vm((half, width), BF),
            vm((width, key_rows), BF),
            vm((pairs, key_rows, LANES), BF),
            vm((pairs, key_rows, LANES), BF),
            vm((pairs, 2 * queries, LANES), BF),
            vm((pairs, 2 * queries, LANES), BF),
            vm((2, queries, width // 2), BF),
            vm((2 * pairs, key_rows, queries), F32),
            vm((2 * pairs, key_rows, queries), F32),
            vm((2 * pairs, 8, queries), F32),
            vm((key_rows, 2 * queries), BF),
            vm((key_rows, 2 * queries), BF),
            vm((key_rows, 2 * LANES), BF),
            vm((2, half, queries), BF),
            vm((pairs, SIDE, SIDE, rows1, LANES), BF),
            vm((pairs, SIDE, SIDE, rows1, LANES), BF),
            vm((pairs, SIDE, SIDE, rows1, LANES), BF),
            vm((pairs, 3, SIDE - 1, SIDE, rows1, LANES), BF),
            vm((pairs, 3, SIDE, rows1, LANES), F32),
            vm((pairs, 3, SIDE - 1, rows1, LANES), F32),
            vm((pairs, 3, SIDE, rows1 // 4, LANES), F32),
            vm((pairs, 3, SIDE - 1, rows1 // 4, LANES), F32),
            vm((2, pairs, 3, rows1 // 8, LANES), F32),
            vm((pairs, 3, rows1 // 8, LANES), F32),
            vm((3, SIDE, SIDE, orows, wide), BF),
            vm((SIDE, orows, wide), F32),
            vm((3, SIDE - 1, SIDE, orows, wide), BF),
            vm((3, SIDE, orows, wide), F32),
            vm((3, SIDE - 1, orows, wide), F32),
            vm((3, SIDE, orows // 4, wide), F32),
            vm((3, SIDE - 1, orows // 4, wide), F32),
            vm((2, 3, orows // 8, wide), F32),
            vm((3, orows // 8, wide), F32),
            dma((4,)), dma((2,)), dma((2,)),
            dma((groups,)), dma((groups,)), dma((groups,)), dma((groups,)), dma((groups,)), dma((groups,)),
            dma((pairs,)), dma((pairs,)),
            dma((units,)), dma((units,)), dma((units,)), dma((units,)), dma((units,)), dma((units,)),
            dma((pairs + 1,)), dma((pairs + 1,)),
        ],
        compiler_params=pltpu.CompilerParams(
            collective_id=0, has_side_effects=True, vmem_limit_bytes=VMEM_LIMIT
        ),
    )(
        latents[0, :, 0], norm_gain.reshape(1, width), cotangent[0, :, 0], kernel, partners[0],
        w_query, w_key, w_value, w_out,
    )


def solution(mesh):
    strips = P("scene", "view", "row", None, None)
    return jax.shard_map(
        shards,
        mesh=mesh,
        in_specs=(
            strips, P(), P(), P(), P(), P(), P(),
            P("scene", "view", None), P("scene", "view"), strips,
        ),
        out_specs=(P(("scene", "view", "row"), None),) * 4,
        check_vma=False,
    )
```

time: 1320 us -> 99.6 us (0.08); the launches traced: 1300 us -> 99.2 us
  blocking collectives: 372 us -> 0 us
  local copies, waits for them, and re-layouts: 367 us -> 6.98 us
  starting transfers between devices: 356 us -> 0 us
  matrix products: 93.5 us -> 0 us
  Pallas kernels: 0 us -> 91.6 us
  waiting for transfers between devices: 57.4 us -> 0 us
  other arithmetic: 32.3 us -> 0 us
  between operations: 17.1 us -> 0.64 us
    unnamed x1 -> x0, blocking collectives: 369 us -> none
    unnamed x128 -> x0, starting transfers between devices: 324 us -> none
    unnamed x138 -> x4, local copies, waits for them, and re-layouts: 180 us -> 5.68 us
    reshape x9 -> x1, local copies, waits for them, and re-layouts: 154 us -> 1.3 us  [shards(): norm_gain.reshape(1, width)]
    dot_general x15 -> x0, matrix products: 93.5 us -> none  [the longest x1 23.3 us: shards(): jnp.einsum('ujs,ujhwc->shwc', match_table, dpair[:, 1:], precision=lax.Pr...]
    pallas_call x0 -> x1, Pallas kernels: none -> 91.6 us  [shards(): pl.pallas_call(kernel_body, out_shape=(jax.ShapeDtypeStruct((rows1 // 8,...]
    all_to_all x3 -> x0, waiting for transfers between devices: 55.9 us -> none  [the longest x1 32.9 us: shards(): lax.all_to_all(returned_part, 'view', split_axis=0, concat_axis=0, tiled=...]
    all_to_all x3 -> x0, starting transfers between devices: 26.7 us -> none  [the longest x1 11 us: shards(): lax.all_to_all(returned_part, 'view', split_axis=0, concat_axis=0, tiled=...]
  transfers between devices with their start and end apart: 134 -> 0, of which waited for: 3 -> 0; matrix products, arithmetic and copies ran while one was open for 12% -> 0% of each run, Pallas kernels for 0% -> 0%
where the time goes in v2:
time: 99.6 us; the launch traced here: 99.2 us
  Pallas kernels  91.6 us (92%)
  local copies, waits for them, and re-layouts  6.98 us (7%)
    pallas_call x1, Pallas kernels, shards(): pl.pallas_call(kernel_body, out_shape=(jax.ShapeDtypeStruct((rows1 // 8,...  91.6 us
    unnamed x4, local copies, waits for them, and re-layouts  5.68 us

profile of v2, /device:TPU:1, one launch (start us, length us, event | category | flops | bytes accessed | tf_op | source)
XLA Modules:
  0.0 99.2 jit_solution(1032615176908081570)
XLA Ops:
  0.6 1.3 %reshape.11.gain = f32[1,1536]{1,0:T(1,128)} reshape(f32[1536]{0:T(1024)} %param.11) | data formatting | bytes 12288 | tf_op jit(solution)/shard_map/reshape | solution.py:530
  1.9 91.6 %shard_map.120 = (f32[12,768]{1,0:T(8,128)}, f32[12,768]{1,0:T(8,128)}, f32[12,768]{1,0:T(8,128)}, f32[6,1536]{1,0:T(8,128)}) custom-call(bf16[4,32,1536]{2,1,0:T(8,128)(2,1)} %bitcast.3, f32[1,1536]{1,0:T(1,128)} %reshape.11.gain, bf16[4,32,1536]{2,1,0:T(8,128)(2,1)} %bitcast.4, bf16[9,1536]{1,0:T(8,128)(2,1)} %taps.1, s32[4,8]{1,0:T(4,128)} %bitcast.5, ...), custom_call_target="tpu_custom_call" | custom-call | tf_op jit(solution)/shard_map/pallas_call | solution.py:472
  93.5 1.4 %copy.17 = f32[12,768]{1,0:T(8,128)} copy(f32[12,768]{1,0:T(8,128)} %get-tuple-element.8) | data formatting | bytes 73728
  94.9 1.4 %copy.18 = f32[12,768]{1,0:T(8,128)} copy(f32[12,768]{1,0:T(8,128)} %get-tuple-element.9) | data formatting | bytes 73728
  96.4 1.4 %copy.19 = f32[12,768]{1,0:T(8,128)} copy(f32[12,768]{1,0:T(8,128)} %get-tuple-element.10) | data formatting | bytes 73728
  97.8 1.4 %copy.20 = f32[6,1536]{1,0:T(8,128)} copy(f32[6,1536]{1,0:T(8,128)} %get-tuple-element.11) | data formatting | bytes 73728

commit v3 on v2

--- a/solution.py
+++ b/solution.py
@@ -11,6 +11,11 @@
 LANES = 128
 EPSILON = 1e-06
 SIDE = 4
+OFFSETS = (
+    (2, 2), (1, 2), (2, 1), (3, 2), (2, 3), (0, 2), (2, 0), (1, 1),
+    (3, 3), (1, 3), (3, 1), (0, 1), (1, 0), (0, 3), (3, 0),
+)
+BATCHES = (4, 4, 4, 2, 1)
 MESH = pl.DeviceIdType.MESH
 VMEM_LIMIT = 62 * 1024 * 1024
 NT = (((1,), (1,)), ((), ()))
@@ -46,8 +51,17 @@
     scale = HEAD_DIM ** (-0.5)
     sibling = (xx, me, 1 - core)
 
+    def group_at(step, strip, sign):
+        a, b = OFFSETS[step - 1]
+        a, b = a + strip * (b - a), b + strip * (a - b)
+        return lax.rem(yy + SIDE + sign * a, SIDE) * SIDE + lax.rem(zz + SIDE + sign * b, SIDE)
+
     def peer(step):
-        return lax.rem(me + step, groups)
+        return group_at(step, core, 1)
+
+    def reverse(step):
+        a, b = OFFSETS[step - 1]
+        return OFFSETS.index(((SIDE - a) % SIDE, (SIDE - b) % SIDE)) + 1
 
     def along(axis, step):
         if axis == 0:
@@ -77,29 +91,16 @@
         copy.start()
 
     steps_of = lax.broadcasted_iota(jnp.int32, (groups, LANES), 0)
-    first_of = lax.rem(me + steps_of, groups) * views
+    first_of = jnp.full((groups, LANES), -2 * views, jnp.int32)
+    for s in range(1, groups):
+        first_of = jnp.where(steps_of == s, peer(s) * views, first_of)
     wanted = jnp.zeros((groups, LANES), jnp.int32)
-    slot_of = lax.broadcasted_iota(jnp.int32, bias.shape, 0)
-    view_of = lax.broadcasted_iota(jnp.int32, bias.shape, 1) // slot_rows
-    slot_first = jnp.where(slot_of < views, -2 * views, lax.rem(me + groups + views - 1 - slot_of, groups) * views)
-    seen = jnp.where(slot_of == view_of, 1, 0)
     for v in range(views):
         for j in range(partners.shape[1]):
-            number = partners[v, j]
-            local = number - first_of
+            local = partners[v, j] - first_of
             wanted = jnp.maximum(wanted, jnp.where((local >= 0) & (local < views), local, 0))
-            local = number - slot_first
-            hit = (local >= 0) & (local < views) & (view_of == v) & (number >= 0)
-            seen = jnp.where(hit, 1, seen)
-    bias[...] = jnp.where(seen > 0, 0.0, -1e30)
-    for step in range(1, groups):
-        ask[step] = jnp.broadcast_to(wanted[step : step + 1], ask.shape[1:])
-
-    for v in range(views):
-        rows = lat[v].astype(F32)
-        mean = jnp.mean(rows * rows, -1, keepdims=True)
-        x[v, core] = (rows * lax.rsqrt(mean + EPSILON) * gain[...]).astype(BF)
-    cot_all[core] = cot[...]
+    for s in range(1, groups):
+        ask[s] = jnp.broadcast_to(wanted[s : s + 1], ask.shape[1:])
 
     pl.semaphore_wait(barrier, groups + SIDE - 1)
 
@@ -115,14 +116,21 @@
         remote(ask.at[s], grant.at[s], ask_send.at[s], ask_recv.at[s], (xx, peer(s), core))
         for s in range(1, groups)
     ]
+    own_cot = remote(cot, cot_all.at[core], own_send.at[1], own_recv.at[1], sibling)
+
+    for v in range(views):
+        rows = lat[v].astype(F32)
+        mean = jnp.mean(rows * rows, -1, keepdims=True)
+        x[v, core] = (rows * lax.rsqrt(mean + EPSILON) * gain[...].reshape(1, width)).astype(BF)
+    cot_all[core] = cot[...]
+
     mine = x.at[pl.ds(0, views), core]
     own_x = remote(mine, mine, own_send.at[0], own_recv.at[0], sibling)
-    own_cot = remote(cot, cot_all.at[core], own_send.at[1], own_recv.at[1], sibling)
 
     blocks = []
     for s in range(1, groups):
-        asks[groups - s - 1].wait_recv()
-        want = grant[groups - s][0:1, 0:1]
+        asks[reverse(s) - 1].wait_recv()
+        want = grant[reverse(s)][0:1, 0:1]
         block = x[0, core]
         for v in range(1, views):
             block = jnp.where(want == v, x[v, core], block)
@@ -133,6 +141,25 @@
             )
         )
     sent += asks + [own_x, own_cot] + blocks
+
+    row_of = lax.broadcasted_iota(jnp.int32, (bias.shape[0], LANES), 0)
+    first_of = jnp.full(row_of.shape, -2 * views, jnp.int32)
+    for s in range(1, groups):
+        for strip in range(2):
+            first_of = jnp.where(row_of == 2 * (views - 1 + s) + strip, group_at(s, strip, -1) * views, first_of)
+    lane_of = lax.broadcasted_iota(jnp.int32, (bias.shape[0], LANES), 1)
+    seen = []
+    for v in range(views):
+        hit = jnp.where(row_of // 2 == v, 1, 0)
+        for j in range(partners.shape[1]):
+            number = partners[v, j]
+            local = number - first_of
+            hit = jnp.where((local >= 0) & (local < views) & (number >= 0), 1, hit)
+        seen.append(jnp.where(hit > 0, 0.0, -1e30))
+    for part in range(views // 2):
+        bias[:, pl.ds(part * LANES, LANES)] = jnp.where(
+            lane_of < slot_rows, seen[2 * part], seen[2 * part + 1]
+        )
 
     own_cot.wait_recv()
     chunk = 2 * LANES
@@ -208,9 +235,9 @@
                 mine = pl.ds(head * queries, queries)
                 s = matmul(keys[pair, rows], qm[pair, mine], NT) * scale
                 top = jnp.full((8, queries), -3e38, F32) if first == 0 else tops[2 * pair + head]
-                for i in range(count):
-                    part = s[i * slot_rows : (i + 1) * slot_rows] + bias[pl.ds(first + i, 1)]
-                    s_all[2 * pair + head, pl.ds((first + i) * slot_rows, slot_rows)] = part
+                for i in range(2 * count):
+                    part = s[i * columns : (i + 1) * columns] + bias[pl.ds(2 * first + i, 1)]
+                    s_all[2 * pair + head, pl.ds(first * slot_rows + i * columns, columns)] = part
                     top = jnp.maximum(top, fold(part, jnp.max))
                 tops[2 * pair + head] = top
                 dp_all[2 * pair + head, rows] = matmul(values[pair, rows], om[pair, mine], NT)
@@ -218,8 +245,7 @@
 
         lax.fori_loop(0, pairs, score, 0)
 
-    size = 4
-    parts = [(i, min(size, slots - i)) for i in range(views, slots, size)]
+    parts = [(views + sum(BATCHES[:i]), count) for i, count in enumerate(BATCHES)]
     before = (0, views)
     forwards = []
     for first, count in parts:
@@ -239,7 +265,7 @@
 
     def send_three(axis, source, target, send, recv, base):
         copies = []
-        for step in range(1, SIDE):
+        for step in (2, 1, 3):
             at, device = along(axis, step)
             copies.append(
                 remote(source(at), target.at[step - 1], send.at[base + step - 1], recv.at[base + step - 1], device)
@@ -267,16 +293,20 @@
         copies = []
         for m in range(3):
             collect(arrived[m])
+            totals = []
             for j in range(SIDE):
                 own = (gq.at[t, xx, j], gk.at[t, j, yy], gv.at[t, zz, j])[m]
                 total = own[...].astype(F32)
                 for i in range(SIDE - 1):
                     total = total + r1[t, m, i, j].astype(F32)
-                if m == 1:
-                    for k in range(SIDE):
-                        p2[t, m, k, pl.ds(j * rows2, rows2)] = total[k * rows2 : (k + 1) * rows2]
-                else:
-                    p2[t, m, j] = total
+                totals.append(total)
+            if m == 1:
+                totals = [
+                    jnp.concatenate([total[k * rows2 : (k + 1) * rows2] for total in totals], axis=0)
+                    for k in range(SIDE)
+                ]
+            for j in range(SIDE):
+                p2[t, m, j] = totals[j].astype(BF)
             copies.append(
                 send_three(orders[m][1], lambda at, m=m: p2.at[t, m, at], r2.at[t, m], s2, d2, 9 * t + 3 * m)
             )
@@ -286,7 +316,9 @@
         copies = []
         for m in range(3):
             collect(arrived[m])
-            total = p2[t, m, place_of[orders[m][1]]] + r2[t, m, 0] + r2[t, m, 1] + r2[t, m, 2]
+            total = p2[t, m, place_of[orders[m][1]]].astype(F32)
+            for i in range(SIDE - 1):
+                total = total + r2[t, m, i].astype(F32)
             for j in range(SIDE):
                 p3[t, m, j] = total[j * rows2 : (j + 1) * rows2]
             copies.append(
@@ -413,7 +445,7 @@
             total = own[...].astype(F32)
             for i in range(SIDE - 1):
                 total = total + o1[u, i, j].astype(F32)
-            po2[u, j] = total
+            po2[u, j] = total.astype(BF)
         osecond.append(
             send_three(oorders[u][1], lambda at, u=u: po2.at[u, at], o2.at[u], s2, d2, 9 * pairs + 3 * u)
         )
@@ -422,7 +454,9 @@
     othird = []
     for u in range(3):
         collect(osecond[u])
-        total = po2[u, place_of[oorders[u][1]]] + o2[u, 0] + o2[u, 1] + o2[u, 2]
+        total = po2[u, place_of[oorders[u][1]]].astype(F32)
+        for i in range(SIDE - 1):
+            total = total + o2[u, i].astype(F32)
         for j in range(SIDE):
             po3[u, j] = total[j * orows2 : (j + 1) * orows2]
         othird.append(
@@ -450,6 +484,19 @@
         copy.wait_send()
 
 
+def leave_kernel(*refs):
+    count = len(refs) // 2
+    for source, target in zip(refs[:count], refs[count:]):
+        target[...] = source[...]
+
+
+def leave(*results):
+    return pl.pallas_call(
+        leave_kernel,
+        out_shape=tuple(jax.ShapeDtypeStruct(r.shape, r.dtype) for r in results),
+    )(*results)
+
+
 def shards(latents, norm_gain, w_query, w_key, w_value, w_out, kernel, partners, counts, cotangent):
     del counts
     views, _, columns, width = latents.shape[1:]
@@ -469,7 +516,7 @@
     in_vmem = pl.BlockSpec(memory_space=pltpu.VMEM)
     in_hbm = pl.BlockSpec(memory_space=pl.ANY)
     units = 9 * (pairs + 1)
-    return pl.pallas_call(
+    results = pl.pallas_call(
         kernel_body,
         out_shape=(jax.ShapeDtypeStruct((rows1 // 8, inner), F32),) * 3
         + (jax.ShapeDtypeStruct((orows // 8, width), F32),),
@@ -481,7 +528,7 @@
             vm((groups, 8, LANES), jnp.int32),
             vm((groups, 8, LANES), jnp.int32),
             vm((groups - 1, columns, width), BF),
-            vm((24, queries), F32),
+            vm((48, queries), F32),
             vm((width, half), BF),
             vm((width, 2 * half), BF),
             vm((half, width), BF),
@@ -502,8 +549,8 @@
             vm((pairs, SIDE, SIDE, rows1, LANES), BF),
             vm((pairs, SIDE, SIDE, rows1, LANES), BF),
             vm((pairs, 3, SIDE - 1, SIDE, rows1, LANES), BF),
-            vm((pairs, 3, SIDE, rows1, LANES), F32),
-            vm((pairs, 3, SIDE - 1, rows1, LANES), F32),
+            vm((pairs, 3, SIDE, rows1, LANES), BF),
+            vm((pairs, 3, SIDE - 1, rows1, LANES), BF),
             vm((pairs, 3, SIDE, rows1 // 4, LANES), F32),
             vm((pairs, 3, SIDE - 1, rows1 // 4, LANES), F32),
             vm((2, pairs, 3, rows1 // 8, LANES), F32),
@@ -511,8 +558,8 @@
             vm((3, SIDE, SIDE, orows, wide), BF),
             vm((SIDE, orows, wide), F32),
             vm((3, SIDE - 1, SIDE, orows, wide), BF),
-            vm((3, SIDE, orows, wide), F32),
-            vm((3, SIDE - 1, orows, wide), F32),
+            vm((3, SIDE, orows, wide), BF),
+            vm((3, SIDE - 1, orows, wide), BF),
             vm((3, SIDE, orows // 4, wide), F32),
             vm((3, SIDE - 1, orows // 4, wide), F32),
             vm((2, 3, orows // 8, wide), F32),
@@ -527,9 +574,10 @@
             collective_id=0, has_side_effects=True, vmem_limit_bytes=VMEM_LIMIT
         ),
     )(
-        latents[0, :, 0], norm_gain.reshape(1, width), cotangent[0, :, 0], kernel, partners[0],
+        latents[0, :, 0], norm_gain, cotangent[0, :, 0], kernel, partners[0],
         w_query, w_key, w_value, w_out,
     )
+    return leave(*results)
 
 
 def solution(mesh):

time: 99.6 us -> 88.4 us (0.89)
  local copies, waits for them, and re-layouts: 6.98 us -> 0 us
  Pallas kernels: 91.6 us -> 87.5 us
    unnamed x4 -> x0, local copies, waits for them, and re-layouts: 5.68 us -> none
    pallas_call x1, Pallas kernels: 91.6 us -> 86 us  [shards(): pl.pallas_call(kernel_body, out_shape=(jax.ShapeDtypeStruct((rows1 // 8,...]
    pallas_call x0 -> x1, Pallas kernels: none -> 1.55 us  [leave(): pl.pallas_call(leave_kernel, out_shape=tuple((jax.ShapeDtypeStruct(r.shap...]
    reshape x1 -> x0, local copies, waits for them, and re-layouts: 1.3 us -> none  [shards(): norm_gain.reshape(1, width)]
where the time goes in v3:
time: 88.4 us; the launch traced here: 88.2 us
  Pallas kernels  87.5 us (99%)
    pallas_call x1, Pallas kernels, shards(): pl.pallas_call(kernel_body, out_shape=(jax.ShapeDtypeStruct((rows1 // 8,...  86 us

profile of v3, /device:TPU:1, one launch (start us, length us, event | category | flops | bytes accessed | tf_op | source)
XLA Modules:
  0.0 88.2 jit_solution(8351918573459540343)
XLA Ops:
  0.6 86.0 %shard_map.120 = (f32[12,768]{1,0:T(8,128)}, f32[12,768]{1,0:T(8,128)}, f32[12,768]{1,0:T(8,128)}, f32[6,1536]{1,0:T(8,128)}) custom-call(bf16[4,32,1536]{2,1,0:T(8,128)(2,1)} %bitcast.3, f32[1536]{0:T(1024)} %gain.1, bf16[4,32,1536]{2,1,0:T(8,128)(2,1)} %bitcast.4, bf16[9,1536]{1,0:T(8,128)(2,1)} %taps.1, s32[4,8]{1,0:T(4,128)} %bitcast.5, ...), custom_call_target="tpu_custom_call" | custom-call | tf_op jit(solution)/shard_map/pallas_call | solution.py:519
  86.6 1.5 %shard_map.121 = (f32[12,768]{1,0:T(8,128)}, f32[12,768]{1,0:T(8,128)}, f32[12,768]{1,0:T(8,128)}, f32[6,1536]{1,0:T(8,128)}) custom-call(f32[12,768]{1,0:T(8,128)} %get-tuple-element.8.refs_0_, f32[12,768]{1,0:T(8,128)} %get-tuple-element.9.refs_1_, f32[12,768]{1,0:T(8,128)} %get-tuple-element.10.refs_2_, f32[6,1536]{1,0:T(8,128)} %get-tuple-element.11.refs_3_), custom_call_target="tpu_custom_call" | custom-call | tf_op jit(solution)/shard_map/pallas_call | solution.py:494

commit v4 on v3

--- a/solution.py
+++ b/solution.py
@@ -12,8 +12,8 @@
 EPSILON = 1e-06
 SIDE = 4
 OFFSETS = (
-    (2, 2), (1, 2), (2, 1), (3, 2), (2, 3), (0, 2), (2, 0), (1, 1),
-    (3, 3), (1, 3), (3, 1), (0, 1), (1, 0), (0, 3), (3, 0),
+    (0, 1), (1, 0), (0, 3), (3, 0), (2, 2), (1, 1), (3, 3), (0, 2),
+    (2, 0), (1, 3), (3, 1), (1, 2), (2, 1), (3, 2), (2, 3),
 )
 BATCHES = (4, 4, 4, 2, 1)
 MESH = pl.DeviceIdType.MESH
@@ -32,7 +32,7 @@
     lat, gain, cot, taps, partners, wq_hbm, wk_hbm, wv_hbm, wo_hbm,
     out_q, out_k, out_v, out_o,
     x, cot_all, ask, grant, outbuf, bias,
-    wq, wkv, wo, xt, keys, values, qm, om, up, s_all, dp_all, tops, p_buf, ds_buf, dkv, mixed,
+    wq, wkv, wo, xt, keys, values, qm, om, qmt, omt, up, s_all, dp_all, tops, p_buf, ds_buf, dkv, mixed,
     gq, gk, gv, r1, p2, r2, p3, r3, f_own, f_sib,
     og, go_tmp, o1, po2, o2, po3, o3, fo_own, fo_sib,
     load_sem, own_send, own_recv, ask_send, ask_recv, out_send, out_recv, fwd_send, fwd_recv,
@@ -157,9 +157,9 @@
             hit = jnp.where((local >= 0) & (local < views) & (number >= 0), 1, hit)
         seen.append(jnp.where(hit > 0, 0.0, -1e30))
     for part in range(views // 2):
-        bias[:, pl.ds(part * LANES, LANES)] = jnp.where(
-            lane_of < slot_rows, seen[2 * part], seen[2 * part + 1]
-        )
+        both = jnp.where(lane_of < slot_rows, seen[2 * part], seen[2 * part + 1])
+        for head in range(2):
+            bias[:, pl.ds(head * queries + part * LANES, LANES)] = both
 
     own_cot.wait_recv()
     chunk = 2 * LANES
@@ -191,25 +191,26 @@
         copy.wait()
 
     lane = lax.broadcasted_iota(jnp.int32, (queries, LANES), 1)
-
-    def split_heads(out, rows_f):
+    sublane = lax.broadcasted_iota(jnp.int32, (LANES, queries), 0)
+
+    def split_heads(out, turned, rows_f):
         rounded = rows_f.astype(BF).astype(F32)
         for pair in range(pairs):
             block = rounded[:, pair * LANES : (pair + 1) * LANES]
             out[pair, pl.ds(0, queries)] = jnp.where(lane < HEAD_DIM, block, 0.0).astype(BF)
             out[pair, pl.ds(queries, queries)] = jnp.where(lane < HEAD_DIM, 0.0, block).astype(BF)
+            block = block.T
+            turned[pair, :, pl.ds(0, queries)] = jnp.where(sublane < HEAD_DIM, block, 0.0).astype(BF)
+            turned[pair, :, pl.ds(queries, queries)] = jnp.where(sublane < HEAD_DIM, 0.0, block).astype(BF)
 
     split_heads(
-        om,
+        om, omt,
         matmul(up[0], wo[:, pl.ds(0, width // 2)], NT) + matmul(up[1], wo[:, pl.ds(width // 2, width // 2)], NT),
     )
     own_x.wait_recv()
-    split_heads(qm, matmul(x[pl.ds(0, views)].reshape(queries, width), wq[...]))
+    split_heads(qm, qmt, matmul(x[pl.ds(0, views)].reshape(queries, width), wq[...]))
 
     tile = 2 * LANES
-    eye = (
-        lax.broadcasted_iota(jnp.int32, (tile, tile), 0) == lax.broadcasted_iota(jnp.int32, (tile, tile), 1)
-    ).astype(F32).astype(BF)
 
     def fold(v, op):
         return op(v.reshape(v.shape[0] // 8, 8, v.shape[1]), axis=0)
@@ -222,31 +223,23 @@
             keys[pair, rows] = out[:, pair * LANES : (pair + 1) * LANES]
             values[pair, rows] = out[:, half + pair * LANES : half + (pair + 1) * LANES]
 
-        def turn(j, carry):
-            lanes = pl.ds(pl.multiple_of(j * tile, tile), tile)
-            part = x[pl.ds(first, count), :, :, lanes].reshape(count * slot_rows, tile)
-            xt[lanes, rows] = matmul(eye, part, NT).astype(BF)
-            return carry
-
-        lax.fori_loop(0, width // tile, turn, 0)
-
-        def score(pair, carry):
-            for head in range(2):
-                mine = pl.ds(head * queries, queries)
-                s = matmul(keys[pair, rows], qm[pair, mine], NT) * scale
-                top = jnp.full((8, queries), -3e38, F32) if first == 0 else tops[2 * pair + head]
-                for i in range(2 * count):
-                    part = s[i * columns : (i + 1) * columns] + bias[pl.ds(2 * first + i, 1)]
-                    s_all[2 * pair + head, pl.ds(first * slot_rows + i * columns, columns)] = part
-                    top = jnp.maximum(top, fold(part, jnp.max))
-                tops[2 * pair + head] = top
-                dp_all[2 * pair + head, rows] = matmul(values[pair, rows], om[pair, mine], NT)
-            return carry
-
-        lax.fori_loop(0, pairs, score, 0)
+        for j in range(width // tile):
+            lanes = pl.ds(j * tile, tile)
+            xt[lanes, rows] = flat[:, j * tile : (j + 1) * tile].T
+
+        for pair in range(pairs):
+            s = matmul(keys[pair, rows], qmt[pair]) * scale
+            top = jnp.full((8, 2 * queries), -3e38, F32) if first == 0 else tops[pair]
+            for i in range(2 * count):
+                part = s[i * columns : (i + 1) * columns] + bias[pl.ds(2 * first + i, 1)]
+                s_all[pair, pl.ds(first * slot_rows + i * columns, columns)] = part
+                top = jnp.maximum(top, fold(part, jnp.max))
+            tops[pair] = top
+            dp_all[pair, rows] = matmul(values[pair, rows], omt[pair])
 
     parts = [(views + sum(BATCHES[:i]), count) for i, count in enumerate(BATCHES)]
-    before = (0, views)
+    before = None
+    batch(0, views)
     forwards = []
     for first, count in parts:
         fresh = []
@@ -255,7 +248,8 @@
             blocks[s - 1].wait_recv()
             place_x = x.at[slot, core]
             fresh.append(remote(place_x, place_x, fwd_send.at[s], fwd_recv.at[s], sibling))
-        batch(*before)
+        if before:
+            batch(*before)
         for copy in fresh:
             copy.wait_recv()
         forwards += fresh
@@ -351,46 +345,41 @@
     mixes = []
 
     def attend(t):
-        for head in range(2):
-            h = 2 * t + head
-            mine = pl.ds(head * queries, queries)
-            top = jnp.max(tops[h], axis=0, keepdims=True)
-
-            def weigh(i, sums, h=h, top=top):
-                rows = pl.ds(pl.multiple_of(i * step, step), step)
-                e = jnp.exp(s_all[h, rows] - top)
-                s_all[h, rows] = e
-                return sums[0] + fold(e, jnp.sum), sums[1] + fold(e * dp_all[h, rows], jnp.sum)
-
-            zero = jnp.zeros((8, queries), F32)
-            total, delta = lax.fori_loop(0, steps, weigh, (zero, zero))
-            inverse = 1.0 / jnp.sum(total, axis=0, keepdims=True)
-            delta = jnp.sum(delta, axis=0, keepdims=True) * inverse
-
-            def close(i, carry, h=h, mine=mine, inverse=inverse, delta=delta):
-                rows = pl.ds(pl.multiple_of(i * step, step), step)
-                p = s_all[h, rows] * inverse
-                p_buf[rows, mine] = p.astype(BF)
-                ds_buf[rows, mine] = (p * (dp_all[h, rows] - delta) * scale).astype(BF)
-                return carry
-
-            lax.fori_loop(0, steps, close, 0)
-
-        small = eye[:LANES, :LANES]
-        vt = matmul(small, values[t], NT).astype(BF)
-        both = matmul(vt, p_buf[...]).astype(BF)
+        top = jnp.max(tops[t], axis=0, keepdims=True)
+
+        def weigh(i, sums):
+            rows = pl.ds(pl.multiple_of(i * step, step), step)
+            e = jnp.exp(s_all[t, rows] - top)
+            s_all[t, rows] = e
+            return sums[0] + fold(e, jnp.sum), sums[1] + fold(e * dp_all[t, rows], jnp.sum)
+
+        zero = jnp.zeros((8, 2 * queries), F32)
+        total, delta = lax.fori_loop(0, steps, weigh, (zero, zero))
+        inverse = 1.0 / jnp.sum(total, axis=0, keepdims=True)
+        delta = jnp.sum(delta, axis=0, keepdims=True) * inverse
+        scaled = inverse * scale
+
+        def close(i, carry):
+            rows = pl.ds(pl.multiple_of(i * step, step), step)
+            e = s_all[t, rows]
+            p_buf[rows] = (e * inverse).astype(BF)
+            ds_buf[rows] = (e * scaled * (dp_all[t, rows] - delta)).astype(BF)
+            return carry
+
+        lax.fori_loop(0, steps, close, 0)
+
+        both = matmul(values[t].T, p_buf[...]).astype(BF)
         mixed[core, pl.ds(t * LANES, HEAD_DIM)] = both[:HEAD_DIM, :queries]
         mixed[core, pl.ds(t * LANES + HEAD_DIM, HEAD_DIM)] = both[HEAD_DIM:, queries:]
         piece = mixed.at[core, pl.ds(t * LANES, LANES)]
         mixes.append(remote(piece, piece, mix_send.at[t], mix_recv.at[t], sibling))
-        kt = matmul(small, keys[t], NT).astype(BF)
-        dq = matmul(kt, ds_buf[...])
-        dqt = jnp.concatenate((dq[:HEAD_DIM, :queries], dq[HEAD_DIM:, queries:]), axis=0).astype(BF)
+        dq = matmul(keys[t].T, ds_buf[...])
+        dq = jnp.concatenate((dq[:HEAD_DIM, :queries], dq[HEAD_DIM:, queries:]), axis=0).T.astype(BF)
         dkv[:, pl.ds(0, LANES)] = matmul(ds_buf[...], qm[t]).astype(BF)
         dkv[:, pl.ds(LANES, LANES)] = matmul(p_buf[...], om[t]).astype(BF)
         for i in range(SIDE):
             rows = pl.ds(i * (width // SIDE), width // SIDE)
-            q_part = matmul(xt[rows, pl.ds(0, queries)], dqt, NT).astype(BF)
+            q_part = matmul(xt[rows, pl.ds(0, queries)], dq).astype(BF)
             gq[t, i] = q_part.reshape(SIDE, rows1, LANES)
             kv = matmul(xt[rows], dkv[...])
             gk[t, i] = kv[:, :LANES].astype(BF).reshape(SIDE, rows1, LANES)
@@ -528,7 +517,7 @@
             vm((groups, 8, LANES), jnp.int32),
             vm((groups, 8, LANES), jnp.int32),
             vm((groups - 1, columns, width), BF),
-            vm((48, queries), F32),
+            vm((48, 2 * queries), F32),
             vm((width, half), BF),
             vm((width, 2 * half), BF),
             vm((half, width), BF),
@@ -537,10 +526,12 @@
             vm((pairs, key_rows, LANES), BF),
             vm((pairs, 2 * queries, LANES), BF),
             vm((pairs, 2 * queries, LANES), BF),
+            vm((pairs, LANES, 2 * queries), BF),
+            vm((pairs, LANES, 2 * queries), BF),
             vm((2, queries, width // 2), BF),
-            vm((2 * pairs, key_rows, queries), F32),
-            vm((2 * pairs, key_rows, queries), F32),
-            vm((2 * pairs, 8, queries), F32),
+            vm((pairs, key_rows, 2 * queries), F32),
+            vm((pairs, key_rows, 2 * queries), F32),
+            vm((pairs, 8, 2 * queries), F32),
             vm((key_rows, 2 * queries), BF),
             vm((key_rows, 2 * queries), BF),
             vm((key_rows, 2 * LANES), BF),

time: 88.4 us -> 81.8 us (0.925)
  Pallas kernels: 87.5 us -> 81 us
    pallas_call x1, Pallas kernels: 86 us -> 79.5 us  [shards(): pl.pallas_call(kernel_body, out_shape=(jax.ShapeDtypeStruct((rows1 // 8,...]
where the time goes in v4:
time: 81.8 us; the launch traced here: 81.6 us
  Pallas kernels  81 us (99%)
    pallas_call x1, Pallas kernels, shards(): pl.pallas_call(kernel_body, out_shape=(jax.ShapeDtypeStruct((rows1 // 8,...  79.5 us

profile of v4, /device:TPU:1, one launch (start us, length us, event | category | flops | bytes accessed | tf_op | source)
XLA Modules:
  0.0 81.6 jit_solution(8947339219945758913)
XLA Ops:
  0.6 79.5 %shard_map.120 = (f32[12,768]{1,0:T(8,128)}, f32[12,768]{1,0:T(8,128)}, f32[12,768]{1,0:T(8,128)}, f32[6,1536]{1,0:T(8,128)}) custom-call(bf16[4,32,1536]{2,1,0:T(8,128)(2,1)} %bitcast.3, f32[1536]{0:T(1024)} %gain.1, bf16[4,32,1536]{2,1,0:T(8,128)(2,1)} %bitcast.4, bf16[9,1536]{1,0:T(8,128)(2,1)} %taps.1, s32[4,8]{1,0:T(4,128)} %bitcast.5, ...), custom_call_target="tpu_custom_call" | custom-call | tf_op jit(solution)/shard_map/pallas_call | solution.py:508
  80.1 1.5 %shard_map.121 = (f32[12,768]{1,0:T(8,128)}, f32[12,768]{1,0:T(8,128)}, f32[12,768]{1,0:T(8,128)}, f32[6,1536]{1,0:T(8,128)}) custom-call(f32[12,768]{1,0:T(8,128)} %get-tuple-element.8.refs_0_, f32[12,768]{1,0:T(8,128)} %get-tuple-element.9.refs_1_, f32[12,768]{1,0:T(8,128)} %get-tuple-element.10.refs_2_, f32[6,1536]{1,0:T(8,128)} %get-tuple-element.11.refs_3_), custom_call_target="tpu_custom_call" | custom-call | tf_op jit(solution)/shard_map/pallas_call | solution.py:483

commit v5 on v4

--- a/solution.py
+++ b/solution.py
@@ -33,10 +33,10 @@
     out_q, out_k, out_v, out_o,
     x, cot_all, ask, grant, outbuf, bias,
     wq, wkv, wo, xt, keys, values, qm, om, qmt, omt, up, s_all, dp_all, tops, p_buf, ds_buf, dkv, mixed,
-    gq, gk, gv, r1, p2, r2, p3, r3, f_own, f_sib,
-    og, go_tmp, o1, po2, o2, po3, o3, fo_own, fo_sib,
+    gk, gv, r1, p2, r2, stage, got, near,
+    xn_r, xq, up_r, dq_all, mx_r, q2, rq2, stage_q, got_q, near_q, o2, ro2, stage_o, got_o, near_o,
     load_sem, own_send, own_recv, ask_send, ask_recv, out_send, out_recv, fwd_send, fwd_recv,
-    mix_send, mix_recv, s1, d1, s2, d2, s3, d3, s4, d4,
+    mix_send, mix_recv, x_send, x_recv, s1, d1, s2, d2, s3, d3,
 ):
     xx, me, core = lax.axis_index("scene"), lax.axis_index("view"), lax.axis_index("row")
     yy, zz = me // SIDE, lax.rem(me, SIDE)
@@ -78,6 +78,9 @@
         pl.semaphore_signal(barrier, inc=1, device_id=(xx, peer(step), core), device_id_type=MESH)
     for step in range(1, SIDE):
         pl.semaphore_signal(barrier, inc=1, device_id=along(0, step)[1], device_id_type=MESH)
+        for axis in range(3):
+            there = along(axis, step)[1][:2] + (1 - core,)
+            pl.semaphore_signal(barrier, inc=1, device_id=there, device_id_type=MESH)
     pl.semaphore_signal(barrier, inc=1, device_id=sibling, device_id_type=MESH)
 
     cols = pl.ds(pl.multiple_of(core * half, LANES), half)
@@ -102,7 +105,7 @@
     for s in range(1, groups):
         ask[s] = jnp.broadcast_to(wanted[s : s + 1], ask.shape[1:])
 
-    pl.semaphore_wait(barrier, groups + SIDE - 1)
+    pl.semaphore_wait(barrier, groups + 4 * (SIDE - 1))
 
     def remote(src, dst, send, recv, device):
         copy = pltpu.make_async_remote_copy(
@@ -141,6 +144,16 @@
             )
         )
     sent += asks + [own_x, own_cot] + blocks
+
+    quarter = width // SIDE
+    own_x.wait_recv()
+    early = []
+    for step in range(1, SIDE):
+        at, device = along(0, step)
+        lanes = pl.ds(pl.multiple_of(at * quarter, LANES), quarter)
+        early.append(
+            remote(x.at[pl.ds(0, views), :, :, lanes], xn_r.at[step - 1], x_send.at[step], x_recv.at[step], device)
+        )
 
     row_of = lax.broadcasted_iota(jnp.int32, (bias.shape[0], LANES), 0)
     first_of = jnp.full(row_of.shape, -2 * views, jnp.int32)
@@ -186,6 +199,14 @@
         return carry
 
     lax.fori_loop(0, views, conv_view, 0)
+    early_up = []
+    for step in range(1, SIDE):
+        early_up.append(
+            remote(
+                up.at[core], up_r.at[step - 1], x_send.at[SIDE + step], x_recv.at[SIDE + step], along(0, step)[1]
+            )
+        )
+    sent += early + early_up
 
     for copy in loads:
         copy.wait()
@@ -207,7 +228,6 @@
         om, omt,
         matmul(up[0], wo[:, pl.ds(0, width // 2)], NT) + matmul(up[1], wo[:, pl.ds(width // 2, width // 2)], NT),
     )
-    own_x.wait_recv()
     split_heads(qm, qmt, matmul(x[pl.ds(0, views)].reshape(queries, width), wq[...]))
 
     tile = 2 * LANES
@@ -257,6 +277,12 @@
     batch(*before)
     sent += forwards
 
+    lanes = pl.ds(pl.multiple_of(xx * quarter, LANES), quarter)
+    xq[:, pl.ds(0, queries)] = x[pl.ds(0, views), :, :, lanes].reshape(queries, quarter).T
+    for step in range(1, SIDE):
+        early[step - 1].wait_recv()
+        xq[:, pl.ds(step * queries, queries)] = xn_r[step - 1].reshape(queries, quarter).T
+
     def send_three(axis, source, target, send, recv, base):
         copies = []
         for step in (2, 1, 3):
@@ -272,79 +298,98 @@
             copy.wait_recv()
 
     place_of = (xx, yy, zz)
-    orders = ((0, 1, 2), (1, 2, 0), (2, 0, 1))
-    rows1 = gq.shape[3]
+    orders = ((1, 2, 0), (2, 0, 1))
+    rows1 = gk.shape[3]
     rows2 = rows1 // SIDE
 
     def phase1(t):
         return [
-            send_three(0, lambda at: gq.at[t, at], r1.at[t, 0], s1, d1, 9 * t),
-            send_three(1, lambda at: gk.at[t, :, at], r1.at[t, 1], s1, d1, 9 * t + 3),
-            send_three(2, lambda at: gv.at[t, at], r1.at[t, 2], s1, d1, 9 * t + 6),
+            send_three(1, lambda at: gk.at[t, :, at], r1.at[t, 0], s1, d1, 6 * t),
+            send_three(2, lambda at: gv.at[t, at], r1.at[t, 1], s1, d1, 6 * t + 3),
+        ]
+
+    def regroup(parts, rows):
+        return [
+            jnp.concatenate([part[k * rows : (k + 1) * rows] for part in parts], axis=0) for k in range(SIDE)
         ]
 
     def phase2(t, arrived):
         copies = []
-        for m in range(3):
+        for m in range(2):
             collect(arrived[m])
             totals = []
             for j in range(SIDE):
-                own = (gq.at[t, xx, j], gk.at[t, j, yy], gv.at[t, zz, j])[m]
+                own = (gk.at[t, j, yy], gv.at[t, zz, j])[m]
                 total = own[...].astype(F32)
                 for i in range(SIDE - 1):
                     total = total + r1[t, m, i, j].astype(F32)
                 totals.append(total)
-            if m == 1:
-                totals = [
-                    jnp.concatenate([total[k * rows2 : (k + 1) * rows2] for total in totals], axis=0)
-                    for k in range(SIDE)
-                ]
+            if m == 0:
+                totals = regroup(totals, rows2)
             for j in range(SIDE):
                 p2[t, m, j] = totals[j].astype(BF)
             copies.append(
-                send_three(orders[m][1], lambda at, m=m: p2.at[t, m, at], r2.at[t, m], s2, d2, 9 * t + 3 * m)
+                send_three(orders[m][1], lambda at, m=m: p2.at[t, m, at], r2.at[t, m], s2, d2, 6 * t + 3 * m)
             )
         return copies
+
+    def second_sum(own, others):
+        total = own[...].astype(F32)
+        for i in range(SIDE - 1):
+            total = total + others[i].astype(F32)
+        return total
+
+    def last_hop(total, axis, pieces, target, beside, unit):
+        rows = total.shape[0] // (2 * SIDE)
+        for j in range(SIDE):
+            for h in range(2):
+                pieces[j, h] = total[(2 * j + h) * rows : (2 * j + h + 1) * rows]
+        copies = []
+        for step in (2, 1, 3):
+            at, device = along(axis, step)
+            for cross in range(2):
+                to = 1 - core if cross else core
+                slot = 7 * unit + 2 * (step - 1) + cross
+                copies.append(
+                    remote(
+                        pieces.at[at, to], target.at[cross, step - 1], s3.at[slot], d3.at[slot], device[:2] + (to,)
+                    )
+                )
+        slot = 7 * unit + 6
+        copies.append(remote(pieces.at[place_of[axis], 1 - core], beside, s3.at[slot], d3.at[slot], sibling))
+        sent.extend(copies)
+        return copies
+
+    def arrive(copies, axis, pieces, target, beside, out, size, offset):
+        collect(copies)
+        span = out.shape[1] // 2
+        total = pieces[place_of[axis], core] + target[0, 0] + target[0, 1] + target[0, 2]
+        out[:, pl.ds(pl.multiple_of(core * span + offset, LANES), size)] = total
+        total = beside[...] + target[1, 0] + target[1, 1] + target[1, 2]
+        out[:, pl.ds(pl.multiple_of((1 - core) * span + offset, LANES), size)] = total
 
     def phase3(t, arrived):
         copies = []
-        for m in range(3):
+        for m in range(2):
             collect(arrived[m])
-            total = p2[t, m, place_of[orders[m][1]]].astype(F32)
-            for i in range(SIDE - 1):
-                total = total + r2[t, m, i].astype(F32)
-            for j in range(SIDE):
-                p3[t, m, j] = total[j * rows2 : (j + 1) * rows2]
+            total = second_sum(p2.at[t, m, place_of[orders[m][1]]], r2.at[t, m])
             copies.append(
-                send_three(orders[m][2], lambda at, m=m: p3.at[t, m, at], r3.at[t, m], s3, d3, 9 * t + 3 * m)
+                last_hop(total, orders[m][2], stage.at[t, m], got.at[t, m], near.at[t, m], 2 * t + m)
             )
         return copies
 
-    outs = (out_q, out_k, out_v)
-
-    def phase4(t, arrived):
-        for m in range(3):
-            collect(arrived[m])
-            total = p3[t, m, place_of[orders[m][2]]] + r3[t, m, 0] + r3[t, m, 1] + r3[t, m, 2]
-            for j in range(2):
-                f_own[j, t, m] = total[j * (rows2 // 2) : (j + 1) * (rows2 // 2)]
-            lanes = pl.ds(pl.multiple_of(core * half + t * LANES, LANES), LANES)
-            outs[m][:, lanes] = f_own[core, t, m]
-        copy = remote(f_own.at[1 - core, t], f_sib.at[t], s4.at[t], d4.at[t], sibling)
-        sent.append(copy)
-        return copy
-
-    def finish(t, copy):
-        copy.wait_recv()
-        lanes = pl.ds(pl.multiple_of((1 - core) * half + t * LANES, LANES), LANES)
-        for m in range(3):
-            outs[m][:, lanes] = f_sib[t, m]
+    def finish(t, arrived):
+        for m in range(2):
+            arrive(
+                arrived[m], orders[m][2], stage.at[t, m], got.at[t, m], near.at[t, m],
+                (out_k, out_v)[m], LANES, t * LANES,
+            )
 
     step = 64
     steps = key_rows // step
-    mixes = []
-
-    def attend(t):
+    mixes, dqs = [], []
+
+    def weights(t):
         top = jnp.max(tops[t], axis=0, keepdims=True)
 
         def weigh(i, sums):
@@ -369,106 +414,99 @@
         lax.fori_loop(0, steps, close, 0)
 
         both = matmul(values[t].T, p_buf[...]).astype(BF)
-        mixed[core, pl.ds(t * LANES, HEAD_DIM)] = both[:HEAD_DIM, :queries]
-        mixed[core, pl.ds(t * LANES + HEAD_DIM, HEAD_DIM)] = both[HEAD_DIM:, queries:]
-        piece = mixed.at[core, pl.ds(t * LANES, LANES)]
+        top = pl.multiple_of(core * half + t * LANES, LANES)
+        mixed[pl.ds(top, HEAD_DIM)] = both[:HEAD_DIM, :queries]
+        mixed[pl.ds(top + HEAD_DIM, HEAD_DIM)] = both[HEAD_DIM:, queries:]
+        piece = mixed.at[pl.ds(top, LANES)]
         mixes.append(remote(piece, piece, mix_send.at[t], mix_recv.at[t], sibling))
         dq = matmul(keys[t].T, ds_buf[...])
-        dq = jnp.concatenate((dq[:HEAD_DIM, :queries], dq[HEAD_DIM:, queries:]), axis=0).T.astype(BF)
+        dq = jnp.concatenate((dq[:HEAD_DIM, :queries], dq[HEAD_DIM:, queries:]), axis=0).T
+        dq_all[t, pl.ds(0, queries)] = dq.astype(BF)
+        copies = []
+        for hop in (2, 1, 3):
+            slot = SIDE * (2 + t) + hop
+            copies.append(
+                remote(
+                    dq_all.at[t, pl.ds(0, queries)], dq_all.at[t, pl.ds(hop * queries, queries)],
+                    x_send.at[slot], x_recv.at[slot], along(0, hop)[1],
+                )
+            )
+        dqs.append(copies)
+        sent.extend(copies)
+
+    def key_grads(t):
         dkv[:, pl.ds(0, LANES)] = matmul(ds_buf[...], qm[t]).astype(BF)
         dkv[:, pl.ds(LANES, LANES)] = matmul(p_buf[...], om[t]).astype(BF)
         for i in range(SIDE):
-            rows = pl.ds(i * (width // SIDE), width // SIDE)
-            q_part = matmul(xt[rows, pl.ds(0, queries)], dq).astype(BF)
-            gq[t, i] = q_part.reshape(SIDE, rows1, LANES)
+            rows = pl.ds(i * quarter, quarter)
             kv = matmul(xt[rows], dkv[...])
             gk[t, i] = kv[:, :LANES].astype(BF).reshape(SIDE, rows1, LANES)
             v_part = kv[:, LANES:]
-            for z in range(SIDE):
-                turned = jnp.concatenate(
-                    [v_part[(SIDE * y + z) * rows2 : (SIDE * y + z + 1) * rows2] for y in range(SIDE)], axis=0
-                )
+            parts = [v_part[y * rows1 : (y + 1) * rows1] for y in range(SIDE)]
+            for z, turned in enumerate(regroup(parts, rows2)):
                 gv[t, z, i] = turned.astype(BF)
 
-    first, second, third, last = {}, {}, {}, {}
-    for t in range(pairs):
-        attend(t)
+    first, second, third = {}, {}, {}
+    for t in range(pairs - 1):
+        weights(t)
+        key_grads(t)
         first[t] = phase1(t)
-        if t >= 1:
-            second[t - 1] = phase2(t - 1, first[t - 1])
-        if t >= 2:
-            third[t - 2] = phase3(t - 2, second[t - 2])
+    t = pairs - 1
+    weights(t)
+    second[0] = phase2(0, first[0])
+    collect(mixes)
     sent += mixes
-
-    collect(mixes)
     channels = 2 * half
-    all_mixed = mixed[...].reshape(channels, queries)
-    orows = og.shape[3]
-    orows2 = orows // SIDE
-    wide = og.shape[4]
-    for i in range(SIDE):
-        part = matmul(all_mixed[i * (channels // SIDE) : (i + 1) * (channels // SIDE)], up[core])
-        for u in range(2):
-            og[u, i] = part[:, u * wide : (u + 1) * wide].astype(BF).reshape(SIDE, orows, wide)
-        for y in range(SIDE):
-            for z in range(SIDE):
-                top = (SIDE * y + z) * orows2
-                go_tmp[z, pl.ds(y * orows2, orows2)] = part[top : top + orows2, 2 * wide : 3 * wide]
-        for z in range(SIDE):
-            og[2, z, i] = go_tmp[z].astype(BF)
-    ofirst = [
-        send_three(0, lambda at: og.at[0, at], o1.at[0], s1, d1, 9 * pairs),
-        send_three(1, lambda at: og.at[1, :, at], o1.at[1], s1, d1, 9 * pairs + 3),
-        send_three(2, lambda at: og.at[2, at], o1.at[2], s1, d1, 9 * pairs + 6),
-    ]
-    oorders = ((0, 1, 2), (1, 0, 2), (2, 0, 1))
-
-    t = pairs - 1
-    third[t - 1] = phase3(t - 1, second[t - 1])
-    second[t] = phase2(t, first[t])
-    osecond = []
-    for u in range(3):
-        collect(ofirst[u])
-        for j in range(SIDE):
-            own = (og.at[0, xx, j], og.at[1, j, yy], og.at[2, zz, j])[u]
-            total = own[...].astype(F32)
-            for i in range(SIDE - 1):
-                total = total + o1[u, i, j].astype(F32)
-            po2[u, j] = total.astype(BF)
-        osecond.append(
-            send_three(oorders[u][1], lambda at, u=u: po2.at[u, at], o2.at[u], s2, d2, 9 * pairs + 3 * u)
+    share = channels // SIDE
+    mxs = []
+    for hop in (2, 1, 3):
+        at, device = along(0, hop)
+        slot = SIDE * (2 + pairs) + hop
+        mxs.append(
+            remote(
+                mixed.at[pl.ds(pl.multiple_of(at * share, 16), share)], mx_r.at[hop - 1],
+                x_send.at[slot], x_recv.at[slot], device,
+            )
         )
-    last[t - 2] = phase4(t - 2, third[t - 2])
-    third[t] = phase3(t, second[t])
-    othird = []
-    for u in range(3):
-        collect(osecond[u])
-        total = po2[u, place_of[oorders[u][1]]].astype(F32)
-        for i in range(SIDE - 1):
-            total = total + o2[u, i].astype(F32)
-        for j in range(SIDE):
-            po3[u, j] = total[j * orows2 : (j + 1) * orows2]
-        othird.append(
-            send_three(oorders[u][2], lambda at, u=u: po3.at[u, at], o3.at[u], s3, d3, 9 * pairs + 3 * u)
-        )
-    last[t - 1] = phase4(t - 1, third[t - 1])
-    last[t] = phase4(t, third[t])
-    for u in range(3):
-        collect(othird[u])
-        total = po3[u, place_of[oorders[u][2]]] + o3[u, 0] + o3[u, 1] + o3[u, 2]
-        for j in range(2):
-            fo_own[j, u] = total[j * (orows2 // 2) : (j + 1) * (orows2 // 2)]
-    olast = remote(fo_own.at[1 - core], fo_sib, s4.at[pairs], d4.at[pairs], sibling)
-    sent.append(olast)
-    for u in range(3):
-        lanes = pl.ds(pl.multiple_of(core * (width // 2) + u * wide, LANES), wide)
-        out_o[:, lanes] = fo_own[core, u]
-    for t in range(pairs):
-        finish(t, last[t])
-    olast.wait_recv()
-    for u in range(3):
-        lanes = pl.ds(pl.multiple_of((1 - core) * (width // 2) + u * wide, LANES), wide)
-        out_o[:, lanes] = fo_sib[u]
+    sent += mxs
+    key_grads(t)
+    first[t] = phase1(t)
+
+    def query_grad(t):
+        collect(dqs[t])
+        g = matmul(xq[...], dq_all[t])
+        parts = [g[y * rows1 : (y + 1) * rows1] for y in range(SIDE)]
+        for z, turned in enumerate(regroup(parts, rows2)):
+            q2[z, :, pl.ds(t * LANES, LANES)] = turned.astype(BF)
+
+    for t in range(pairs - 1):
+        query_grad(t)
+    second[1] = phase2(1, first[1])
+    query_grad(pairs - 1)
+    q_second = send_three(2, lambda at: q2.at[at], rq2, s2, d2, 6 * pairs)
+    third[0] = phase3(0, second[0])
+
+    collect(early_up)
+    own = mixed[pl.ds(pl.multiple_of(xx * share, 16), share)]
+    g = matmul(own, up[core])
+    collect(mxs)
+    for hop in range(1, SIDE):
+        g = g + matmul(mx_r[hop - 1], up_r[hop - 1])
+    o2[...] = g.astype(BF).reshape(SIDE, share // SIDE, width // 2)
+    o_second = send_three(1, lambda at: o2.at[at], ro2, s2, d2, 6 * pairs + 3)
+
+    second[2] = phase2(2, first[2])
+    third[1] = phase3(1, second[1])
+    collect(q_second)
+    q_third = last_hop(second_sum(q2.at[zz], rq2), 1, stage_q, got_q, near_q, 2 * pairs)
+    collect(o_second)
+    o_third = last_hop(second_sum(o2.at[yy], ro2), 2, stage_o, got_o, near_o, 2 * pairs + 1)
+    finish(0, third[0])
+    third[2] = phase3(2, second[2])
+    finish(1, third[1])
+    arrive(q_third, 1, stage_q, got_q, near_q, out_q, half, 0)
+    arrive(o_third, 2, stage_o, got_o, near_o, out_o, width // 2, 0)
+    finish(2, third[2])
     for copy in sent:
         copy.wait_send()
 
@@ -499,12 +537,10 @@
     queries = views * slot_rows
     rows1 = width // 16
     orows = inner // 16
-    wide = width // 6
     vm = pltpu.VMEM
     dma = pltpu.SemaphoreType.DMA
     in_vmem = pl.BlockSpec(memory_space=pltpu.VMEM)
     in_hbm = pl.BlockSpec(memory_space=pl.ANY)
-    units = 9 * (pairs + 1)
     results = pl.pallas_call(
         kernel_body,
         out_shape=(jax.ShapeDtypeStruct((rows1 // 8, inner), F32),) * 3
@@ -535,31 +571,35 @@
             vm((key_rows, 2 * queries), BF),
             vm((key_rows, 2 * queries), BF),
             vm((key_rows, 2 * LANES), BF),
-            vm((2, half, queries), BF),
+            vm((2 * half, queries), BF),
             vm((pairs, SIDE, SIDE, rows1, LANES), BF),
             vm((pairs, SIDE, SIDE, rows1, LANES), BF),
-            vm((pairs, SIDE, SIDE, rows1, LANES), BF),
-            vm((pairs, 3, SIDE - 1, SIDE, rows1, LANES), BF),
-            vm((pairs, 3, SIDE, rows1, LANES), BF),
-            vm((pairs, 3, SIDE - 1, rows1, LANES), BF),
-            vm((pairs, 3, SIDE, rows1 // 4, LANES), F32),
-            vm((pairs, 3, SIDE - 1, rows1 // 4, LANES), F32),
-            vm((2, pairs, 3, rows1 // 8, LANES), F32),
-            vm((pairs, 3, rows1 // 8, LANES), F32),
-            vm((3, SIDE, SIDE, orows, wide), BF),
-            vm((SIDE, orows, wide), F32),
-            vm((3, SIDE - 1, SIDE, orows, wide), BF),
-            vm((3, SIDE, orows, wide), BF),
-            vm((3, SIDE - 1, orows, wide), BF),
-            vm((3, SIDE, orows // 4, wide), F32),
-            vm((3, SIDE - 1, orows // 4, wide), F32),
-            vm((2, 3, orows // 8, wide), F32),
-            vm((3, orows // 8, wide), F32),
+            vm((pairs, 2, SIDE - 1, SIDE, rows1, LANES), BF),
+            vm((pairs, 2, SIDE, rows1, LANES), BF),
+            vm((pairs, 2, SIDE - 1, rows1, LANES), BF),
+            vm((pairs, 2, SIDE, 2, rows1 // 8, LANES), F32),
+            vm((pairs, 2, 2, SIDE - 1, rows1 // 8, LANES), F32),
+            vm((pairs, 2, rows1 // 8, LANES), F32),
+            vm((SIDE - 1, views, 2, columns, width // SIDE), BF),
+            vm((width // SIDE, SIDE * queries), BF),
+            vm((SIDE - 1, queries, width // 2), BF),
+            vm((pairs, SIDE * queries, LANES), BF),
+            vm((SIDE - 1, inner // SIDE, queries), BF),
+            vm((SIDE, rows1, half), BF),
+            vm((SIDE - 1, rows1, half), BF),
+            vm((SIDE, 2, rows1 // 8, half), F32),
+            vm((2, SIDE - 1, rows1 // 8, half), F32),
+            vm((rows1 // 8, half), F32),
+            vm((SIDE, orows, width // 2), BF),
+            vm((SIDE - 1, orows, width // 2), BF),
+            vm((SIDE, 2, orows // 8, width // 2), F32),
+            vm((2, SIDE - 1, orows // 8, width // 2), F32),
+            vm((orows // 8, width // 2), F32),
             dma((4,)), dma((2,)), dma((2,)),
             dma((groups,)), dma((groups,)), dma((groups,)), dma((groups,)), dma((groups,)), dma((groups,)),
-            dma((pairs,)), dma((pairs,)),
-            dma((units,)), dma((units,)), dma((units,)), dma((units,)), dma((units,)), dma((units,)),
-            dma((pairs + 1,)), dma((pairs + 1,)),
+            dma((pairs,)), dma((pairs,)), dma((SIDE * (pairs + 3),)), dma((SIDE * (pairs + 3),)),
+            dma((6 * pairs,)), dma((6 * pairs,)), dma((6 * pairs + 6,)), dma((6 * pairs + 6,)),
+            dma((14 * pairs + 14,)), dma((14 * pairs + 14,)),
         ],
         compiler_params=pltpu.CompilerParams(
             collective_id=0, has_side_effects=True, vmem_limit_bytes=VMEM_LIMIT

time: 81.8 us -> 75 us (0.917)
  Pallas kernels: 81 us -> 74.2 us
    pallas_call x1, Pallas kernels: 79.5 us -> 72.7 us  [shards(): pl.pallas_call(kernel_body, out_shape=(jax.ShapeDtypeStruct((rows1 // 8,...]
where the time goes in v5:
time: 75 us; the launch traced here: 74.8 us
  Pallas kernels  74.2 us (99%)
    pallas_call x1, Pallas kernels, shards(): pl.pallas_call(kernel_body, out_shape=(jax.ShapeDtypeStruct((rows1 // 8,...  72.7 us
    pallas_call x1, Pallas kernels, leave(): pl.pallas_call(leave_kernel, out_shape=tuple((jax.ShapeDtypeStruct(r.shap...  1.55 us

profile of v5, /device:TPU:1, one launch (start us, length us, event | category | flops | bytes accessed | tf_op | source)
XLA Modules:
  0.0 74.8 jit_solution(12946322739460775822)
XLA Ops:
  0.6 72.7 %shard_map.120 = (f32[12,768]{1,0:T(8,128)}, f32[12,768]{1,0:T(8,128)}, f32[12,768]{1,0:T(8,128)}, f32[6,1536]{1,0:T(8,128)}) custom-call(bf16[4,32,1536]{2,1,0:T(8,128)(2,1)} %bitcast.3, f32[1536]{0:T(1024)} %gain.1, bf16[4,32,1536]{2,1,0:T(8,128)(2,1)} %bitcast.4, bf16[9,1536]{1,0:T(8,128)(2,1)} %taps.1, s32[4,8]{1,0:T(4,128)} %bitcast.5, ...), custom_call_target="tpu_custom_call" | custom-call | tf_op jit(solution)/shard_map/pallas_call | solution.py:544
  73.3 1.5 %shard_map.121 = (f32[12,768]{1,0:T(8,128)}, f32[12,768]{1,0:T(8,128)}, f32[12,768]{1,0:T(8,128)}, f32[6,1536]{1,0:T(8,128)}) custom-call(f32[12,768]{1,0:T(8,128)} %get-tuple-element.8.refs_0_, f32[12,768]{1,0:T(8,128)} %get-tuple-element.9.refs_1_, f32[12,768]{1,0:T(8,128)} %get-tuple-element.10.refs_2_, f32[6,1536]{1,0:T(8,128)} %get-tuple-element.11.refs_3_), custom_call_target="tpu_custom_call" | custom-call | tf_op jit(solution)/shard_map/pallas_call | solution.py:521

commit v6 on v5

--- a/solution.py
+++ b/solution.py
@@ -16,6 +16,7 @@
     (2, 0), (1, 3), (3, 1), (1, 2), (2, 1), (3, 2), (2, 3),
 )
 BATCHES = (4, 4, 4, 2, 1)
+EARLY = 12
 MESH = pl.DeviceIdType.MESH
 VMEM_LIMIT = 62 * 1024 * 1024
 NT = (((1,), (1,)), ((), ()))
@@ -34,7 +35,7 @@
     x, cot_all, ask, grant, outbuf, bias,
     wq, wkv, wo, xt, keys, values, qm, om, qmt, omt, up, s_all, dp_all, tops, p_buf, ds_buf, dkv, mixed,
     gk, gv, r1, p2, r2, stage, got, near,
-    xn_r, xq, up_r, dq_all, mx_r, q2, rq2, stage_q, got_q, near_q, o2, ro2, stage_o, got_o, near_o,
+    xn_r, xq, up_r, dq_all, mx_r, sums, o2, ro2, stage_o, got_o, near_o,
     load_sem, own_send, own_recv, ask_send, ask_recv, out_send, out_recv, fwd_send, fwd_recv,
     mix_send, mix_recv, x_send, x_recv, s1, d1, s2, d2, s3, d3,
 ):
@@ -257,6 +258,20 @@
             tops[pair] = top
             dp_all[pair, rows] = matmul(values[pair, rows], omt[pair])
 
+    stride = 64
+    strides = key_rows // stride
+
+    def weigh(t, top, low, high):
+        def body(i, carry):
+            rows = pl.ds(pl.multiple_of(i * stride, stride), stride)
+            e = jnp.exp(s_all[t, rows] - top)
+            s_all[t, rows] = e
+            return carry[0] + fold(e, jnp.sum), carry[1] + fold(e * dp_all[t, rows], jnp.sum)
+
+        zero = jnp.zeros((8, 2 * queries), F32)
+        total, delta = lax.fori_loop(low, high, body, (zero, zero))
+        return jnp.sum(total, axis=0, keepdims=True), jnp.sum(delta, axis=0, keepdims=True)
+
     parts = [(views + sum(BATCHES[:i]), count) for i, count in enumerate(BATCHES)]
     before = None
     batch(0, views)
@@ -270,6 +285,12 @@
             fresh.append(remote(place_x, place_x, fwd_send.at[s], fwd_recv.at[s], sibling))
         if before:
             batch(*before)
+            if sum(before) == EARLY:
+                for t in range(pairs):
+                    top = jnp.max(tops[t], axis=0, keepdims=True)
+                    total, delta = weigh(t, top, 0, EARLY * slot_rows // stride)
+                    for i, row in enumerate((top, total, delta)):
+                        sums[t, pl.ds(i, 1)] = row
         for copy in fresh:
             copy.wait_recv()
         forwards += fresh
@@ -298,15 +319,9 @@
             copy.wait_recv()
 
     place_of = (xx, yy, zz)
-    orders = ((1, 2, 0), (2, 0, 1))
+    orders = ((1, 2, 0), (2, 0, 1), (0, 2, 1))
     rows1 = gk.shape[3]
     rows2 = rows1 // SIDE
-
-    def phase1(t):
-        return [
-            send_three(1, lambda at: gk.at[t, :, at], r1.at[t, 0], s1, d1, 6 * t),
-            send_three(2, lambda at: gv.at[t, at], r1.at[t, 1], s1, d1, 6 * t + 3),
-        ]
 
     def regroup(parts, rows):
         return [
@@ -316,7 +331,7 @@
     def phase2(t, arrived):
         copies = []
         for m in range(2):
-            collect(arrived[m])
+            arrived[m]()
             totals = []
             for j in range(SIDE):
                 own = (gk.at[t, j, yy], gv.at[t, zz, j])[m]
@@ -329,7 +344,7 @@
             for j in range(SIDE):
                 p2[t, m, j] = totals[j].astype(BF)
             copies.append(
-                send_three(orders[m][1], lambda at, m=m: p2.at[t, m, at], r2.at[t, m], s2, d2, 6 * t + 3 * m)
+                send_three(orders[m][1], lambda at, m=m: p2.at[t, m, at], r2.at[t, m], s2, d2, 9 * t + 3 * m)
             )
         return copies
 
@@ -368,50 +383,41 @@
         total = beside[...] + target[1, 0] + target[1, 1] + target[1, 2]
         out[:, pl.ds(pl.multiple_of((1 - core) * span + offset, LANES), size)] = total
 
-    def phase3(t, arrived):
-        copies = []
-        for m in range(2):
-            collect(arrived[m])
-            total = second_sum(p2.at[t, m, place_of[orders[m][1]]], r2.at[t, m])
-            copies.append(
-                last_hop(total, orders[m][2], stage.at[t, m], got.at[t, m], near.at[t, m], 2 * t + m)
-            )
-        return copies
-
-    def finish(t, arrived):
-        for m in range(2):
-            arrive(
-                arrived[m], orders[m][2], stage.at[t, m], got.at[t, m], near.at[t, m],
-                (out_k, out_v)[m], LANES, t * LANES,
-            )
-
-    step = 64
-    steps = key_rows // step
+    def phase3(t, m, arrived):
+        collect(arrived)
+        total = second_sum(p2.at[t, m, place_of[orders[m][1]]], r2.at[t, m])
+        return last_hop(total, orders[m][2], stage.at[t, m], got.at[t, m], near.at[t, m], 3 * t + m)
+
+    def finish(t, m, arrived):
+        arrive(
+            arrived, orders[m][2], stage.at[t, m], got.at[t, m], near.at[t, m],
+            (out_k, out_v, out_q)[m], LANES, t * LANES,
+        )
+
     mixes, dqs = [], []
 
     def weights(t):
         top = jnp.max(tops[t], axis=0, keepdims=True)
-
-        def weigh(i, sums):
-            rows = pl.ds(pl.multiple_of(i * step, step), step)
-            e = jnp.exp(s_all[t, rows] - top)
-            s_all[t, rows] = e
-            return sums[0] + fold(e, jnp.sum), sums[1] + fold(e * dp_all[t, rows], jnp.sum)
-
-        zero = jnp.zeros((8, 2 * queries), F32)
-        total, delta = lax.fori_loop(0, steps, weigh, (zero, zero))
-        inverse = 1.0 / jnp.sum(total, axis=0, keepdims=True)
-        delta = jnp.sum(delta, axis=0, keepdims=True) * inverse
-        scaled = inverse * scale
-
-        def close(i, carry):
-            rows = pl.ds(pl.multiple_of(i * step, step), step)
-            e = s_all[t, rows]
-            p_buf[rows] = (e * inverse).astype(BF)
-            ds_buf[rows] = (e * scaled * (dp_all[t, rows] - delta)).astype(BF)
-            return carry
-
-        lax.fori_loop(0, steps, close, 0)
+        early_strides = EARLY * slot_rows // stride
+        factor = jnp.exp(sums[t, 0:1] - top)
+        total, delta = weigh(t, top, early_strides, strides)
+        inverse = 1.0 / (total + factor * sums[t, 1:2])
+        delta = (delta + factor * sums[t, 2:3]) * inverse
+
+        def close(low, high, inverse):
+            scaled = inverse * scale
+
+            def body(i, carry):
+                rows = pl.ds(pl.multiple_of(i * stride, stride), stride)
+                e = s_all[t, rows]
+                p_buf[rows] = (e * inverse).astype(BF)
+                ds_buf[rows] = (e * scaled * (dp_all[t, rows] - delta)).astype(BF)
+                return carry
+
+            lax.fori_loop(low, high, body, 0)
+
+        close(0, early_strides, inverse * factor)
+        close(early_strides, strides, inverse)
 
         both = matmul(values[t].T, p_buf[...]).astype(BF)
         top = pl.multiple_of(core * half + t * LANES, LANES)
@@ -434,6 +440,24 @@
         dqs.append(copies)
         sent.extend(copies)
 
+    def first_hop(t, m, i):
+        copies = []
+        for hop in (2, 1, 3):
+            at, device = along(orders[m][0], hop)
+            slot = 6 * t + 3 * m + hop - 1
+            source, target = (gk.at[t, :, at], gv.at[t, at])[m], r1.at[t, m, hop - 1]
+            if i is None:
+                copies.append(
+                    pltpu.make_async_remote_copy(
+                        src_ref=source, dst_ref=target, send_sem=s1.at[slot], recv_sem=d1.at[slot],
+                        device_id=device, device_id_type=MESH,
+                    )
+                )
+            else:
+                source = (gk.at[t, i, at], gv.at[t, at, i])[m]
+                remote(source, target.at[i], s1.at[slot], d1.at[slot], device)
+        return copies
+
     def key_grads(t):
         dkv[:, pl.ds(0, LANES)] = matmul(ds_buf[...], qm[t]).astype(BF)
         dkv[:, pl.ds(LANES, LANES)] = matmul(p_buf[...], om[t]).astype(BF)
@@ -441,72 +465,93 @@
             rows = pl.ds(i * quarter, quarter)
             kv = matmul(xt[rows], dkv[...])
             gk[t, i] = kv[:, :LANES].astype(BF).reshape(SIDE, rows1, LANES)
+            first_hop(t, 0, i)
             v_part = kv[:, LANES:]
             parts = [v_part[y * rows1 : (y + 1) * rows1] for y in range(SIDE)]
             for z, turned in enumerate(regroup(parts, rows2)):
                 gv[t, z, i] = turned.astype(BF)
-
-    first, second, third = {}, {}, {}
-    for t in range(pairs - 1):
-        weights(t)
-        key_grads(t)
-        first[t] = phase1(t)
-    t = pairs - 1
-    weights(t)
-    second[0] = phase2(0, first[0])
-    collect(mixes)
-    sent += mixes
+            first_hop(t, 1, i)
+        whole = [first_hop(t, m, None) for m in range(2)]
+        sent.extend(whole[0] + whole[1])
+        return [functools.partial(collect, copies) for copies in whole]
+
     channels = 2 * half
     share = channels // SIDE
-    mxs = []
-    for hop in (2, 1, 3):
-        at, device = along(0, hop)
-        slot = SIDE * (2 + pairs) + hop
-        mxs.append(
-            remote(
-                mixed.at[pl.ds(pl.multiple_of(at * share, 16), share)], mx_r.at[hop - 1],
-                x_send.at[slot], x_recv.at[slot], device,
+    mxs = [[], []]
+
+    def send_mixed(part):
+        low, high = ((0, share // 3), (share // 3, share))[part]
+        for hop in (2, 1, 3):
+            at, device = along(0, hop)
+            slot = SIDE * (2 + pairs + part) + hop
+            mxs[part].append(
+                remote(
+                    mixed.at[pl.ds(pl.multiple_of(at * share + low, 16), high - low)],
+                    mx_r.at[hop - 1, pl.ds(low, high - low)], x_send.at[slot], x_recv.at[slot], device,
+                )
             )
-        )
-    sent += mxs
-    key_grads(t)
-    first[t] = phase1(t)
+        sent.extend(mxs[part])
 
     def query_grad(t):
         collect(dqs[t])
         g = matmul(xq[...], dq_all[t])
         parts = [g[y * rows1 : (y + 1) * rows1] for y in range(SIDE)]
         for z, turned in enumerate(regroup(parts, rows2)):
-            q2[z, :, pl.ds(t * LANES, LANES)] = turned.astype(BF)
-
-    for t in range(pairs - 1):
-        query_grad(t)
-    second[1] = phase2(1, first[1])
-    query_grad(pairs - 1)
-    q_second = send_three(2, lambda at: q2.at[at], rq2, s2, d2, 6 * pairs)
-    third[0] = phase3(0, second[0])
+            p2[t, 2, z] = turned.astype(BF)
+        return send_three(2, lambda at: p2.at[t, 2, at], r2.at[t, 2], s2, d2, 9 * t + 6)
+
+    first, second, third = {}, {}, {}
+
+    def hop2(t):
+        second[t, 0], second[t, 1] = phase2(t, first[t])
+
+    def hop3(t, *ms):
+        for m in ms:
+            third[t, m] = phase3(t, m, second[t, m])
+
+    weights(0)
+    first[0] = key_grads(0)
+    weights(1)
+    first[1] = key_grads(1)
+    collect(mixes[:2])
+    send_mixed(0)
+    second[0, 2] = query_grad(0)
+    weights(2)
+    hop2(0)
+    collect(mixes[2:])
+    send_mixed(1)
+    first[2] = key_grads(2)
+    sent += mixes
+
+    second[1, 2] = query_grad(1)
+    hop3(0, 2, 0, 1)
+    hop2(1)
+    second[2, 2] = query_grad(2)
+    hop3(1, 2)
 
     collect(early_up)
     own = mixed[pl.ds(pl.multiple_of(xx * share, 16), share)]
     g = matmul(own, up[core])
-    collect(mxs)
+    for part in range(2):
+        collect(mxs[part])
     for hop in range(1, SIDE):
         g = g + matmul(mx_r[hop - 1], up_r[hop - 1])
     o2[...] = g.astype(BF).reshape(SIDE, share // SIDE, width // 2)
-    o_second = send_three(1, lambda at: o2.at[at], ro2, s2, d2, 6 * pairs + 3)
-
-    second[2] = phase2(2, first[2])
-    third[1] = phase3(1, second[1])
-    collect(q_second)
-    q_third = last_hop(second_sum(q2.at[zz], rq2), 1, stage_q, got_q, near_q, 2 * pairs)
+    o_second = send_three(1, lambda at: o2.at[at], ro2, s2, d2, 9 * pairs)
+
+    hop2(2)
+    hop3(1, 0, 1)
+    for m in range(3):
+        finish(0, m, third[0, m])
+    hop3(2, 2)
     collect(o_second)
-    o_third = last_hop(second_sum(o2.at[yy], ro2), 2, stage_o, got_o, near_o, 2 * pairs + 1)
-    finish(0, third[0])
-    third[2] = phase3(2, second[2])
-    finish(1, third[1])
-    arrive(q_third, 1, stage_q, got_q, near_q, out_q, half, 0)
+    o_third = last_hop(second_sum(o2.at[yy], ro2), 2, stage_o, got_o, near_o, 3 * pairs)
+    hop3(2, 0, 1)
+    for m in range(3):
+        finish(1, m, third[1, m])
+    for m in (2, 0, 1):
+        finish(2, m, third[2, m])
     arrive(o_third, 2, stage_o, got_o, near_o, out_o, width // 2, 0)
-    finish(2, third[2])
     for copy in sent:
         copy.wait_send()
 
@@ -575,21 +620,17 @@
             vm((pairs, SIDE, SIDE, rows1, LANES), BF),
             vm((pairs, SIDE, SIDE, rows1, LANES), BF),
             vm((pairs, 2, SIDE - 1, SIDE, rows1, LANES), BF),
-            vm((pairs, 2, SIDE, rows1, LANES), BF),
-            vm((pairs, 2, SIDE - 1, rows1, LANES), BF),
-            vm((pairs, 2, SIDE, 2, rows1 // 8, LANES), F32),
-            vm((pairs, 2, 2, SIDE - 1, rows1 // 8, LANES), F32),
-            vm((pairs, 2, rows1 // 8, LANES), F32),
+            vm((pairs, 3, SIDE, rows1, LANES), BF),
+            vm((pairs, 3, SIDE - 1, rows1, LANES), BF),
+            vm((pairs, 3, SIDE, 2, rows1 // 8, LANES), F32),
+            vm((pairs, 3, 2, SIDE - 1, rows1 // 8, LANES), F32),
+            vm((pairs, 3, rows1 // 8, LANES), F32),
             vm((SIDE - 1, views, 2, columns, width // SIDE), BF),
             vm((width // SIDE, SIDE * queries), BF),
             vm((SIDE - 1, queries, width // 2), BF),
             vm((pairs, SIDE * queries, LANES), BF),
             vm((SIDE - 1, inner // SIDE, queries), BF),
-            vm((SIDE, rows1, half), BF),
-            vm((SIDE - 1, rows1, half), BF),
-            vm((SIDE, 2, rows1 // 8, half), F32),
-            vm((2, SIDE - 1, rows1 // 8, half), F32),
-            vm((rows1 // 8, half), F32),
+            vm((pairs, 8, 2 * queries), F32),
             vm((SIDE, orows, width // 2), BF),
             vm((SIDE - 1, orows, width // 2), BF),
             vm((SIDE, 2, orows // 8, width // 2), F32),
@@ -597,9 +638,9 @@
             vm((orows // 8, width // 2), F32),
             dma((4,)), dma((2,)), dma((2,)),
             dma((groups,)), dma((groups,)), dma((groups,)), dma((groups,)), dma((groups,)), dma((groups,)),
-            dma((pairs,)), dma((pairs,)), dma((SIDE * (pairs + 3),)), dma((SIDE * (pairs + 3),)),
-            dma((6 * pairs,)), dma((6 * pairs,)), dma((6 * pairs + 6,)), dma((6 * pairs + 6,)),
-            dma((14 * pairs + 14,)), dma((14 * pairs + 14,)),
+            dma((pairs,)), dma((pairs,)), dma((SIDE * (pairs + 4),)), dma((SIDE * (pairs + 4),)),
+            dma((6 * pairs,)), dma((6 * pairs,)), dma((9 * pairs + 3,)), dma((9 * pairs + 3,)),
+            dma((21 * pairs + 7,)), dma((21 * pairs + 7,)),
         ],
         compiler_params=pltpu.CompilerParams(
             collective_id=0, has_side_effects=True, vmem_limit_bytes=VMEM_LIMIT

time: 75 us -> 76.6 us (1.021)
  Pallas kernels: 74.2 us -> 75.8 us
    pallas_call x1, Pallas kernels: 72.7 us -> 74.3 us  [shards(): pl.pallas_call(kernel_body, out_shape=(jax.ShapeDtypeStruct((rows1 // 8,...]
where the time goes in v6:
time: 76.6 us; the launch traced here: 76.4 us
  Pallas kernels  75.8 us (99%)
    pallas_call x1, Pallas kernels, shards(): pl.pallas_call(kernel_body, out_shape=(jax.ShapeDtypeStruct((rows1 // 8,...  74.3 us
    pallas_call x1, Pallas kernels, leave(): pl.pallas_call(leave_kernel, out_shape=tuple((jax.ShapeDtypeStruct(r.shap...  1.55 us

profile of v6, /device:TPU:1, one launch (start us, length us, event | category | flops | bytes accessed | tf_op | source)
XLA Modules:
  0.0 76.4 jit_solution(14909964545166467289)
XLA Ops:
  0.6 74.3 %shard_map.120 = (f32[12,768]{1,0:T(8,128)}, f32[12,768]{1,0:T(8,128)}, f32[12,768]{1,0:T(8,128)}, f32[6,1536]{1,0:T(8,128)}) custom-call(bf16[4,32,1536]{2,1,0:T(8,128)(2,1)} %bitcast.3, f32[1536]{0:T(1024)} %gain.1, bf16[4,32,1536]{2,1,0:T(8,128)(2,1)} %bitcast.4, bf16[9,1536]{1,0:T(8,128)(2,1)} %taps.1, s32[4,8]{1,0:T(4,128)} %bitcast.5, ...), custom_call_target="tpu_custom_call" | custom-call | tf_op jit(solution)/shard_map/pallas_call | solution.py:589
  74.9 1.5 %shard_map.121 = (f32[12,768]{1,0:T(8,128)}, f32[12,768]{1,0:T(8,128)}, f32[12,768]{1,0:T(8,128)}, f32[6,1536]{1,0:T(8,128)}) custom-call(f32[12,768]{1,0:T(8,128)} %get-tuple-element.8.refs_0_, f32[12,768]{1,0:T(8,128)} %get-tuple-element.9.refs_1_, f32[12,768]{1,0:T(8,128)} %get-tuple-element.10.refs_2_, f32[6,1536]{1,0:T(8,128)} %get-tuple-element.11.refs_3_), custom_call_target="tpu_custom_call" | custom-call | tf_op jit(solution)/shard_map/pallas_call | solution.py:566

commit v7 on v6

--- a/solution.py
+++ b/solution.py
@@ -15,8 +15,8 @@
     (0, 1), (1, 0), (0, 3), (3, 0), (2, 2), (1, 1), (3, 3), (0, 2),
     (2, 0), (1, 3), (3, 1), (1, 2), (2, 1), (3, 2), (2, 3),
 )
-BATCHES = (4, 4, 4, 2, 1)
-EARLY = 12
+BATCHES = (4, 4, 4, 3)
+EARLY = 8
 MESH = pl.DeviceIdType.MESH
 VMEM_LIMIT = 62 * 1024 * 1024
 NT = (((1,), (1,)), ((), ()))
@@ -30,13 +30,13 @@
 
 
 def kernel_body(
-    lat, gain, cot, taps, partners, wq_hbm, wk_hbm, wv_hbm, wo_hbm,
+    lat_hbm, gain_hbm, cot_hbm, taps_hbm, partners_hbm, wq_hbm, wk_hbm, wv_hbm, wo_hbm,
     out_q, out_k, out_v, out_o,
-    x, cot_all, ask, grant, outbuf, bias,
+    lat, gain, taps, partners, x, cot_all, ask, grant, outbuf, bias,
     wq, wkv, wo, xt, keys, values, qm, om, qmt, omt, up, s_all, dp_all, tops, p_buf, ds_buf, dkv, mixed,
     gk, gv, r1, p2, r2, stage, got, near,
-    xn_r, xq, up_r, dq_all, mx_r, sums, o2, ro2, stage_o, got_o, near_o,
-    load_sem, own_send, own_recv, ask_send, ask_recv, out_send, out_recv, fwd_send, fwd_recv,
+    xn_r, xq, up_r, dq_all, mx_r, sums, q2, rq2, stage_q, got_q, near_q, o2, ro2, stage_o, got_o, near_o,
+    load_sem, small_sem, own_send, own_recv, ask_send, ask_recv, out_send, out_recv, fwd_send, fwd_recv,
     mix_send, mix_recv, x_send, x_recv, s1, d1, s2, d2, s3, d3,
 ):
     xx, me, core = lax.axis_index("scene"), lax.axis_index("view"), lax.axis_index("row")
@@ -74,6 +74,15 @@
         at = lax.rem(zz + step, SIDE)
         return at, (xx, yy * SIDE + at, core)
 
+    small = [
+        pltpu.make_async_copy(partners_hbm, partners, small_sem.at[0]),
+        pltpu.make_async_copy(lat_hbm, lat, small_sem.at[1]),
+        pltpu.make_async_copy(gain_hbm, gain, small_sem.at[2]),
+        pltpu.make_async_copy(cot_hbm, cot_all.at[core], small_sem.at[3]),
+        pltpu.make_async_copy(taps_hbm, taps, small_sem.at[4]),
+    ]
+    for copy in small:
+        copy.start()
     barrier = pltpu.get_barrier_semaphore()
     for step in range(1, groups):
         pl.semaphore_signal(barrier, inc=1, device_id=(xx, peer(step), core), device_id_type=MESH)
@@ -99,6 +108,7 @@
     for s in range(1, groups):
         first_of = jnp.where(steps_of == s, peer(s) * views, first_of)
     wanted = jnp.zeros((groups, LANES), jnp.int32)
+    small[0].wait()
     for v in range(views):
         for j in range(partners.shape[1]):
             local = partners[v, j] - first_of
@@ -120,13 +130,14 @@
         remote(ask.at[s], grant.at[s], ask_send.at[s], ask_recv.at[s], (xx, peer(s), core))
         for s in range(1, groups)
     ]
-    own_cot = remote(cot, cot_all.at[core], own_send.at[1], own_recv.at[1], sibling)
-
+    own_cot = remote(cot_hbm, cot_all.at[core], own_send.at[1], own_recv.at[1], sibling)
+
+    for copy in small[1:3]:
+        copy.wait()
     for v in range(views):
         rows = lat[v].astype(F32)
         mean = jnp.mean(rows * rows, -1, keepdims=True)
         x[v, core] = (rows * lax.rsqrt(mean + EPSILON) * gain[...].reshape(1, width)).astype(BF)
-    cot_all[core] = cot[...]
 
     mine = x.at[pl.ds(0, views), core]
     own_x = remote(mine, mine, own_send.at[0], own_recv.at[0], sibling)
@@ -175,6 +186,8 @@
         for head in range(2):
             bias[:, pl.ds(head * queries + part * LANES, LANES)] = both
 
+    for copy in small[3:]:
+        copy.wait()
     own_cot.wait_recv()
     chunk = 2 * LANES
     place = lax.broadcasted_iota(jnp.int32, (columns, chunk), 0)
@@ -273,6 +286,13 @@
         return jnp.sum(total, axis=0, keepdims=True), jnp.sum(delta, axis=0, keepdims=True)
 
     parts = [(views + sum(BATCHES[:i]), count) for i, count in enumerate(BATCHES)]
+    def turn_quarters():
+        lanes = pl.ds(pl.multiple_of(xx * quarter, LANES), quarter)
+        xq[:, pl.ds(0, queries)] = x[pl.ds(0, views), :, :, lanes].reshape(queries, quarter).T
+        for hop in range(1, SIDE):
+            early[hop - 1].wait_recv()
+            xq[:, pl.ds(hop * queries, queries)] = xn_r[hop - 1].reshape(queries, quarter).T
+
     before = None
     batch(0, views)
     forwards = []
@@ -291,18 +311,14 @@
                     total, delta = weigh(t, top, 0, EARLY * slot_rows // stride)
                     for i, row in enumerate((top, total, delta)):
                         sums[t, pl.ds(i, 1)] = row
+            if sum(before) == EARLY + BATCHES[1]:
+                turn_quarters()
         for copy in fresh:
             copy.wait_recv()
         forwards += fresh
         before = (first, count)
     batch(*before)
     sent += forwards
-
-    lanes = pl.ds(pl.multiple_of(xx * quarter, LANES), quarter)
-    xq[:, pl.ds(0, queries)] = x[pl.ds(0, views), :, :, lanes].reshape(queries, quarter).T
-    for step in range(1, SIDE):
-        early[step - 1].wait_recv()
-        xq[:, pl.ds(step * queries, queries)] = xn_r[step - 1].reshape(queries, quarter).T
 
     def send_three(axis, source, target, send, recv, base):
         copies = []
@@ -319,7 +335,7 @@
             copy.wait_recv()
 
     place_of = (xx, yy, zz)
-    orders = ((1, 2, 0), (2, 0, 1), (0, 2, 1))
+    orders = ((1, 2, 0), (2, 0, 1))
     rows1 = gk.shape[3]
     rows2 = rows1 // SIDE
 
@@ -331,7 +347,7 @@
     def phase2(t, arrived):
         copies = []
         for m in range(2):
-            arrived[m]()
+            collect(arrived[m])
             totals = []
             for j in range(SIDE):
                 own = (gk.at[t, j, yy], gv.at[t, zz, j])[m]
@@ -391,7 +407,7 @@
     def finish(t, m, arrived):
         arrive(
             arrived, orders[m][2], stage.at[t, m], got.at[t, m], near.at[t, m],
-            (out_k, out_v, out_q)[m], LANES, t * LANES,
+            (out_k, out_v)[m], LANES, t * LANES,
         )
 
     mixes, dqs = [], []
@@ -440,40 +456,26 @@
         dqs.append(copies)
         sent.extend(copies)
 
-    def first_hop(t, m, i):
-        copies = []
-        for hop in (2, 1, 3):
-            at, device = along(orders[m][0], hop)
-            slot = 6 * t + 3 * m + hop - 1
-            source, target = (gk.at[t, :, at], gv.at[t, at])[m], r1.at[t, m, hop - 1]
-            if i is None:
-                copies.append(
-                    pltpu.make_async_remote_copy(
-                        src_ref=source, dst_ref=target, send_sem=s1.at[slot], recv_sem=d1.at[slot],
-                        device_id=device, device_id_type=MESH,
-                    )
-                )
-            else:
-                source = (gk.at[t, i, at], gv.at[t, at, i])[m]
-                remote(source, target.at[i], s1.at[slot], d1.at[slot], device)
-        return copies
-
-    def key_grads(t):
+    def first_hop(t):
+        return [
+            send_three(1, lambda at: gk.at[t, :, at], r1.at[t, 0], s1, d1, 6 * t),
+            send_three(2, lambda at: gv.at[t, at], r1.at[t, 1], s1, d1, 6 * t + 3),
+        ]
+
+    def key_grads(t, between=None):
         dkv[:, pl.ds(0, LANES)] = matmul(ds_buf[...], qm[t]).astype(BF)
         dkv[:, pl.ds(LANES, LANES)] = matmul(p_buf[...], om[t]).astype(BF)
         for i in range(SIDE):
             rows = pl.ds(i * quarter, quarter)
             kv = matmul(xt[rows], dkv[...])
             gk[t, i] = kv[:, :LANES].astype(BF).reshape(SIDE, rows1, LANES)
-            first_hop(t, 0, i)
             v_part = kv[:, LANES:]
             parts = [v_part[y * rows1 : (y + 1) * rows1] for y in range(SIDE)]
             for z, turned in enumerate(regroup(parts, rows2)):
                 gv[t, z, i] = turned.astype(BF)
-            first_hop(t, 1, i)
-        whole = [first_hop(t, m, None) for m in range(2)]
-        sent.extend(whole[0] + whole[1])
-        return [functools.partial(collect, copies) for copies in whole]
+            if i == 1 and between:
+                between()
+        return first_hop(t)
 
     channels = 2 * half
     share = channels // SIDE
@@ -497,8 +499,7 @@
         g = matmul(xq[...], dq_all[t])
         parts = [g[y * rows1 : (y + 1) * rows1] for y in range(SIDE)]
         for z, turned in enumerate(regroup(parts, rows2)):
-            p2[t, 2, z] = turned.astype(BF)
-        return send_three(2, lambda at: p2.at[t, 2, at], r2.at[t, 2], s2, d2, 9 * t + 6)
+            q2[z, :, pl.ds(t * LANES, LANES)] = turned.astype(BF)
 
     first, second, third = {}, {}, {}
 
@@ -515,19 +516,22 @@
     first[1] = key_grads(1)
     collect(mixes[:2])
     send_mixed(0)
-    second[0, 2] = query_grad(0)
+    query_grad(0)
     weights(2)
+
+    def last_mixed():
+        collect(mixes[2:])
+        send_mixed(1)
+
+    first[2] = key_grads(2, last_mixed)
     hop2(0)
-    collect(mixes[2:])
-    send_mixed(1)
-    first[2] = key_grads(2)
     sent += mixes
 
-    second[1, 2] = query_grad(1)
-    hop3(0, 2, 0, 1)
+    query_grad(1)
     hop2(1)
-    second[2, 2] = query_grad(2)
-    hop3(1, 2)
+    query_grad(2)
+    q_second = send_three(2, lambda at: q2.at[at], rq2, s2, d2, 9 * pairs + 3)
+    hop3(0, 0, 1)
 
     collect(early_up)
     own = mixed[pl.ds(pl.multiple_of(xx * share, 16), share)]
@@ -541,15 +545,17 @@
 
     hop2(2)
     hop3(1, 0, 1)
-    for m in range(3):
+    for m in range(2):
         finish(0, m, third[0, m])
-    hop3(2, 2)
+    collect(q_second)
+    q_third = last_hop(second_sum(q2.at[zz], rq2), 1, stage_q, got_q, near_q, 3 * pairs + 1)
+    hop3(2, 0, 1)
     collect(o_second)
     o_third = last_hop(second_sum(o2.at[yy], ro2), 2, stage_o, got_o, near_o, 3 * pairs)
-    hop3(2, 0, 1)
-    for m in range(3):
+    for m in range(2):
         finish(1, m, third[1, m])
-    for m in (2, 0, 1):
+    arrive(q_third, 1, stage_q, got_q, near_q, out_q, half, 0)
+    for m in range(2):
         finish(2, m, third[2, m])
     arrive(o_third, 2, stage_o, got_o, near_o, out_o, width // 2, 0)
     for copy in sent:
@@ -590,9 +596,13 @@
         kernel_body,
         out_shape=(jax.ShapeDtypeStruct((rows1 // 8, inner), F32),) * 3
         + (jax.ShapeDtypeStruct((orows // 8, width), F32),),
-        in_specs=[in_vmem] * 4 + [pl.BlockSpec(memory_space=pltpu.SMEM)] + [in_hbm] * 4,
+        in_specs=[in_hbm] * 9,
         out_specs=(in_vmem,) * 4,
         scratch_shapes=[
+            vm((views, columns, width), BF),
+            vm((width,), F32),
+            vm(kernel.shape, BF),
+            pltpu.SMEM(partners.shape[1:], jnp.int32),
             vm((slots, 2, columns, width), BF),
             vm((2, views, columns, width), BF),
             vm((groups, 8, LANES), jnp.int32),
@@ -620,27 +630,32 @@
             vm((pairs, SIDE, SIDE, rows1, LANES), BF),
             vm((pairs, SIDE, SIDE, rows1, LANES), BF),
             vm((pairs, 2, SIDE - 1, SIDE, rows1, LANES), BF),
-            vm((pairs, 3, SIDE, rows1, LANES), BF),
-            vm((pairs, 3, SIDE - 1, rows1, LANES), BF),
-            vm((pairs, 3, SIDE, 2, rows1 // 8, LANES), F32),
-            vm((pairs, 3, 2, SIDE - 1, rows1 // 8, LANES), F32),
-            vm((pairs, 3, rows1 // 8, LANES), F32),
+            vm((pairs, 2, SIDE, rows1, LANES), BF),
+            vm((pairs, 2, SIDE - 1, rows1, LANES), BF),
+            vm((pairs, 2, SIDE, 2, rows1 // 8, LANES), F32),
+            vm((pairs, 2, 2, SIDE - 1, rows1 // 8, LANES), F32),
+            vm((pairs, 2, rows1 // 8, LANES), F32),
             vm((SIDE - 1, views, 2, columns, width // SIDE), BF),
             vm((width // SIDE, SIDE * queries), BF),
             vm((SIDE - 1, queries, width // 2), BF),
             vm((pairs, SIDE * queries, LANES), BF),
             vm((SIDE - 1, inner // SIDE, queries), BF),
             vm((pairs, 8, 2 * queries), F32),
+            vm((SIDE, rows1, half), BF),
+            vm((SIDE - 1, rows1, half), BF),
+            vm((SIDE, 2, rows1 // 8, half), F32),
+            vm((2, SIDE - 1, rows1 // 8, half), F32),
+            vm((rows1 // 8, half), F32),
             vm((SIDE, orows, width // 2), BF),
             vm((SIDE - 1, orows, width // 2), BF),
             vm((SIDE, 2, orows // 8, width // 2), F32),
             vm((2, SIDE - 1, orows // 8, width // 2), F32),
             vm((orows // 8, width // 2), F32),
-            dma((4,)), dma((2,)), dma((2,)),
+            dma((4,)), dma((5,)), dma((2,)), dma((2,)),
             dma((groups,)), dma((groups,)), dma((groups,)), dma((groups,)), dma((groups,)), dma((groups,)),
             dma((pairs,)), dma((pairs,)), dma((SIDE * (pairs + 4),)), dma((SIDE * (pairs + 4),)),
-            dma((6 * pairs,)), dma((6 * pairs,)), dma((9 * pairs + 3,)), dma((9 * pairs + 3,)),
-            dma((21 * pairs + 7,)), dma((21 * pairs + 7,)),
+            dma((6 * pairs,)), dma((6 * pairs,)), dma((9 * pairs + 6,)), dma((9 * pairs + 6,)),
+            dma((21 * pairs + 14,)), dma((21 * pairs + 14,)),
         ],
         compiler_params=pltpu.CompilerParams(
             collective_id=0, has_side_effects=True, vmem_limit_bytes=VMEM_LIMIT

time: 76.6 us -> 74.4 us (0.971)
  Pallas kernels: 75.8 us -> 73.6 us
    pallas_call x1, Pallas kernels: 74.3 us -> 72 us  [shards(): pl.pallas_call(kernel_body, out_shape=(jax.ShapeDtypeStruct((rows1 // 8,...]
where the time goes in v7:
time: 74.4 us; the launch traced here: 74.2 us
  Pallas kernels  73.6 us (99%)
    pallas_call x1, Pallas kernels, shards(): pl.pallas_call(kernel_body, out_shape=(jax.ShapeDtypeStruct((rows1 // 8,...  72 us
    pallas_call x1, Pallas kernels, leave(): pl.pallas_call(leave_kernel, out_shape=tuple((jax.ShapeDtypeStruct(r.shap...  1.55 us

profile of v7, /device:TPU:1, one launch (start us, length us, event | category | flops | bytes accessed | tf_op | source)
XLA Modules:
  0.0 74.2 jit_solution(809780230137846210)
XLA Ops:
  0.6 72.0 %shard_map.120 = (f32[12,768]{1,0:T(8,128)}, f32[12,768]{1,0:T(8,128)}, f32[12,768]{1,0:T(8,128)}, f32[6,1536]{1,0:T(8,128)}) custom-call(bf16[4,32,1536]{2,1,0:T(8,128)(2,1)} %bitcast.3, f32[1536]{0:T(1024)} %gain_hbm.1, bf16[4,32,1536]{2,1,0:T(8,128)(2,1)} %bitcast.4, bf16[9,1536]{1,0:T(8,128)(2,1)} %taps_hbm.1, s32[4,8]{1,0:T(4,128)} %bitcast.5, ...), custom_call_target="tpu_custom_call" | custom-call | tf_op jit(solution)/shard_map/pallas_call | solution.py:595
  72.7 1.5 %shard_map.121 = (f32[12,768]{1,0:T(8,128)}, f32[12,768]{1,0:T(8,128)}, f32[12,768]{1,0:T(8,128)}, f32[6,1536]{1,0:T(8,128)}) custom-call(f32[12,768]{1,0:T(8,128)} %get-tuple-element.8.refs_0_, f32[12,768]{1,0:T(8,128)} %get-tuple-element.9.refs_1_, f32[12,768]{1,0:T(8,128)} %get-tuple-element.10.refs_2_, f32[6,1536]{1,0:T(8,128)} %get-tuple-element.11.refs_3_), custom_call_target="tpu_custom_call" | custom-call | tf_op jit(solution)/shard_map/pallas_call | solution.py:572

commit v8 on v7

--- a/solution.py
+++ b/solution.py
@@ -412,29 +412,47 @@
 
     mixes, dqs = [], []
 
+    early_strides = EARLY * slot_rows // stride
+
+    def rest(t, unrolled):
+        top = jnp.max(tops[t], axis=0, keepdims=True)
+        factor = jnp.exp(sums[t, 0:1] - top)
+        if unrolled:
+            total, delta = jnp.zeros((8, 2 * queries), F32), jnp.zeros((8, 2 * queries), F32)
+            for i in range(early_strides, strides):
+                rows = pl.ds(i * stride, stride)
+                e = jnp.exp(s_all[t, rows] - top)
+                s_all[t, rows] = e
+                total, delta = total + fold(e, jnp.sum), delta + fold(e * dp_all[t, rows], jnp.sum)
+            total, delta = jnp.sum(total, axis=0, keepdims=True), jnp.sum(delta, axis=0, keepdims=True)
+        else:
+            total, delta = weigh(t, top, early_strides, strides)
+        inverse = 1.0 / (total + factor * sums[t, 1:2])
+        return inverse * factor, inverse, (delta + factor * sums[t, 2:3]) * inverse
+
+    def close(t, low, high, inverse, delta, unrolled):
+        scaled = inverse * scale
+
+        def body(i, carry):
+            start = i * stride if unrolled else pl.multiple_of(i * stride, stride)
+            rows = pl.ds(start, stride)
+            e = s_all[t, rows]
+            p_buf[rows] = (e * inverse).astype(BF)
+            ds_buf[rows] = (e * scaled * (dp_all[t, rows] - delta)).astype(BF)
+            return carry
+
+        if unrolled:
+            for i in range(low, high):
+                body(i, 0)
+        else:
+            lax.fori_loop(low, high, body, 0)
+
     def weights(t):
-        top = jnp.max(tops[t], axis=0, keepdims=True)
-        early_strides = EARLY * slot_rows // stride
-        factor = jnp.exp(sums[t, 0:1] - top)
-        total, delta = weigh(t, top, early_strides, strides)
-        inverse = 1.0 / (total + factor * sums[t, 1:2])
-        delta = (delta + factor * sums[t, 2:3]) * inverse
-
-        def close(low, high, inverse):
-            scaled = inverse * scale
-
-            def body(i, carry):
-                rows = pl.ds(pl.multiple_of(i * stride, stride), stride)
-                e = s_all[t, rows]
-                p_buf[rows] = (e * inverse).astype(BF)
-                ds_buf[rows] = (e * scaled * (dp_all[t, rows] - delta)).astype(BF)
-                return carry
-
-            lax.fori_loop(low, high, body, 0)
-
-        close(0, early_strides, inverse * factor)
-        close(early_strides, strides, inverse)
-
+        first_inverse, inverse, delta = rest(t, False)
+        close(t, 0, early_strides, first_inverse, delta, False)
+        close(t, early_strides, strides, inverse, delta, False)
+
+    def from_queries(t):
         both = matmul(values[t].T, p_buf[...]).astype(BF)
         top = pl.multiple_of(core * half + t * LANES, LANES)
         mixed[pl.ds(top, HEAD_DIM)] = both[:HEAD_DIM, :queries]
@@ -462,7 +480,7 @@
             send_three(2, lambda at: gv.at[t, at], r1.at[t, 1], s1, d1, 6 * t + 3),
         ]
 
-    def key_grads(t, between=None):
+    def key_grads(t, between=None, follow=None):
         dkv[:, pl.ds(0, LANES)] = matmul(ds_buf[...], qm[t]).astype(BF)
         dkv[:, pl.ds(LANES, LANES)] = matmul(p_buf[...], om[t]).astype(BF)
         for i in range(SIDE):
@@ -475,6 +493,15 @@
                 gv[t, z, i] = turned.astype(BF)
             if i == 1 and between:
                 between()
+            if follow is not None and i == 0:
+                first_inverse, inverse, delta = rest(follow, True)
+            elif follow is not None:
+                low = early_strides + (strides - early_strides) * (i - 2) // 2
+                high = early_strides + (strides - early_strides) * (i - 1) // 2
+                if i == 1:
+                    close(follow, 0, early_strides, first_inverse, delta, True)
+                else:
+                    close(follow, low, high, inverse, delta, True)
         return first_hop(t)
 
     channels = 2 * half
@@ -511,13 +538,14 @@
             third[t, m] = phase3(t, m, second[t, m])
 
     weights(0)
-    first[0] = key_grads(0)
-    weights(1)
-    first[1] = key_grads(1)
+    from_queries(0)
+    first[0] = key_grads(0, follow=1)
+    from_queries(1)
+    first[1] = key_grads(1, follow=2)
     collect(mixes[:2])
     send_mixed(0)
     query_grad(0)
-    weights(2)
+    from_queries(2)
 
     def last_mixed():
         collect(mixes[2:])
@@ -552,14 +580,14 @@
     hop3(2, 0, 1)
     collect(o_second)
     o_third = last_hop(second_sum(o2.at[yy], ro2), 2, stage_o, got_o, near_o, 3 * pairs)
+    for copy in sent:
+        copy.wait_send()
     for m in range(2):
         finish(1, m, third[1, m])
     arrive(q_third, 1, stage_q, got_q, near_q, out_q, half, 0)
     for m in range(2):
         finish(2, m, third[2, m])
     arrive(o_third, 2, stage_o, got_o, near_o, out_o, width // 2, 0)
-    for copy in sent:
-        copy.wait_send()
 
 
 def leave_kernel(*refs):

time: 74.4 us -> 72.7 us (0.977)
  Pallas kernels: 73.6 us -> 71.9 us
    pallas_call x1, Pallas kernels: 72 us -> 70.4 us  [shards(): pl.pallas_call(kernel_body, out_shape=(jax.ShapeDtypeStruct((rows1 // 8,...]
where the time goes in v8:
time: 72.7 us; the launch traced here: 72.5 us
  Pallas kernels  71.9 us (99%)
    pallas_call x1, Pallas kernels, shards(): pl.pallas_call(kernel_body, out_shape=(jax.ShapeDtypeStruct((rows1 // 8,...  70.4 us
    pallas_call x1, Pallas kernels, leave(): pl.pallas_call(leave_kernel, out_shape=tuple((jax.ShapeDtypeStruct(r.shap...  1.55 us

profile of v8, /device:TPU:1, one launch (start us, length us, event | category | flops | bytes accessed | tf_op | source)
XLA Modules:
  0.0 72.5 jit_solution(5266253614276249895)
XLA Ops:
  0.6 70.4 %shard_map.120 = (f32[12,768]{1,0:T(8,128)}, f32[12,768]{1,0:T(8,128)}, f32[12,768]{1,0:T(8,128)}, f32[6,1536]{1,0:T(8,128)}) custom-call(bf16[4,32,1536]{2,1,0:T(8,128)(2,1)} %bitcast.3, f32[1536]{0:T(1024)} %gain_hbm.1, bf16[4,32,1536]{2,1,0:T(8,128)(2,1)} %bitcast.4, bf16[9,1536]{1,0:T(8,128)(2,1)} %taps_hbm.1, s32[4,8]{1,0:T(4,128)} %bitcast.5, ...), custom_call_target="tpu_custom_call" | custom-call | tf_op jit(solution)/shard_map/pallas_call | solution.py:623
  71.0 1.5 %shard_map.121 = (f32[12,768]{1,0:T(8,128)}, f32[12,768]{1,0:T(8,128)}, f32[12,768]{1,0:T(8,128)}, f32[6,1536]{1,0:T(8,128)}) custom-call(f32[12,768]{1,0:T(8,128)} %get-tuple-element.8.refs_0_, f32[12,768]{1,0:T(8,128)} %get-tuple-element.9.refs_1_, f32[12,768]{1,0:T(8,128)} %get-tuple-element.10.refs_2_, f32[6,1536]{1,0:T(8,128)} %get-tuple-element.11.refs_3_), custom_call_target="tpu_custom_call" | custom-call | tf_op jit(solution)/shard_map/pallas_call | solution.py:600

commit v9 on v8

--- a/solution.py
+++ b/solution.py
@@ -448,9 +448,9 @@
             lax.fori_loop(low, high, body, 0)
 
     def weights(t):
-        first_inverse, inverse, delta = rest(t, False)
-        close(t, 0, early_strides, first_inverse, delta, False)
-        close(t, early_strides, strides, inverse, delta, False)
+        first_inverse, inverse, delta = rest(t, True)
+        close(t, 0, early_strides, first_inverse, delta, True)
+        close(t, early_strides, strides, inverse, delta, True)
 
     def from_queries(t):
         both = matmul(values[t].T, p_buf[...]).astype(BF)

time: 72.7 us -> 72.6 us (level)
  no operation moved by 1% of the time
where the time goes in v9:
time: 72.6 us; the launch traced here: 72.4 us
  Pallas kernels  71.8 us (99%)
    pallas_call x1, Pallas kernels, shards(): pl.pallas_call(kernel_body, out_shape=(jax.ShapeDtypeStruct((rows1 // 8,...  70.2 us
    pallas_call x1, Pallas kernels, leave(): pl.pallas_call(leave_kernel, out_shape=tuple((jax.ShapeDtypeStruct(r.shap...  1.55 us

profile of v9, /device:TPU:1, one launch (start us, length us, event | category | flops | bytes accessed | tf_op | source)
XLA Modules:
  0.0 72.4 jit_solution(7867546274588824673)
XLA Ops:
  0.6 70.2 %shard_map.120 = (f32[12,768]{1,0:T(8,128)}, f32[12,768]{1,0:T(8,128)}, f32[12,768]{1,0:T(8,128)}, f32[6,1536]{1,0:T(8,128)}) custom-call(bf16[4,32,1536]{2,1,0:T(8,128)(2,1)} %bitcast.3, f32[1536]{0:T(1024)} %gain_hbm.1, bf16[4,32,1536]{2,1,0:T(8,128)(2,1)} %bitcast.4, bf16[9,1536]{1,0:T(8,128)(2,1)} %taps_hbm.1, s32[4,8]{1,0:T(4,128)} %bitcast.5, ...), custom_call_target="tpu_custom_call" | custom-call | tf_op jit(solution)/shard_map/pallas_call | solution.py:623
  70.9 1.5 %shard_map.121 = (f32[12,768]{1,0:T(8,128)}, f32[12,768]{1,0:T(8,128)}, f32[12,768]{1,0:T(8,128)}, f32[6,1536]{1,0:T(8,128)}) custom-call(f32[12,768]{1,0:T(8,128)} %get-tuple-element.8.refs_0_, f32[12,768]{1,0:T(8,128)} %get-tuple-element.9.refs_1_, f32[12,768]{1,0:T(8,128)} %get-tuple-element.10.refs_2_, f32[6,1536]{1,0:T(8,128)} %get-tuple-element.11.refs_3_), custom_call_target="tpu_custom_call" | custom-call | tf_op jit(solution)/shard_map/pallas_call | solution.py:600
